TPU v7x, 32 devices: a whole 2x2x4 slice. The times are simulated.
32 devices in a mesh: expert: 4 (over z), dp: 8 (over y, x, core).
Axes of the slice: x: 2, y: 2, z: 4, core: 2. Of those that a mesh axis runs over, the one named last changes fastest.
Arguments:
- tokens: bfloat16 [2048, 4096], P(('expert', 'dp')), may hold values from -6 to 6
- out_grad: bfloat16 [2048, 4096], P(('expert', 'dp')), may hold values from -6 to 6
- routes: int32 [2048, 8], P(('expert', 'dp')), may hold values from 0 to 31, all different within a row; in each aligned block of 64 rows (0 to 63, 64 to 127, ...) at most 24 rows name the same one
- gate_probs: bfloat16 [2048, 8], P(('expert', 'dp')), may hold values from 0.019897461 to 0.5
- doc_ids: int32 [2048], P(('expert', 'dp')), may hold values from 0 to 31, never falling along the last dimension, each value on 1 to 256 neighbouring positions
- w_gate: bfloat16 [32, 4096, 1024], P(('expert', 'dp')), may hold values from -0.09375 to 0.09375
- w_up: bfloat16 [32, 4096, 1024], P(('expert', 'dp')), may hold values from -0.09375 to 0.09375
- proj_hidden: bfloat16 [1024, 32], replicated, may hold values from -0.1875 to 0.1875
- proj_out: bfloat16 [4096, 32], replicated, may hold values from -0.09375 to 0.09375
Outputs:
- sketches: float32 [32, 32, 1024], P(('expert', 'dp'))
Inputs may be any that keep to these rules, and one draw needn't show every extreme that they name: `routes`: each row names 8 different experts; among the rows of one device no expert is named by more than 24 rows, and in every draw some device's rows name some expert exactly 24 times. `doc_ids`: never falling along the tokens; every document has 1 to 256 tokens, one exactly 256.
All inputs are finite; a program needn't handle non-finite values.
Results may differ from a plain program's by a relative error of at most 0.005.
Values may be sent and summed in bfloat16 or wider, within the bound.
No kernel may reach another device: no remote copies, remote signals or barrier semaphores. Data moves between devices by JAX's collectives and lax.ppermute only.
A program may use at most 128 MiB of HBM per device.

v0:
```python
import functools

import jax
import jax.numpy as jnp
from jax import lax
from jax.experimental import pallas as pl
from jax.experimental.pallas import tpu as pltpu
from jax.sharding import PartitionSpec as P

AXES = ("expert", "dp")
LANES = 128
MIB = 1 << 20


def place(width, first):
    rows = lax.broadcasted_iota(jnp.int32, (width, LANES), 0)
    lanes = lax.broadcasted_iota(jnp.int32, (width, LANES), 1)
    return (lanes == rows + first).astype(jnp.bfloat16)


def dot(a, b):
    return jnp.dot(a, b, preferred_element_type=jnp.float32)


def extend_kernel(rank, top, tokens, grads, proj, routes, gates, docs, out):
    width = tokens.shape[1]
    projected = dot(grads[...], proj[...]).astype(jnp.bfloat16)
    meta = dot(projected, place(rank, 0))
    meta += dot(gates[...], place(top, rank))
    meta += dot(routes[...].astype(jnp.float32).astype(jnp.bfloat16), place(top, rank + top))
    lanes = lax.broadcasted_iota(jnp.int32, meta.shape, 1)
    meta = jnp.where(lanes == rank + 2 * top, docs[...].astype(jnp.float32), meta)
    out[:, :width] = tokens[...]
    out[:, width:] = meta.astype(jnp.bfloat16)


def extend(tokens, out_grad, proj_out, routes, gate_probs, doc_ids):
    rows, width = tokens.shape
    body = functools.partial(extend_kernel, proj_out.shape[1], routes.shape[1])
    return pl.pallas_call(
        body,
        out_shape=jax.ShapeDtypeStruct((rows, width + LANES), jnp.bfloat16),
        compiler_params=pltpu.CompilerParams(vmem_limit_bytes=16 * MIB),
        name="extend_rows",
    )(tokens, out_grad, proj_out, routes, gate_probs, doc_ids.reshape(rows, 1))


def compact_kernel(count, capacity, top, rank, spans, experts, *refs):
    sources, outs = refs[:count], refs[count:]
    rows, total = sources[0].shape
    width = total - LANES
    meta = jnp.concatenate([s[:, width:] for s in sources], axis=0).astype(jnp.float32)
    lanes = lax.broadcasted_iota(jnp.int32, meta.shape, 1)
    is_route = (lanes >= rank + top) & (lanes < rank + 2 * top)
    hits = jnp.zeros(meta.shape, jnp.float32)
    for q in range(len(outs)):
        named = is_route & (meta == experts[q].astype(jnp.float32))
        hit = jnp.sum(named.astype(jnp.float32), axis=1, keepdims=True)
        hits = jnp.where(lanes == q, hit, hits)
    every = count * rows
    here = lax.broadcasted_iota(jnp.int32, (every, every), 0)
    other = lax.broadcasted_iota(jnp.int32, (every, every), 1)
    earlier = ((other < here) & (other // rows == here // rows)).astype(jnp.bfloat16)
    before = dot(earlier, hits.astype(jnp.bfloat16))
    first = (lax.broadcasted_iota(jnp.int32, meta.shape, 0) // rows * capacity).astype(jnp.float32)
    slots = jnp.where(hits > 0, before + first, -1.0).T
    spot = lax.broadcasted_iota(jnp.int32, (count * capacity, every), 0).astype(jnp.float32)
    picks = [(spot == slots[q : q + 1, :]).astype(jnp.bfloat16) for q in range(len(outs))]
    step = 4 * LANES
    by_span = {}
    for q, span in enumerate(spans):
        by_span.setdefault(span, []).append(q)
    for (start, stop), members in by_span.items():
        pick = jnp.concatenate([picks[q] for q in members], axis=0)
        for at in range(start, stop, step):
            end = min(at + step, stop)
            block = jnp.concatenate([s[:, at:end] for s in sources], axis=0)
            found = dot(pick, block).astype(jnp.bfloat16)
            for i, q in enumerate(members):
                outs[q][:, at - start : end - start] = found[
                    i * count * capacity : (i + 1) * count * capacity
                ]


def compact(sources, experts, spans, capacity, top, rank):
    count = len(sources)
    body = functools.partial(compact_kernel, count, capacity, top, rank, tuple(spans))
    size = sum(s.size for s in sources)
    return pl.pallas_call(
        body,
        out_shape=[
            jax.ShapeDtypeStruct((count * capacity, b - a), jnp.bfloat16) for a, b in spans
        ],
        in_specs=[pl.BlockSpec(memory_space=pltpu.SMEM)]
        + [pl.BlockSpec(memory_space=pltpu.VMEM)] * count,
        out_specs=[pl.BlockSpec(memory_space=pltpu.VMEM)] * len(spans),
        compiler_params=pltpu.CompilerParams(vmem_limit_bytes=24 * MIB),
        cost_estimate=pl.CostEstimate(flops=4 * 10**8, bytes_accessed=4 * size, transcendentals=0),
        name="compact_rows",
    )(jnp.stack(experts), *sources)


def sketch_kernel(spots, top, rank, steps, docs_total, expert, *refs):
    pieces = refs[: len(spots)]
    gate_w, up_w, proj, total_in, total_out, rows_at, hidden_at = refs[len(spots) :]
    width = rows_at.shape[1] - LANES
    step = pl.program_id(0)

    @pl.when(step == 0)
    def _():
        for ref, (row, column) in zip(pieces, spots):
            r, c = ref.shape
            rows_at[row : row + r, column : column + c] = ref[...]

    rows = rows_at[:, :width]
    gate_part = dot(rows, gate_w[0])
    up_part = dot(rows, up_w[0])
    hidden_at[step] = (gate_part / (1.0 + jnp.exp(-gate_part)) * up_part).astype(jnp.bfloat16)

    @pl.when(step == steps - 1)
    def _():
        tile = gate_w.shape[2]
        side = dot(hidden_at[0], proj[:tile])
        for s in range(1, steps):
            side += dot(hidden_at[s], proj[s * tile : (s + 1) * tile])
        meta = rows_at[:, width:]
        wide = meta.astype(jnp.float32)
        lanes = lax.broadcasted_iota(jnp.int32, wide.shape, 1)
        is_route = (lanes >= rank + top) & (lanes < rank + 2 * top)
        named = (is_route & (wide == expert[0].astype(jnp.float32))).astype(jnp.float32)
        gate = jnp.sum(wide * pltpu.roll(named, LANES - top, 1), axis=1, keepdims=True)
        spread_from = lax.broadcasted_iota(jnp.int32, (LANES, rank * rank), 0)
        spread_to = lax.broadcasted_iota(jnp.int32, (LANES, rank * rank), 1) // rank
        spread = (spread_from == spread_to).astype(jnp.bfloat16)
        output_side = dot(meta, spread) * gate
        outer = output_side * jnp.concatenate([side] * (rank * rank // LANES), axis=1)
        doc = jnp.sum(jnp.where(lanes == rank + 2 * top, wide, 0.0), axis=1, keepdims=True)
        ids = lax.broadcasted_iota(jnp.int32, (wide.shape[0], docs_total), 1).astype(jnp.float32)
        table = (ids == doc).astype(jnp.bfloat16)
        high = outer.astype(jnp.bfloat16)
        low = (outer - high.astype(jnp.float32)).astype(jnp.bfloat16)
        over_rows = (((0,), (0,)), ((), ()))
        total = total_in[...]
        for part in (high, low):
            total += lax.dot_general(table, part, over_rows, preferred_element_type=jnp.float32)
        total_out[...] = total


def sketch(pieces, spots, rows, expert, w_gate, w_up, proj_wide, total, top, rank):
    width, hidden = w_gate.shape[1:]
    tile = 256
    steps = hidden // tile
    body = functools.partial(sketch_kernel, tuple(spots), top, rank, steps, total.shape[0])
    whole = lambda a: pl.BlockSpec(a.shape, lambda i: (0,) * a.ndim)
    return pl.pallas_call(
        body,
        grid=(steps,),
        out_shape=jax.ShapeDtypeStruct(total.shape, jnp.float32),
        in_specs=[pl.BlockSpec(memory_space=pltpu.SMEM)]
        + [whole(p) for p in pieces]
        + [pl.BlockSpec((1, width, tile), lambda i: (0, 0, i))] * 2
        + [whole(proj_wide), whole(total)],
        out_specs=whole(total),
        scratch_shapes=[
            pltpu.VMEM((rows, width + LANES), jnp.bfloat16),
            pltpu.VMEM((steps, rows, tile), jnp.bfloat16),
        ],
        compiler_params=pltpu.CompilerParams(vmem_limit_bytes=40 * MIB),
        cost_estimate=pl.CostEstimate(
            flops=4 * rows * width * hidden,
            bytes_accessed=4 * width * hidden,
            transcendentals=rows * hidden,
        ),
        name="sketch_rows",
    )(expert, *pieces, w_gate, w_up, proj_wide, total)


def on_device(tokens, out_grad, routes, gate_probs, doc_ids, w_gate, w_up, proj_hidden, proj_out):
    groups, planes = lax.axis_size("expert"), lax.axis_size("dp")
    devices = groups * planes
    row_count, width = tokens.shape
    top = routes.shape[1]
    rank = proj_out.shape[1]
    capacity = max(2, 3 * row_count * top // (2 * devices))
    me = lax.axis_index(AXES).astype(jnp.int32)

    def swap(value, bits):
        return lax.ppermute(value, AXES, [(i, i ^ bits) for i in range(devices)])

    def turn(value, by):
        pairs = [(((g + by) % groups, p), (g, p)) for g in range(groups) for p in range(planes)]
        return lax.ppermute(
            value, AXES, [(a * planes + b, c * planes + d) for (a, b), (c, d) in pairs]
        )

    ext = extend(tokens, out_grad, proj_out, routes, gate_probs, doc_ids)
    order = sorted(range(groups), key=lambda j: min(j, groups - j))
    slots = [ext if j == 0 else turn(ext, j) for j in order]
    bits = [1 << b for b in range(1, planes.bit_length() - 1)]
    last = sum(bits)
    columns = {0: slots}
    for mask in sorted(range(2, last, 2), key=lambda m: bin(m).count("1")):
        low = mask & -mask
        columns[mask] = [swap(s, low) for s in columns[mask ^ low]]

    tiles = (width + LANES) // LANES
    cuts = [LANES * (tiles * i // len(bits)) for i in range(len(bits) + 1)]
    full = (0, width + LANES)
    span_of = {last ^ b: (cuts[i], cuts[i + 1]) for i, b in enumerate(bits)}
    half = groups * capacity
    args = (capacity, top, rank)
    proj_wide = jnp.tile(proj_hidden, (1, LANES // rank))
    total = jnp.zeros((devices, rank * rank), jnp.float32)
    own = me.reshape(1)
    far, far_spots = [], []

    for mask in columns:
        experts, spans = [me, me ^ 1], [full, full]
        if mask in span_of:
            hop = last ^ mask
            experts += [me ^ hop, me ^ hop ^ 1]
            spans += [span_of[mask]] * 2
        found = compact(columns[mask], experts, spans, *args)
        if mask in span_of:
            far += [swap(found[2], hop), swap(found[3], hop ^ 1)]
            far_spots += [(0, span_of[mask][0]), (half, span_of[mask][0])]
        pieces = [found[0], swap(found[1], 1)]
        spots = [(0, 0), (half, 0)]
        total = sketch(pieces, spots, 2 * half, own, w_gate, w_up, proj_wide, total, top, rank)
    total = sketch(far, far_spots, 2 * half, own, w_gate, w_up, proj_wide, total, top, rank)
    owned = lax.all_to_all(total, AXES, split_axis=0, concat_axis=0, tiled=True)
    return owned[None]


def solution(mesh):
    placed = (
        P(AXES, None),
        P(AXES, None),
        P(AXES, None),
        P(AXES, None),
        P(AXES),
        P(AXES, None, None),
        P(AXES, None, None),
        P(),
        P(),
    )
    return jax.shard_map(
        on_device,
        mesh=mesh,
        in_specs=placed,
        out_specs=P(AXES, None, None),
        check_vma=False,
    )
```

profile of v0, /device:TPU:0, one launch (start us, length us, event | category | flops | bytes accessed | tf_op | source)
XLA Modules:
  0.0 168.7 jit_solution(14103378214680605357)
XLA Ops:
  0.0 1.5 copy.23.proj
  1.5 0.8 copy.24.routes
  2.2 0.7 copy.26.docs
  3.0 0.8 copy.25.gates
  3.8 1.0 copy-done.10
  4.8 1.0 copy-done.11
  5.8 0.5 extend_rows.1.refs_0_
  6.3 5.0 %collective-permute-start.1 = (bf16[64,4224]{1,0:T(8,128)(2,1)S(1)}, bf16[64,4224]{1,0:T(8,128)(2,1)}, u32[]{:S(2)}, u32[]{:S(2)}) collective-permute-start(bf16[64,4224]{1,0:T(8,128)(2,1)S(1)} %extend_rows.1.refs_0_), channel_id=1, source_target_pairs={{8,0},{9,1},{10,2},{11,3},{12,4},{13,5},{14,6},{15,7},{16,8},{17,9... | collective-permute-start | bytes 1622024 | tf_op jit(solution)/shard_map/ppermute | solution.py:192
  11.4 1.0 collective-permute-start.5
  12.4 1.5 collective-permute-start
  13.9 10.2 %collective-permute-done.1.refs_1_ = bf16[64,4224]{1,0:T(8,128)(2,1)} collective-permute-done((bf16[64,4224]{1,0:T(8,128)(2,1)S(1)}, bf16[64,4224]{1,0:T(8,128)(2,1)}, u32[]{:S(2)}, u32[]{:S(2)}) %collective-permute-start.1) | collective-permute-done | bytes 540704 | tf_op jit(solution)/shard_map/ppermute | solution.py:192
  24.0 1.5 collective-permute-start.2
  25.5 11.2 %collective-permute-done.3.refs_2_ = bf16[64,4224]{1,0:T(8,128)(2,1)} collective-permute-done((bf16[64,4224]{1,0:T(8,128)(2,1)S(1)}, bf16[64,4224]{1,0:T(8,128)(2,1)}, u32[]{:S(2)}, u32[]{:S(2)}) %collective-permute-start.3) | collective-permute-done | bytes 540704 | tf_op jit(solution)/shard_map/ppermute | solution.py:192
  36.7 1.5 collective-permute-start.4
  38.2 19.4 %collective-permute-done.5.refs_3_ = bf16[64,4224]{1,0:T(8,128)(2,1)} collective-permute-done((bf16[64,4224]{1,0:T(8,128)(2,1)S(1)}, bf16[64,4224]{1,0:T(8,128)(2,1)}, u32[]{:S(2)}, u32[]{:S(2)}) %collective-permute-start.5) | collective-permute-done | bytes 540704 | tf_op jit(solution)/shard_map/ppermute | solution.py:192
  57.6 1.5 collective-permute-start.6
  59.1 1.5 collective-permute-start.9
  60.7 3.2 %compact_rows.5 = (bf16[96,4224]{1,0:T(8,128)(2,1)S(1)}, bf16[96,4224]{1,0:T(8,128)(2,1)}) custom-call(s32[2]{0:T(128)S(1)} %pad_add_fusion.3.experts, bf16[64,4224]{1,0:T(8,128)(2,1)S(1)} %extend_rows.1.refs_0_, bf16[64,4224]{1,0:T(8,128)(2,1)} %collective-permute-done.1.refs_1_, bf16[64,4224]{1,0:T(8,128)(2,1)} %collective-permute-done.3.refs_2_, ...), custom_call_target="tpu_custom_call" | custom-call | flops 400000000 | bytes 4325376 | tf_op jit(solution)/shard_map/compact_rows/pallas_call | solution.py:89
  64.0 0.8 copy-done.8
  64.8 0.5 collective-permute-start.10
  65.3 1.5 collective-permute-start.11
  66.8 4.2 %collective-permute-done.6.refs_3_ = bf16[64,4224]{1,0:T(8,128)(2,1)} collective-permute-done((bf16[64,4224]{1,0:T(8,128)(2,1)}, bf16[64,4224]{1,0:T(8,128)(2,1)}, u32[]{:S(2)}, u32[]{:S(2)}) %collective-permute-start.6) | collective-permute-done | bytes 540704 | tf_op jit(solution)/shard_map/ppermute | solution.py:188
  71.1 1.5 collective-permute-start.12
  72.7 1.0 copy-done.9
  73.8 3.4 %compact_rows.3 = (bf16[96,4224]{1,0:T(8,128)(2,1)S(1)}, bf16[96,4224]{1,0:T(8,128)(2,1)}, bf16[96,2176]{1,0:T(8,128)(2,1)S(1)}, bf16[96,2176]{1,0:T(8,128)(2,1)}) custom-call(s32[4]{0:T(128)S(1)} %pad_add_fusion.experts, bf16[64,4224]{1,0:T(8,128)(2,1)S(1)} %copy-done.9, bf16[64,4224]{1,0:T(8,128)(2,1)} %collective-permute-done.2.refs_1_, ...), custom_call_target="tpu_custom_call" | custom-call | flops 400000000 | bytes 4325376 | tf_op jit(solution)/shard_map/compact_rows/pallas_call | solution.py:89
  77.2 0.9 copy-done.2
  78.1 0.8 copy-done.6
  79.0 7.1 %collective-permute-done.10.refs_1_ = bf16[64,4224]{1,0:T(8,128)(2,1)} collective-permute-done((bf16[64,4224]{1,0:T(8,128)(2,1)}, bf16[64,4224]{1,0:T(8,128)(2,1)}, u32[]{:S(2)}, u32[]{:S(2)}) %collective-permute-start.10) | collective-permute-done | bytes 540704 | tf_op jit(solution)/shard_map/ppermute | solution.py:188
  86.0 11.6 %collective-permute-done.11.refs_2_ = bf16[64,4224]{1,0:T(8,128)(2,1)} collective-permute-done((bf16[64,4224]{1,0:T(8,128)(2,1)}, bf16[64,4224]{1,0:T(8,128)(2,1)}, u32[]{:S(2)}, u32[]{:S(2)}) %collective-permute-start.11) | collective-permute-done | bytes 540704 | tf_op jit(solution)/shard_map/ppermute | solution.py:188
  97.6 9.2 %collective-permute-done.12.refs_3_ = bf16[64,4224]{1,0:T(8,128)(2,1)} collective-permute-done((bf16[64,4224]{1,0:T(8,128)(2,1)}, bf16[64,4224]{1,0:T(8,128)(2,1)}, u32[]{:S(2)}, u32[]{:S(2)}) %collective-permute-start.12) | collective-permute-done | bytes 540704 | tf_op jit(solution)/shard_map/ppermute | solution.py:188
  106.9 1.0 copy-done.7
  107.9 3.3 %compact_rows.4 = (bf16[96,4224]{1,0:T(8,128)(2,1)S(1)}, bf16[96,4224]{1,0:T(8,128)(2,1)}, bf16[96,2048]{1,0:T(8,128)(2,1)S(1)}, bf16[96,2048]{1,0:T(8,128)(2,1)S(1)}) custom-call(s32[4]{0:T(128)S(1)} %pad_add_fusion.2.experts, bf16[64,4224]{1,0:T(8,128)(2,1)S(1)} %copy-done.7, bf16[64,4224]{1,0:T(8,128)(2,1)} %collective-permute-done.10.refs_1_, ...), custom_call_target="tpu_custom_call" | custom-call | flops 400000000 | bytes 4325376 | tf_op jit(solution)/shard_map/compact_rows/pallas_call | solution.py:89
  111.2 0.9 copy-done.4
  112.1 0.8 copy-done.12
  112.9 0.7 copy-done.13
  113.7 0.2 copy.30.refs_4_.refs_6_
  113.8 0.6 collective-permute-start.13
  114.4 1.3 collective-permute-start.14
  115.8 1.5 collective-permute-start.7
  117.3 3.4 %copy-done = bf16[1,4096,1024]{2,1,0:T(8,128)(2,1)S(1)} copy-done((bf16[1,4096,1024]{2,1,0:T(8,128)(2,1)S(1)}, bf16[1,4096,1024]{2,1,0:T(8,128)(2,1)}, u32[]{:S(2)}) %copy-start) | copy-done | bytes 8388632
  120.7 7.8 %sketch_rows.4.refs_5_ = f32[32,1024]{1,0:T(8,128)S(1)} custom-call(s32[1]{0:T(128)} %bitcast.expert, bf16[96,4224]{1,0:T(8,128)(2,1)S(1)} %get-tuple-element.23.refs_0_, bf16[96,4224]{1,0:T(8,128)(2,1)S(1)} %collective-permute-done.17.refs_1_, bf16[1,4096,1024]{2,1,0:T(8,128)(2,1)S(1)} %copy-done, bf16[1,4096,1024]{2,1,0:T(8,128)(2,1)} %refs_5_.1, ...), custom_call_target="tpu_custom_call" | custom-call | flops 3221225472 | bytes 16777216 | tf_op jit(solution)/shard_map/sketch_rows/pallas_call | solution.py:155
  128.5 0.2 collective-permute-start.8
  128.7 3.4 %copy-done.1 = bf16[1,4096,1024]{2,1,0:T(8,128)(2,1)S(1)} copy-done((bf16[1,4096,1024]{2,1,0:T(8,128)(2,1)S(1)}, bf16[1,4096,1024]{2,1,0:T(8,128)(2,1)}, u32[]{:S(2)}) %copy-start.1) | copy-done | bytes 8388632
  132.1 7.9 %sketch_rows.5.refs_5_ = f32[32,1024]{1,0:T(8,128)S(1)} custom-call(s32[1]{0:T(128)} %bitcast.expert, bf16[96,4224]{1,0:T(8,128)(2,1)S(1)} %copy-done.3, bf16[96,4224]{1,0:T(8,128)(2,1)S(1)} %collective-permute-done.16.refs_1_, bf16[1,4096,1024]{2,1,0:T(8,128)(2,1)S(1)} %copy-done.1, bf16[1,4096,1024]{2,1,0:T(8,128)(2,1)} %refs_5_.1, ...), custom_call_target="tpu_custom_call" | custom-call | flops 3221225472 | bytes 16777216 | tf_op jit(solution)/shard_map/sketch_rows/pallas_call | solution.py:155
  140.0 8.2 %sketch_rows.6.refs_7_ = f32[32,1024]{1,0:T(8,128)S(1)} custom-call(s32[1]{0:T(128)} %bitcast.expert, bf16[96,4224]{1,0:T(8,128)(2,1)S(1)} %copy-done.5, bf16[96,4224]{1,0:T(8,128)(2,1)} %collective-permute-done.15.refs_1_, bf16[1,4096,1024]{2,1,0:T(8,128)(2,1)S(1)} %copy-done.1, bf16[1,4096,1024]{2,1,0:T(8,128)(2,1)} %refs_5_.1, ...), custom_call_target="tpu_custom_call" | custom-call | flops 3221225472 | bytes 16777216 | tf_op jit(solution)/shard_map/sketch_rows/pallas_call | solution.py:155
  148.3 7.8 %sketch_rows.7 = f32[32,1024]{1,0:T(8,128)S(1)} custom-call(s32[1]{0:T(128)} %bitcast.expert, bf16[96,2176]{1,0:T(8,128)(2,1)S(1)} %collective-permute-done.7.refs_0_, bf16[96,2176]{1,0:T(8,128)(2,1)S(1)} %collective-permute-done.8.refs_1_, bf16[96,2048]{1,0:T(8,128)(2,1)S(1)} %collective-permute-done.13.refs_2_, ...), custom_call_target="tpu_custom_call" | custom-call | flops 3221225472 | bytes 16777216 | tf_op jit(solution)/shard_map/sketch_rows/pallas_call | solution.py:155
  156.2 11.8 %all_to_all.9 = f32[32,1,1024]{2,1,0:T(1,128)S(1)} all-to-all(f32[32,1,1024]{2,1,0:T(1,128)S(1)} %copy.31), channel_id=1, replica_groups=mesh['expert'=4,'dp'=8] {'expert','dp'}, dimensions={0} | all-to-all | bytes 262144 | tf_op jit(solution)/shard_map/all_to_all | solution.py:231
  168.0 0.7 copy.32
  (44 shorter events, 0.5 us)
Async XLA Ops:
  0.0 113.6 %copy-start.14 = (bf16[1024,32]{0,1:T(8,128)(2,1)S(1)}, bf16[1024,32]{0,1:T(8,128)(2,1)}, u32[]{:S(2)}) copy-start(bf16[1024,32]{0,1:T(8,128)(2,1)} %param.16) | copy-start | bytes 196612
  3.8 1.0 copy-start.10
  4.8 1.0 copy-start.11
  6.3 17.7 %collective-permute-start.1 = (bf16[64,4224]{1,0:T(8,128)(2,1)S(1)}, bf16[64,4224]{1,0:T(8,128)(2,1)}, u32[]{:S(2)}, u32[]{:S(2)}) collective-permute-start(bf16[64,4224]{1,0:T(8,128)(2,1)S(1)} %extend_rows.1.refs_0_), channel_id=1, source_target_pairs={{8,0},{9,1},{10,2},{11,3},{12,4},{13,5},{14,6},{15,7},{16,8},{17,9... | collective-permute-start | bytes 1622024 | tf_op jit(solution)/shard_map/ppermute | solution.py:192
  11.4 25.4 %collective-permute-start.3 = (bf16[64,4224]{1,0:T(8,128)(2,1)S(1)}, bf16[64,4224]{1,0:T(8,128)(2,1)}, u32[]{:S(2)}, u32[]{:S(2)}) collective-permute-start(bf16[64,4224]{1,0:T(8,128)(2,1)S(1)} %extend_rows.1.refs_0_), channel_id=1, source_target_pairs={{24,0},{25,1},{26,2},{27,3},{28,4},{29,5},{30,6},{31,7},{0,8},{1,9... | collective-permute-start | bytes 1622024 | tf_op jit(solution)/shard_map/ppermute | solution.py:192
  11.4 46.3 %collective-permute-start.5 = (bf16[64,4224]{1,0:T(8,128)(2,1)S(1)}, bf16[64,4224]{1,0:T(8,128)(2,1)}, u32[]{:S(2)}, u32[]{:S(2)}) collective-permute-start(bf16[64,4224]{1,0:T(8,128)(2,1)S(1)} %extend_rows.1.refs_0_), channel_id=1, source_target_pairs={{16,0},{17,1},{18,2},{19,3},{20,4},{21,5},{22,6},{23,7},{24,8},{25... | collective-permute-start | bytes 1622024 | tf_op jit(solution)/shard_map/ppermute | solution.py:192
  12.4 51.6 %collective-permute-start = (bf16[64,4224]{1,0:T(8,128)(2,1)S(1)}, bf16[64,4224]{1,0:T(8,128)(2,1)S(1)}, u32[]{:S(2)}, u32[]{:S(2)}) collective-permute-start(bf16[64,4224]{1,0:T(8,128)(2,1)S(1)} %extend_rows.1.refs_0_), channel_id=1, source_target_pairs={{0,2},{1,3},{2,0},{3,1},{4,6},{5,7},{6,4},{7,5},{8,10},{9,11},{10,... | collective-permute-start | bytes 1622024 | tf_op jit(solution)/shard_map/ppermute | solution.py:188
  24.0 40.8 %collective-permute-start.2 = (bf16[64,4224]{1,0:T(8,128)(2,1)}, bf16[64,4224]{1,0:T(8,128)(2,1)}, u32[]{:S(2)}, u32[]{:S(2)}) collective-permute-start(bf16[64,4224]{1,0:T(8,128)(2,1)} %collective-permute-done.1.refs_1_), channel_id=1, source_target_pairs={{0,2},{1,3},{2,0},{3,1},{4,6},{5,7},{6,4},{7,5},{8,10},{9,11},{10,... | collective-permute-start | bytes 1622024 | tf_op jit(solution)/shard_map/ppermute | solution.py:188
  36.7 28.6 %collective-permute-start.4 = (bf16[64,4224]{1,0:T(8,128)(2,1)}, bf16[64,4224]{1,0:T(8,128)(2,1)}, u32[]{:S(2)}, u32[]{:S(2)}) collective-permute-start(bf16[64,4224]{1,0:T(8,128)(2,1)} %collective-permute-done.3.refs_2_), channel_id=1, source_target_pairs={{0,2},{1,3},{2,0},{3,1},{4,6},{5,7},{6,4},{7,5},{8,10},{9,11},{10,... | collective-permute-start | bytes 1622024 | tf_op jit(solution)/shard_map/ppermute | solution.py:188
  57.6 13.5 %collective-permute-start.6 = (bf16[64,4224]{1,0:T(8,128)(2,1)}, bf16[64,4224]{1,0:T(8,128)(2,1)}, u32[]{:S(2)}, u32[]{:S(2)}) collective-permute-start(bf16[64,4224]{1,0:T(8,128)(2,1)} %collective-permute-done.5.refs_3_), channel_id=1, source_target_pairs={{0,2},{1,3},{2,0},{3,1},{4,6},{5,7},{6,4},{7,5},{8,10},{9,11},{10,... | collective-permute-start | bytes 1622024 | tf_op jit(solution)/shard_map/ppermute | solution.py:188
  59.1 18.9 %collective-permute-start.9 = (bf16[64,4224]{1,0:T(8,128)(2,1)S(1)}, bf16[64,4224]{1,0:T(8,128)(2,1)S(1)}, u32[]{:S(2)}, u32[]{:S(2)}) collective-permute-start(bf16[64,4224]{1,0:T(8,128)(2,1)S(1)} %extend_rows.1.refs_0_), channel_id=1, source_target_pairs={{0,4},{1,5},{2,6},{3,7},{4,0},{5,1},{6,2},{7,3},{8,12},{9,13},{10,... | collective-permute-start | bytes 1622024 | tf_op jit(solution)/shard_map/ppermute | solution.py:188
  64.0 0.8 copy-start.8
  64.8 51.0 %collective-permute-start.17 = (bf16[96,4224]{1,0:T(8,128)(2,1)}, bf16[96,4224]{1,0:T(8,128)(2,1)S(1)}, u32[]{:S(2)}, u32[]{:S(2)}) collective-permute-start(bf16[96,4224]{1,0:T(8,128)(2,1)} %get-tuple-element.24), channel_id=1, source_target_pairs={{0,1},{1,0},{2,3},{3,2},{4,5},{5,4},{6,7},{7,6},{8,9},{9,8},{10,11... | collective-permute-start | bytes 2433032 | tf_op jit(solution)/shard_map/ppermute | solution.py:188
  64.8 21.2 %collective-permute-start.10 = (bf16[64,4224]{1,0:T(8,128)(2,1)}, bf16[64,4224]{1,0:T(8,128)(2,1)}, u32[]{:S(2)}, u32[]{:S(2)}) collective-permute-start(bf16[64,4224]{1,0:T(8,128)(2,1)} %collective-permute-done.1.refs_1_), channel_id=1, source_target_pairs={{0,4},{1,5},{2,6},{3,7},{4,0},{5,1},{6,2},{7,3},{8,12},{9,13},{10,... | collective-permute-start | bytes 1622024 | tf_op jit(solution)/shard_map/ppermute | solution.py:188
  65.3 32.3 %collective-permute-start.11 = (bf16[64,4224]{1,0:T(8,128)(2,1)}, bf16[64,4224]{1,0:T(8,128)(2,1)}, u32[]{:S(2)}, u32[]{:S(2)}) collective-permute-start(bf16[64,4224]{1,0:T(8,128)(2,1)} %collective-permute-done.3.refs_2_), channel_id=1, source_target_pairs={{0,4},{1,5},{2,6},{3,7},{4,0},{5,1},{6,2},{7,3},{8,12},{9,13},{10,... | collective-permute-start | bytes 1622024 | tf_op jit(solution)/shard_map/ppermute | solution.py:188
  71.1 35.8 %collective-permute-start.12 = (bf16[64,4224]{1,0:T(8,128)(2,1)}, bf16[64,4224]{1,0:T(8,128)(2,1)}, u32[]{:S(2)}, u32[]{:S(2)}) collective-permute-start(bf16[64,4224]{1,0:T(8,128)(2,1)} %collective-permute-done.5.refs_3_), channel_id=1, source_target_pairs={{0,4},{1,5},{2,6},{3,7},{4,0},{5,1},{6,2},{7,3},{8,12},{9,13},{10,... | collective-permute-start | bytes 1622024 | tf_op jit(solution)/shard_map/ppermute | solution.py:188
  72.7 1.0 copy-start.9
  77.2 0.9 copy-start.2
  78.1 0.8 copy-start.6
  78.9 49.6 %collective-permute-start.16 = (bf16[96,4224]{1,0:T(8,128)(2,1)}, bf16[96,4224]{1,0:T(8,128)(2,1)S(1)}, u32[]{:S(2)}, u32[]{:S(2)}) collective-permute-start(bf16[96,4224]{1,0:T(8,128)(2,1)} %get-tuple-element.22), channel_id=1, source_target_pairs={{0,1},{1,0},{2,3},{3,2},{4,5},{5,4},{6,7},{7,6},{8,9},{9,8},{10,11... | collective-permute-start | bytes 2433032 | tf_op jit(solution)/shard_map/ppermute | solution.py:188
  106.9 1.0 copy-start.7
  111.2 0.9 copy-start.4
  112.1 0.8 copy-start.12
  112.9 0.7 copy-start.13
  113.6 26.4 %collective-permute-start.15 = (bf16[96,4224]{1,0:T(8,128)(2,1)}, bf16[96,4224]{1,0:T(8,128)(2,1)}, u32[]{:S(2)}, u32[]{:S(2)}) collective-permute-start(bf16[96,4224]{1,0:T(8,128)(2,1)} %get-tuple-element.20), channel_id=1, source_target_pairs={{0,1},{1,0},{2,3},{3,2},{4,5},{5,4},{6,7},{7,6},{8,9},{9,8},{10,11... | collective-permute-start | bytes 2433032 | tf_op jit(solution)/shard_map/ppermute | solution.py:188
  113.8 34.4 %collective-permute-start.13 = (bf16[96,2048]{1,0:T(8,128)(2,1)}, bf16[96,2048]{1,0:T(8,128)(2,1)S(1)}, u32[]{:S(2)}, u32[]{:S(2)}) collective-permute-start(bf16[96,2048]{1,0:T(8,128)(2,1)} %copy-done.13), channel_id=1, source_target_pairs={{0,2},{1,3},{2,0},{3,1},{4,6},{5,7},{6,4},{7,5},{8,10},{9,11},{10,... | collective-permute-start | bytes 1179656 | tf_op jit(solution)/shard_map/ppermute | solution.py:188
  114.4 33.8 %collective-permute-start.14 = (bf16[96,2048]{1,0:T(8,128)(2,1)}, bf16[96,2048]{1,0:T(8,128)(2,1)S(1)}, u32[]{:S(2)}, u32[]{:S(2)}) collective-permute-start(bf16[96,2048]{1,0:T(8,128)(2,1)} %copy-done.12), channel_id=1, source_target_pairs={{0,3},{1,2},{2,1},{3,0},{4,7},{5,6},{6,5},{7,4},{8,11},{9,10},{10,... | collective-permute-start | bytes 1179656 | tf_op jit(solution)/shard_map/ppermute | solution.py:188
  115.8 32.5 %collective-permute-start.7 = (bf16[96,2176]{1,0:T(8,128)(2,1)S(1)}, bf16[96,2176]{1,0:T(8,128)(2,1)S(1)}, u32[]{:S(2)}, u32[]{:S(2)}) collective-permute-start(bf16[96,2176]{1,0:T(8,128)(2,1)S(1)} %get-tuple-element.15), channel_id=1, source_target_pairs={{0,4},{1,5},{2,6},{3,7},{4,0},{5,1},{6,2},{7,3},{8,12},{9,13},{10,... | collective-permute-start | bytes 1253384 | tf_op jit(solution)/shard_map/ppermute | solution.py:188
  117.3 3.4 %copy-start = (bf16[1,4096,1024]{2,1,0:T(8,128)(2,1)S(1)}, bf16[1,4096,1024]{2,1,0:T(8,128)(2,1)}, u32[]{:S(2)}) copy-start(bf16[1,4096,1024]{2,1,0:T(8,128)(2,1)} %refs_4_.1) | copy-start | bytes 25165828
  120.7 8.0 %copy-start.3 = (bf16[96,4224]{1,0:T(8,128)(2,1)S(1)}, bf16[96,4224]{1,0:T(8,128)(2,1)}, u32[]{:S(2)}) copy-start(bf16[96,4224]{1,0:T(8,128)(2,1)} %copy-done.2) | copy-start | bytes 2433028
  128.5 19.7 %collective-permute-start.8 = (bf16[96,2176]{1,0:T(8,128)(2,1)}, bf16[96,2176]{1,0:T(8,128)(2,1)S(1)}, u32[]{:S(2)}, u32[]{:S(2)}) collective-permute-start(bf16[96,2176]{1,0:T(8,128)(2,1)} %get-tuple-element.16), channel_id=1, source_target_pairs={{0,5},{1,4},{2,7},{3,6},{4,1},{5,0},{6,3},{7,2},{8,13},{9,12},{10,... | collective-permute-start | bytes 1253384 | tf_op jit(solution)/shard_map/ppermute | solution.py:188
  128.7 3.4 %copy-start.1 = (bf16[1,4096,1024]{2,1,0:T(8,128)(2,1)S(1)}, bf16[1,4096,1024]{2,1,0:T(8,128)(2,1)}, u32[]{:S(2)}) copy-start(bf16[1,4096,1024]{2,1,0:T(8,128)(2,1)} %refs_4_.1) | copy-start | bytes 25165828
  132.1 8.0 %copy-start.5 = (bf16[96,4224]{1,0:T(8,128)(2,1)S(1)}, bf16[96,4224]{1,0:T(8,128)(2,1)}, u32[]{:S(2)}) copy-start(bf16[96,4224]{1,0:T(8,128)(2,1)} %copy-done.4) | copy-start | bytes 2433028
  132.1 16.2 %slice-start = ((s8[8388608]{0:T(1024)(128)(4,1)}), s8[4194304]{0:T(1024)(128)(4,1)S(1)}, s32[]{:S(2)}) async-start(s8[8388608]{0:T(1024)(128)(4,1)} %bitcast.10), calls=%async_computation.1 | async-start | bytes 8388608
  140.0 8.3 %slice-start.1 = ((s8[8388608]{0:T(1024)(128)(4,1)}), s8[4194304]{0:T(1024)(128)(4,1)S(1)}, s32[]{:S(2)}) async-start(s8[8388608]{0:T(1024)(128)(4,1)} %bitcast.10), calls=%async_computation.2 | async-start | bytes 8388608
where the time goes:
time: 169 us
  waiting for transfers between devices  73 us (43%)
  Pallas kernels  42.1 us (25%)
  local copies, waits for them, and re-layouts  20.7 us (12%)
  starting transfers between devices  20.7 us (12%)
  blocking collectives  11.8 us (7%)
    ppermute x3, waiting for transfers between devices, turn(): lax.ppermute(value, AXES, [(a * planes + b, c * planes + d) for (a, b), (...  40.8 us
    ppermute x15, waiting for transfers between devices, swap(): return lax.ppermute(value, AXES, [(i, i ^ bits) for i in range(devices)])  32.2 us
    pallas_call x4, Pallas kernels, sketch(): pl.pallas_call(body, grid=(steps,), out_shape=jax.ShapeDtypeStruct(total....  31.7 us
    unnamed x37, local copies, waits for them, and re-layouts  18.9 us
    ppermute x15, starting transfers between devices, swap(): return lax.ppermute(value, AXES, [(i, i ^ bits) for i in range(devices)])  14.7 us
    all_to_all x1, blocking collectives, on_device(): owned = lax.all_to_all(total, AXES, split_axis=0, concat_axis=0, tiled=True)  11.8 us
    pallas_call x3, Pallas kernels, compact(): pl.pallas_call(body, out_shape=[jax.ShapeDtypeStruct((count * capacity, b...  10 us
    ppermute x3, starting transfers between devices, turn(): lax.ppermute(value, AXES, [(a * planes + b, c * planes + d) for (a, b), (...  6.06 us
  transfers between devices with their start and end apart: 18, of which 7 were waited for; matrix products, arithmetic and copies ran while one was open for 0% of the time, Pallas kernels for 20%

commit v1 on v0

v1 whole, which is shorter than its diff:
```python
import functools

import jax
import jax.numpy as jnp
from jax import lax
from jax.experimental import pallas as pl
from jax.experimental.pallas import tpu as pltpu
from jax.sharding import PartitionSpec as P

AXES = ("expert", "dp")
LANES = 128
MIB = 1 << 20


def place(width, first):
    rows = lax.broadcasted_iota(jnp.int32, (width, LANES), 0)
    lanes = lax.broadcasted_iota(jnp.int32, (width, LANES), 1)
    return (lanes == rows + first).astype(jnp.bfloat16)


def dot(a, b):
    return jnp.dot(a, b, preferred_element_type=jnp.float32)


def across(a, b, over):
    return lax.dot_general(a, b, ((over[:1], over[1:]), ((), ())), preferred_element_type=jnp.float32)


def extend_kernel(rank, top, tokens, grads, proj, routes, gates, docs, out):
    width = tokens.shape[1]
    small = jnp.float32
    projected = across(grads[...], proj[...], (1, 1)).astype(jnp.bfloat16)
    meta = dot(projected, place(rank, 0))
    meta += across(gates[...], place(top, rank), (0, 0))
    meta += across(routes[...].astype(small).astype(jnp.bfloat16), place(top, rank + top), (0, 0))
    doc = jnp.concatenate([docs[...].astype(small)] * 8, axis=0).astype(jnp.bfloat16)
    meta += across(doc, place(8, rank + 2 * top), (0, 0))
    out[:, :width] = tokens[...]
    out[:, width:] = meta.astype(jnp.bfloat16)


def extend(tokens, out_grad, proj_out, routes, gate_probs, doc_ids):
    rows, width = tokens.shape
    body = functools.partial(extend_kernel, proj_out.shape[1], routes.shape[1])
    return pl.pallas_call(
        body,
        out_shape=jax.ShapeDtypeStruct((rows, width + LANES), jnp.bfloat16),
        compiler_params=pltpu.CompilerParams(vmem_limit_bytes=16 * MIB),
        name="extend_rows",
    )(tokens, out_grad, proj_out.T, routes.T, gate_probs.T, doc_ids.reshape(1, rows))


def compact_kernel(capacity, top, rank, spans, parts, experts, after, *refs):
    count = len(refs) - len(parts)
    sources, outs = refs[:count], refs[count:]
    rows, total = sources[0].shape
    width = total - LANES
    meta = jnp.concatenate([s[:, width:] for s in sources], axis=0).astype(jnp.float32)
    lanes = lax.broadcasted_iota(jnp.int32, meta.shape, 1)
    is_route = (lanes >= rank + top) & (lanes < rank + 2 * top)
    named_by = sorted({q for members in parts for q in members})
    hits = jnp.zeros(meta.shape, jnp.float32)
    for q in named_by:
        named = is_route & (meta == experts[q].astype(jnp.float32))
        hit = jnp.sum(named.astype(jnp.float32), axis=1, keepdims=True)
        hits = jnp.where(lanes == q, hit, hits)
    every = count * rows
    here = lax.broadcasted_iota(jnp.int32, (every, every), 0)
    other = lax.broadcasted_iota(jnp.int32, (every, every), 1)
    earlier = ((other < here) & (other // rows == here // rows)).astype(jnp.bfloat16)
    before = dot(earlier, hits.astype(jnp.bfloat16))
    first = (lax.broadcasted_iota(jnp.int32, meta.shape, 0) // rows * capacity).astype(jnp.float32)
    slots = jnp.where(hits > 0, before + first, -1.0).T
    step = 4 * LANES
    for out, members, (low, high, start, stop) in zip(outs, parts, spans):
        picked = (high - low) * capacity
        spot = lax.broadcasted_iota(jnp.int32, (picked, (high - low) * rows), 0) + low * capacity
        spot = spot.astype(jnp.float32)
        pick = jnp.concatenate(
            [
                (spot == slots[q : q + 1, low * rows : high * rows]).astype(jnp.bfloat16)
                for q in members
            ],
            axis=0,
        )
        for at in range(start, stop, step):
            end = min(at + step, stop)
            block = jnp.concatenate([s[:, at:end] for s in sources[low:high]], axis=0)
            found = dot(pick, block)
            for i in range(len(members)):
                out[i, :, at - start : end - start] = found[
                    i * picked : (i + 1) * picked
                ].astype(jnp.bfloat16)


def compact(sources, experts, parts, spans, after, capacity, top, rank):
    body = functools.partial(compact_kernel, capacity, top, rank, tuple(spans), tuple(parts))
    size = sum(s.size for s in sources)
    shapes = [
        jax.ShapeDtypeStruct((len(p), (high - low) * capacity, stop - start), jnp.bfloat16)
        for p, (low, high, start, stop) in zip(parts, spans)
    ]
    return pl.pallas_call(
        body,
        out_shape=shapes,
        in_specs=[pl.BlockSpec(memory_space=pltpu.SMEM)]
        + [pl.BlockSpec(memory_space=pltpu.VMEM)] * (1 + len(sources)),
        out_specs=[pl.BlockSpec(memory_space=pltpu.VMEM)] * len(parts),
        compiler_params=pltpu.CompilerParams(vmem_limit_bytes=16 * MIB),
        cost_estimate=pl.CostEstimate(flops=4 * 10**8, bytes_accessed=4 * size, transcendentals=0),
        name="compact_rows",
    )(experts, after, *sources)


def hold_kernel(gate_w, up_w, gate_out, up_out, done, sems):
    copies = [
        pltpu.make_async_copy(gate_w.at[0], gate_out, sems.at[0]),
        pltpu.make_async_copy(up_w.at[0], up_out, sems.at[1]),
    ]
    for copy in copies:
        copy.start()
    for copy in copies:
        copy.wait()
    done[...] = jnp.zeros_like(done)


def hold(w_gate, w_up):
    shape = w_gate.shape[1:]
    return pl.pallas_call(
        hold_kernel,
        out_shape=[pltpu.VMEM(shape, jnp.bfloat16)] * 2
        + [jax.ShapeDtypeStruct((8, LANES), jnp.float32)],
        in_specs=[pl.BlockSpec(memory_space=pltpu.HBM)] * 2,
        out_specs=[pl.BlockSpec(memory_space=pltpu.VMEM)] * 3,
        scratch_shapes=[pltpu.SemaphoreType.DMA((2,))],
        compiler_params=pltpu.CompilerParams(vmem_limit_bytes=2 * MIB),
        cost_estimate=pl.CostEstimate(flops=0, bytes_accessed=16 * MIB, transcendentals=0),
        name="hold_weights",
    )(*[pltpu.with_memory_space_constraint(w, pltpu.HBM) for w in (w_gate, w_up)])


def sketch_kernel(spots, top, rank, docs_total, expert, *refs):
    pieces = refs[: len(spots)]
    gate_w, up_w, proj, total_in, total_out, rows_at, hidden_at = refs[len(spots) :]
    width, hidden = gate_w.shape
    for ref, (lead, row, column) in zip(pieces, spots):
        r, c = ref.shape[1:]
        if r % 16:
            below = row + r // 16 * 16
            rows_at[below : below + 16, column : column + c] = jnp.zeros((16, c), jnp.bfloat16)
        rows_at[row : row + r, column : column + c] = ref[lead]

    rows = rows_at[:, :width]
    tile = 256
    for at in range(0, hidden, tile):
        gate_part = dot(rows, gate_w[:, at : at + tile])
        up_part = dot(rows, up_w[:, at : at + tile])
        value = gate_part / (1.0 + jnp.exp(-gate_part)) * up_part
        hidden_at[:, at : at + tile] = value.astype(jnp.bfloat16)

    wide_proj = jnp.concatenate([proj[...]] * (LANES // rank), axis=0)
    side = across(hidden_at[...], wide_proj, (1, 1))
    meta = rows_at[:, width:]
    wide = meta.astype(jnp.float32)
    lanes = lax.broadcasted_iota(jnp.int32, wide.shape, 1)
    is_route = (lanes >= rank + top) & (lanes < rank + 2 * top)
    named = (is_route & (wide == expert[0].astype(jnp.float32))).astype(jnp.float32)
    gate = jnp.sum(wide * pltpu.roll(named, LANES - top, 1), axis=1, keepdims=True)
    spread_from = lax.broadcasted_iota(jnp.int32, (LANES, rank * rank), 0)
    spread_to = lax.broadcasted_iota(jnp.int32, (LANES, rank * rank), 1) // rank
    spread = (spread_from == spread_to).astype(jnp.bfloat16)
    output_side = dot(meta, spread) * gate
    outer = output_side * jnp.concatenate([side] * (rank * rank // LANES), axis=1)
    doc = jnp.sum(jnp.where(lanes == rank + 2 * top, wide, 0.0), axis=1, keepdims=True)
    ids = lax.broadcasted_iota(jnp.int32, (wide.shape[0], docs_total), 1).astype(jnp.float32)
    table = (ids == doc).astype(jnp.bfloat16)
    high = outer.astype(jnp.bfloat16)
    low = (outer - high.astype(jnp.float32)).astype(jnp.bfloat16)
    total = total_in[...]
    for part in (high, low):
        total += across(table, part, (0, 0))
    total_out[...] = total


def sketch(pieces, expert, weights, proj, total, top, rank):
    width, hidden = weights[0].shape
    rows, arrays, spots = 0, [], []
    for beside in pieces:
        for array, lead, column in beside:
            arrays.append(array)
            spots.append((lead, rows, column))
        rows += -(-beside[0][0].shape[1] // 16) * 16
    body = functools.partial(sketch_kernel, tuple(spots), top, rank, total.shape[0])
    vmem = pl.BlockSpec(memory_space=pltpu.VMEM)
    return pl.pallas_call(
        body,
        out_shape=jax.ShapeDtypeStruct(total.shape, jnp.float32),
        in_specs=[pl.BlockSpec(memory_space=pltpu.SMEM)] + [vmem] * (len(arrays) + 4),
        out_specs=vmem,
        scratch_shapes=[
            pltpu.VMEM((rows, width + LANES), jnp.bfloat16),
            pltpu.VMEM((rows, hidden), jnp.bfloat16),
        ],
        compiler_params=pltpu.CompilerParams(vmem_limit_bytes=20 * MIB),
        cost_estimate=pl.CostEstimate(
            flops=4 * rows * width * hidden,
            bytes_accessed=2 * rows * width,
            transcendentals=rows * hidden,
        ),
        name="sketch_rows",
    )(expert, *arrays, *weights, proj, total)


def on_device(tokens, out_grad, routes, gate_probs, doc_ids, w_gate, w_up, proj_hidden, proj_out):
    groups, planes = lax.axis_size("expert"), lax.axis_size("dp")
    devices = groups * planes
    row_count, width = tokens.shape
    top = routes.shape[1]
    rank = proj_out.shape[1]
    capacity = max(2, 3 * row_count * top // (2 * devices))
    me = lax.axis_index(AXES).astype(jnp.int32)

    def swap(value, bits):
        return lax.ppermute(value, AXES, [(i, i ^ bits) for i in range(devices)])

    def turn(value, by):
        pairs = [(((g + by) % groups, p), (g, p)) for g in range(groups) for p in range(planes)]
        return lax.ppermute(
            value, AXES, [(a * planes + b, c * planes + d) for (a, b), (c, d) in pairs]
        )

    ext = extend(tokens, out_grad, proj_out, routes, gate_probs, doc_ids)
    order = sorted(range(groups), key=lambda j: min(j, groups - j))
    slots = [ext if j == 0 else turn(ext, j) for j in order]
    bits = [1 << b for b in range(1, planes.bit_length() - 1)]
    last = sum(bits)
    masks = sorted(range(2, last, 2), key=lambda m: bin(m).count("1"))
    ends = [i for i, m in enumerate(masks) if m ^ last in bits]
    hops = [last ^ masks[i] for i in ends]
    tiles = (width + LANES) // LANES
    cuts = [LANES * (tiles * i // len(bits)) for i in range(len(bits) + 1)]
    full = (0, width + LANES)
    *weights, held = hold(w_gate, w_up)
    total = jnp.zeros((devices, rank * rank), jnp.float32)
    experts = jnp.stack([me, me ^ 1] + [me ^ hop ^ b for hop in hops for b in (0, 1)])
    own = me.reshape(1)
    args = (held, capacity, top, rank)

    def add(pieces):
        return sketch(pieces, own, weights, proj_hidden.T, total, top, rank)

    phases = [range(groups - 2), [groups - 2], [groups - 1]]
    waiting = []
    for phase in phases:
        n = len(phase)
        if phase is phases[-1]:
            slots[-1], total, *early = lax.optimization_barrier((slots[-1], total, *early))
        columns = {0: [slots[i] for i in phase]}
        for mask in masks:
            low = mask & -mask
            columns[mask] = [swap(s, low) for s in columns[mask ^ low]]
        if phase is phases[-1]:
            mine = compact(slots, experts, [(0,), (1,)], [(0, groups) + full] * 2, *args)
            total = add(waiting + [[(mine[0], 0, 0)], [(swap(mine[1], 1), 0, 0)]])
            columns, total = lax.optimization_barrier((columns, total))
        parts, spans = [(0,), (1,)], [(0, n * len(masks)) + full] * 2
        for k, i in enumerate(ends):
            parts.append((2 + 2 * k, 3 + 2 * k))
            spans.append((n * i, n * i + n, cuts[k], cuts[k + 1]))
        sources = [s for mask in masks for s in columns[mask]]
        found = compact(sources, experts, parts, spans, *args)
        arrived = [swap(f, hop) for f, hop in zip(found[2:], hops)]
        beside = [swap(f, 1) for f in arrived]
        far = [
            [(f, 0, cuts[k]) for k, f in enumerate(arrived)],
            [(f, 1, cuts[k]) for k, f in enumerate(beside)],
        ]
        near = [[(found[0], 0, 0)], [(swap(found[1], 1), 0, 0)]]
        if phase is phases[-1]:
            total = add(near + far)
        else:
            total = add(waiting + near)
            if not waiting:
                early = arrived
            waiting = far
    owned = lax.all_to_all(total, AXES, split_axis=0, concat_axis=0, tiled=True)
    return owned[None]


def solution(mesh):
    placed = (
        P(AXES, None),
        P(AXES, None),
        P(AXES, None),
        P(AXES, None),
        P(AXES),
        P(AXES, None, None),
        P(AXES, None, None),
        P(),
        P(),
    )
    return jax.shard_map(
        on_device,
        mesh=mesh,
        in_specs=placed,
        out_specs=P(AXES, None, None),
        check_vma=False,
    )
```

time: 169 us -> 147 us (0.87)
  waiting for transfers between devices: 73 us -> 60.5 us
  Pallas kernels: 42.1 us -> 30 us
  starting transfers between devices: 20.7 us -> 25.1 us
    ppermute x3, waiting for transfers between devices: 40.8 us -> 17.7 us  [turn(): lax.ppermute(value, AXES, [(a * planes + b, c * planes + d) for (a, b), (...]
    pallas_call x7 -> x9, Pallas kernels: 41.7 us -> 29.6 us  [the longest x4 16.5 us: sketch(): pl.pallas_call(body, out_shape=jax.ShapeDtypeStruct(total.shape, jnp.floa...]
    ppermute x15 -> x24, waiting for transfers between devices: 32.2 us -> 42.8 us  [swap(): return lax.ppermute(value, AXES, [(i, i ^ bits) for i in range(devices)])]
    ppermute x3, starting transfers between devices: 6.06 us -> 9.89 us  [turn(): lax.ppermute(value, AXES, [(a * planes + b, c * planes + d) for (a, b), (...]
    unnamed x37 -> x22, local copies, waits for them, and re-layouts: 18.9 us -> 18.3 us
    ppermute x15 -> x24, starting transfers between devices: 14.7 us -> 15.2 us  [swap(): return lax.ppermute(value, AXES, [(i, i ^ bits) for i in range(devices)])]
  transfers between devices with their start and end apart: 18 -> 27, of which waited for: 7 -> 9; matrix products, arithmetic and copies ran while one was open for 0% -> 0% of each run, Pallas kernels for 20% -> 16%
where the time goes in v1:
time: 147 us
  waiting for transfers between devices  60.5 us (41%)
  Pallas kernels  30 us (20%)
  starting transfers between devices  25.1 us (17%)
  local copies, waits for them, and re-layouts  19.3 us (13%)
  blocking collectives  12 us (8%)
    ppermute x24, waiting for transfers between devices, swap(): return lax.ppermute(value, AXES, [(i, i ^ bits) for i in range(devices)])  42.8 us
    unnamed x22, local copies, waits for them, and re-layouts  18.3 us
    ppermute x3, waiting for transfers between devices, turn(): lax.ppermute(value, AXES, [(a * planes + b, c * planes + d) for (a, b), (...  17.7 us
    pallas_call x4, Pallas kernels, sketch(): pl.pallas_call(body, out_shape=jax.ShapeDtypeStruct(total.shape, jnp.floa...  16.5 us
    ppermute x24, starting transfers between devices, swap(): return lax.ppermute(value, AXES, [(i, i ^ bits) for i in range(devices)])  15.2 us
    all_to_all x1, blocking collectives, on_device(): owned = lax.all_to_all(total, AXES, split_axis=0, concat_axis=0, tiled=True)  12 us
    ppermute x3, starting transfers between devices, turn(): lax.ppermute(value, AXES, [(a * planes + b, c * planes + d) for (a, b), (...  9.89 us
    pallas_call x4, Pallas kernels, compact(): pl.pallas_call(body, out_shape=shapes, in_specs=[pl.BlockSpec(memory_spac...  7.22 us
  transfers between devices with their start and end apart: 27, of which 9 were waited for; matrix products, arithmetic and copies ran while one was open for 0% of the time, Pallas kernels for 16%

profile of v1, /device:TPU:0, one launch (start us, length us, event | category | flops | bytes accessed | tf_op | source)
XLA Modules:
  0.0 147.0 jit_solution(1052687561596615180)
XLA Ops:
  0.0 1.0 copy-done.5
  1.0 1.0 copy-done.6
  2.1 0.9 copy-done.7
  3.0 0.7 copy-done.8
  3.7 0.7 copy-done.9
  4.4 0.7 copy-done.10
  5.5 5.0 %collective-permute-start.2 = (bf16[64,4224]{1,0:T(8,128)(2,1)S(1)}, bf16[64,4224]{1,0:T(8,128)(2,1)S(1)}, u32[]{:S(2)}, u32[]{:S(2)}) collective-permute-start(bf16[64,4224]{1,0:T(8,128)(2,1)S(1)} %extend_rows.1.refs_0_), channel_id=1, source_target_pairs={{8,0},{9,1},{10,2},{11,3},{12,4},{13,5},{14,6},{15,7},{16,8},{17,9... | collective-permute-start | bytes 1622024 | tf_op jit(solution)/shard_map/ppermute | solution.py:228
  10.5 1.5 %collective-permute-start.1 = (bf16[64,4224]{1,0:T(8,128)(2,1)S(1)}, bf16[64,4224]{1,0:T(8,128)(2,1)S(1)}, u32[]{:S(2)}, u32[]{:S(2)}) collective-permute-start(bf16[64,4224]{1,0:T(8,128)(2,1)S(1)} %extend_rows.1.refs_0_), channel_id=1, source_target_pairs={{0,2},{1,3},{2,0},{3,1},{4,6},{5,7},{6,4},{7,5},{8,10},{9,11},{10,... | collective-permute-start | bytes 1622024 | tf_op jit(solution)/shard_map/ppermute | solution.py:224
  12.0 1.5 %collective-permute-start.4 = (bf16[64,4224]{1,0:T(8,128)(2,1)S(1)}, bf16[64,4224]{1,0:T(8,128)(2,1)S(1)}, u32[]{:S(2)}, u32[]{:S(2)}) collective-permute-start(bf16[64,4224]{1,0:T(8,128)(2,1)S(1)} %extend_rows.1.refs_0_), channel_id=1, source_target_pairs={{0,4},{1,5},{2,6},{3,7},{4,0},{5,1},{6,2},{7,3},{8,12},{9,13},{10,... | collective-permute-start | bytes 1622024 | tf_op jit(solution)/shard_map/ppermute | solution.py:224
  13.6 8.5 %collective-permute-done.2.refs_1_ = bf16[64,4224]{1,0:T(8,128)(2,1)S(1)} collective-permute-done((bf16[64,4224]{1,0:T(8,128)(2,1)S(1)}, bf16[64,4224]{1,0:T(8,128)(2,1)S(1)}, u32[]{:S(2)}, u32[]{:S(2)}) %collective-permute-start.2) | collective-permute-done | bytes 540704 | tf_op jit(solution)/shard_map/ppermute | solution.py:228
  22.1 1.5 %collective-permute-start.3 = (bf16[64,4224]{1,0:T(8,128)(2,1)S(1)}, bf16[64,4224]{1,0:T(8,128)(2,1)S(1)}, u32[]{:S(2)}, u32[]{:S(2)}) collective-permute-start(bf16[64,4224]{1,0:T(8,128)(2,1)S(1)} %collective-permute-done.2.refs_1_), channel_id=1, source_target_pairs={{0,2},{1,3},{2,0},{3,1},{4,6},{5,7},{6,4},{7,5},{8,10},{9,11},{10,... | collective-permute-start | bytes 1622024 | tf_op jit(solution)/shard_map/ppermute | solution.py:224
  23.6 1.5 %collective-permute-start.5 = (bf16[64,4224]{1,0:T(8,128)(2,1)S(1)}, bf16[64,4224]{1,0:T(8,128)(2,1)}, u32[]{:S(2)}, u32[]{:S(2)}) collective-permute-start(bf16[64,4224]{1,0:T(8,128)(2,1)S(1)} %collective-permute-done.2.refs_1_), channel_id=1, source_target_pairs={{0,4},{1,5},{2,6},{3,7},{4,0},{5,1},{6,2},{7,3},{8,12},{9,13},{10,... | collective-permute-start | bytes 1622024 | tf_op jit(solution)/shard_map/ppermute | solution.py:224
  25.5 5.8 %hold_weights.1 = (bf16[4096,1024]{1,0:T(8,128)(2,1)S(1)}, bf16[4096,1024]{1,0:T(8,128)(2,1)S(1)}, f32[8,128]{1,0:T(8,128)S(1)}) custom-call(bf16[1,4096,1024]{2,1,0:T(8,128)(2,1)} %gate_w.1, bf16[1,4096,1024]{2,1,0:T(8,128)(2,1)} %up_w.1), custom_call_target="tpu_custom_call" | custom-call | bytes 16777216 | tf_op jit(solution)/shard_map/hold_weights/pallas_call | solution.py:129
  31.4 3.3 %copy-done = bf16[4096,1024]{1,0:T(8,128)(2,1)} copy-done((bf16[4096,1024]{1,0:T(8,128)(2,1)}, bf16[4096,1024]{1,0:T(8,128)(2,1)S(1)}, u32[]{:S(2)}) %copy-start) | copy-done | bytes 8388632
  34.7 3.2 %copy-done.2 = bf16[4096,1024]{1,0:T(8,128)(2,1)} copy-done((bf16[4096,1024]{1,0:T(8,128)(2,1)}, bf16[4096,1024]{1,0:T(8,128)(2,1)S(1)}, u32[]{:S(2)}) %copy-start.2) | copy-done | bytes 8388632
  38.0 2.6 %compact_rows.4 = (bf16[1,96,4224]{2,1,0:T(8,128)(2,1)S(1)}, bf16[1,96,4224]{2,1,0:T(8,128)(2,1)S(1)}, bf16[2,48,2048]{2,1,0:T(8,128)(2,1)S(1)}, bf16[2,48,2176]{2,1,0:T(8,128)(2,1)S(1)}) custom-call(s32[6]{0:T(128)S(1)} %stack.24.experts, f32[8,128]{1,0:T(8,128)S(1)} %get-tuple-element.27.after, bf16[64,4224]{1,0:T(8,128)(2,1)S(1)} %collective-permute-done.1.refs_0_, ...), custom_call_target="tpu_custom_call" | custom-call | flops 400000000 | bytes 4325376 | tf_op jit(solution)/shard_map/compact_rows/pallas_call | solution.py:103
  40.7 0.6 collective-permute-start.11
  41.3 0.7 collective-permute-start.12
  42.0 1.5 %collective-permute-start.7 = (bf16[2,48,2176]{2,1,0:T(8,128)(2,1)S(1)}, bf16[2,48,2176]{2,1,0:T(8,128)(2,1)S(1)}, u32[]{:S(2)}, u32[]{:S(2)}) collective-permute-start(bf16[2,48,2176]{2,1,0:T(8,128)(2,1)S(1)} %get-tuple-element.29), channel_id=1, source_target_pairs={{0,2},{1,3},{2,0},{3,1},{4,6},{5,7},{6,4},{7,5},{8,10},{9,11},{10,... | collective-permute-start | bytes 1253384 | tf_op jit(solution)/shard_map/ppermute | solution.py:224
  43.5 1.3 collective-permute-start.6
  44.8 19.5 %collective-permute-done.7.refs_1_ = bf16[2,48,2176]{2,1,0:T(8,128)(2,1)S(1)} collective-permute-done((bf16[2,48,2176]{2,1,0:T(8,128)(2,1)S(1)}, bf16[2,48,2176]{2,1,0:T(8,128)(2,1)S(1)}, u32[]{:S(2)}, u32[]{:S(2)}) %collective-permute-start.7) | collective-permute-done | bytes 417824 | tf_op jit(solution)/shard_map/ppermute | solution.py:224
  64.4 1.4 compact_rows.5
  65.8 0.6 collective-permute-start.13
  66.5 4.4 %collective-permute-start = (bf16[64,4224]{1,0:T(8,128)(2,1)S(1)}, bf16[64,4224]{1,0:T(8,128)(2,1)S(1)}, u32[]{:S(2)}, u32[]{:S(2)}) collective-permute-start(bf16[64,4224]{1,0:T(8,128)(2,1)S(1)} %extend_rows.1.refs_0_), channel_id=1, source_target_pairs={{16,0},{17,1},{18,2},{19,3},{20,4},{21,5},{22,6},{23,7},{24,8},{25... | collective-permute-start | bytes 1622024 | tf_op jit(solution)/shard_map/ppermute | solution.py:228
  70.9 3.4 %copy-done.1 = bf16[4096,1024]{1,0:T(8,128)(2,1)S(1)} copy-done((bf16[4096,1024]{1,0:T(8,128)(2,1)S(1)}, bf16[4096,1024]{1,0:T(8,128)(2,1)}, u32[]{:S(2)}) %copy-start.1) | copy-done | bytes 8388632
  74.3 3.4 %copy-done.3 = bf16[4096,1024]{1,0:T(8,128)(2,1)S(1)} copy-done((bf16[4096,1024]{1,0:T(8,128)(2,1)S(1)}, bf16[4096,1024]{1,0:T(8,128)(2,1)}, u32[]{:S(2)}) %copy-start.3) | copy-done | bytes 8388632
  77.6 3.9 %sketch_rows.4.refs_9_ = f32[32,1024]{1,0:T(8,128)S(1)} custom-call(s32[1]{0:T(128)} %bitcast.expert, bf16[1,96,4224]{2,1,0:T(8,128)(2,1)S(1)} %get-tuple-element.34.refs_0_, bf16[1,96,4224]{2,1,0:T(8,128)(2,1)S(1)} %collective-permute-done.14.refs_1_, bf16[4096,1024]{1,0:T(8,128)(2,1)S(1)} %copy-done.1, bf16[4096,1024]{1,0:T(8,128)(2,1)S(1)} %copy-done.3, ...), custom_call_target="tpu_custom_call" | custom-call | flops 3221225472 | bytes 1572864 | tf_op jit(solution)/shard_map/sketch_rows/pallas_call | solution.py:195
  81.6 3.9 %sketch_rows.5.refs_9_ = f32[32,1024]{1,0:T(8,128)S(1)} custom-call(s32[1]{0:T(128)} %bitcast.expert, bf16[2,48,2048]{2,1,0:T(8,128)(2,1)S(1)} %collective-permute-done.6.refs_0_, bf16[2,48,2176]{2,1,0:T(8,128)(2,1)S(1)} %collective-permute-done.7.refs_1_, bf16[2,48,2048]{2,1,0:T(8,128)(2,1)S(1)} %collective-permute-done.8.refs_2_, ...), custom_call_target="tpu_custom_call" | custom-call | flops 3221225472 | bytes 1572864 | tf_op jit(solution)/shard_map/sketch_rows/pallas_call | solution.py:195
  85.5 9.2 %collective-permute-done.refs_3_ = bf16[64,4224]{1,0:T(8,128)(2,1)S(1)} collective-permute-done((bf16[64,4224]{1,0:T(8,128)(2,1)S(1)}, bf16[64,4224]{1,0:T(8,128)(2,1)S(1)}, u32[]{:S(2)}, u32[]{:S(2)}) %collective-permute-start) | collective-permute-done | bytes 540704 | tf_op jit(solution)/shard_map/ppermute | solution.py:228
  94.7 1.7 %compact_rows.6 = (bf16[1,96,4224]{2,1,0:T(8,128)(2,1)S(1)}, bf16[1,96,4224]{2,1,0:T(8,128)(2,1)S(1)}) custom-call(s32[6]{0:T(128)S(1)} %stack.24.experts, f32[8,128]{1,0:T(8,128)S(1)} %get-tuple-element.27.after, bf16[64,4224]{1,0:T(8,128)(2,1)S(1)} %extend_rows.1.refs_0_, bf16[64,4224]{1,0:T(8,128)(2,1)S(1)} %collective-permute-done.2.refs_1_, ...), custom_call_target="tpu_custom_call" | custom-call | flops 400000000 | bytes 4325376 | tf_op jit(solution)/shard_map/compact_rows/pallas_call | solution.py:103
  96.6 0.5 collective-permute-start.18
  97.2 0.5 collective-permute-start.17
  97.7 6.5 %collective-permute-done.18.refs_1_ = bf16[2,24,2176]{2,1,0:T(8,128)(2,1)S(1)} collective-permute-done((bf16[2,24,2176]{2,1,0:T(8,128)(2,1)S(1)}, bf16[2,24,2176]{2,1,0:T(8,128)(2,1)S(1)}, u32[]{:S(2)}, u32[]{:S(2)}) %collective-permute-start.18) | collective-permute-done | bytes 208928 | tf_op jit(solution)/shard_map/ppermute | solution.py:224
  104.2 0.5 collective-permute-start.19
  104.7 1.0 collective-permute-start.15
  105.6 0.5 collective-permute-start.16
  106.1 5.3 %sketch_rows.6.refs_9_ = f32[32,1024]{1,0:T(8,128)S(1)} custom-call(s32[1]{0:T(128)} %bitcast.expert, bf16[2,24,2048]{2,1,0:T(8,128)(2,1)S(1)} %collective-permute-done.17.refs_0_, bf16[2,24,2176]{2,1,0:T(8,128)(2,1)S(1)} %collective-permute-done.18.refs_1_, bf16[2,24,2048]{2,1,0:T(8,128)(2,1)S(1)} %collective-permute-done.19.refs_2_, ...), custom_call_target="tpu_custom_call" | custom-call | flops 4294967296 | bytes 2097152 | tf_op jit(solution)/shard_map/sketch_rows/pallas_call | solution.py:195
  111.5 7.4 %collective-permute-done.15.refs_0_ = bf16[64,4224]{1,0:T(8,128)(2,1)S(1)} collective-permute-done((bf16[64,4224]{1,0:T(8,128)(2,1)S(1)}, bf16[64,4224]{1,0:T(8,128)(2,1)S(1)}, u32[]{:S(2)}, u32[]{:S(2)}) %collective-permute-start.15) | collective-permute-done | bytes 540704 | tf_op jit(solution)/shard_map/ppermute | solution.py:224
  118.8 1.2 collective-permute-done.16.refs_1_
  120.0 1.5 compact_rows.7
  121.5 0.6 collective-permute-start.24
  122.1 0.5 collective-permute-start.23
  122.6 5.4 %collective-permute-done.24.refs_3_ = bf16[2,24,2176]{2,1,0:T(8,128)(2,1)S(1)} collective-permute-done((bf16[2,24,2176]{2,1,0:T(8,128)(2,1)S(1)}, bf16[2,24,2176]{2,1,0:T(8,128)(2,1)S(1)}, u32[]{:S(2)}, u32[]{:S(2)}) %collective-permute-start.24) | collective-permute-done | bytes 208928 | tf_op jit(solution)/shard_map/ppermute | solution.py:224
  128.0 1.4 collective-permute-done.23.refs_2_
  129.4 1.4 collective-permute-done.25.refs_4_
  130.9 3.3 %sketch_rows.7 = f32[32,1024]{1,0:T(8,128)S(1)} custom-call(s32[1]{0:T(128)} %bitcast.expert, bf16[1,48,4224]{2,1,0:T(8,128)(2,1)S(1)} %get-tuple-element.44.refs_0_, bf16[1,48,4224]{2,1,0:T(8,128)(2,1)S(1)} %collective-permute-done.22.refs_1_, bf16[2,24,2048]{2,1,0:T(8,128)(2,1)S(1)} %collective-permute-done.23.refs_2_, ...), custom_call_target="tpu_custom_call" | custom-call | flops 2684354560 | bytes 1310720 | tf_op jit(solution)/shard_map/sketch_rows/pallas_call | solution.py:195
  134.3 12.0 %all_to_all.9 = f32[32,1,1024]{2,1,0:T(1,128)S(1)} all-to-all(f32[32,1,1024]{2,1,0:T(1,128)S(1)} %copy.10), channel_id=1, replica_groups=mesh['expert'=4,'dp'=8] {'expert','dp'}, dimensions={0} | all-to-all | bytes 262144 | tf_op jit(solution)/shard_map/all_to_all | solution.py:286
  146.3 0.7 copy.11
  (43 shorter events, 1.5 us)
Async XLA Ops:
  0.0 1.0 copy-start.5
  1.0 1.0 copy-start.6
  2.1 0.9 copy-start.7
  3.0 0.7 copy-start.8
  3.7 0.7 copy-start.9
  4.4 0.7 copy-start.10
  5.5 16.6 %collective-permute-start.2 = (bf16[64,4224]{1,0:T(8,128)(2,1)S(1)}, bf16[64,4224]{1,0:T(8,128)(2,1)S(1)}, u32[]{:S(2)}, u32[]{:S(2)}) collective-permute-start(bf16[64,4224]{1,0:T(8,128)(2,1)S(1)} %extend_rows.1.refs_0_), channel_id=1, source_target_pairs={{8,0},{9,1},{10,2},{11,3},{12,4},{13,5},{14,6},{15,7},{16,8},{17,9... | collective-permute-start | bytes 1622024 | tf_op jit(solution)/shard_map/ppermute | solution.py:228
  10.5 27.5 %collective-permute-start.1 = (bf16[64,4224]{1,0:T(8,128)(2,1)S(1)}, bf16[64,4224]{1,0:T(8,128)(2,1)S(1)}, u32[]{:S(2)}, u32[]{:S(2)}) collective-permute-start(bf16[64,4224]{1,0:T(8,128)(2,1)S(1)} %extend_rows.1.refs_0_), channel_id=1, source_target_pairs={{0,2},{1,3},{2,0},{3,1},{4,6},{5,7},{6,4},{7,5},{8,10},{9,11},{10,... | collective-permute-start | bytes 1622024 | tf_op jit(solution)/shard_map/ppermute | solution.py:224
  12.0 26.0 %collective-permute-start.4 = (bf16[64,4224]{1,0:T(8,128)(2,1)S(1)}, bf16[64,4224]{1,0:T(8,128)(2,1)S(1)}, u32[]{:S(2)}, u32[]{:S(2)}) collective-permute-start(bf16[64,4224]{1,0:T(8,128)(2,1)S(1)} %extend_rows.1.refs_0_), channel_id=1, source_target_pairs={{0,4},{1,5},{2,6},{3,7},{4,0},{5,1},{6,2},{7,3},{8,12},{9,13},{10,... | collective-permute-start | bytes 1622024 | tf_op jit(solution)/shard_map/ppermute | solution.py:224
  22.1 15.9 %collective-permute-start.3 = (bf16[64,4224]{1,0:T(8,128)(2,1)S(1)}, bf16[64,4224]{1,0:T(8,128)(2,1)S(1)}, u32[]{:S(2)}, u32[]{:S(2)}) collective-permute-start(bf16[64,4224]{1,0:T(8,128)(2,1)S(1)} %collective-permute-done.2.refs_1_), channel_id=1, source_target_pairs={{0,2},{1,3},{2,0},{3,1},{4,6},{5,7},{6,4},{7,5},{8,10},{9,11},{10,... | collective-permute-start | bytes 1622024 | tf_op jit(solution)/shard_map/ppermute | solution.py:224
  23.6 14.5 %collective-permute-start.5 = (bf16[64,4224]{1,0:T(8,128)(2,1)S(1)}, bf16[64,4224]{1,0:T(8,128)(2,1)}, u32[]{:S(2)}, u32[]{:S(2)}) collective-permute-start(bf16[64,4224]{1,0:T(8,128)(2,1)S(1)} %collective-permute-done.2.refs_1_), channel_id=1, source_target_pairs={{0,4},{1,5},{2,6},{3,7},{4,0},{5,1},{6,2},{7,3},{8,12},{9,13},{10,... | collective-permute-start | bytes 1622024 | tf_op jit(solution)/shard_map/ppermute | solution.py:224
  25.1 15.6 %collective-permute-start.10 = (bf16[64,4224]{1,0:T(8,128)(2,1)S(1)}, bf16[64,4224]{1,0:T(8,128)(2,1)S(1)}, u32[]{:S(2)}, u32[]{:S(2)}) collective-permute-start(bf16[64,4224]{1,0:T(8,128)(2,1)S(1)} %extend_rows.1.refs_0_), channel_id=1, source_target_pairs={{24,0},{25,1},{26,2},{27,3},{28,4},{29,5},{30,6},{31,7},{0,8},{1,9... | collective-permute-start | bytes 1622024 | tf_op jit(solution)/shard_map/ppermute | solution.py:228
  25.5 45.3 %copy-start.4 = (bf16[1024,32]{0,1:T(8,128)(2,1)S(1)}, bf16[1024,32]{0,1:T(8,128)(2,1)}, u32[]{:S(2)}) copy-start(bf16[1024,32]{0,1:T(8,128)(2,1)} %param.16) | copy-start | bytes 196612
  31.4 3.3 %copy-start = (bf16[4096,1024]{1,0:T(8,128)(2,1)}, bf16[4096,1024]{1,0:T(8,128)(2,1)S(1)}, u32[]{:S(2)}) copy-start(bf16[4096,1024]{1,0:T(8,128)(2,1)S(1)} %get-tuple-element.32.refs_2_.refs_6_) | copy-start | bytes 25165828
  34.7 3.2 %copy-start.2 = (bf16[4096,1024]{1,0:T(8,128)(2,1)}, bf16[4096,1024]{1,0:T(8,128)(2,1)S(1)}, u32[]{:S(2)}) copy-start(bf16[4096,1024]{1,0:T(8,128)(2,1)S(1)} %get-tuple-element.33.refs_3_.refs_7_) | copy-start | bytes 25165828
  40.6 30.2 %collective-permute-start.14 = (bf16[1,96,4224]{2,1,0:T(8,128)(2,1)S(1)}, bf16[1,96,4224]{2,1,0:T(8,128)(2,1)S(1)}, u32[]{:S(2)}, u32[]{:S(2)}) collective-permute-start(bf16[1,96,4224]{2,1,0:T(8,128)(2,1)S(1)} %get-tuple-element.35), channel_id=1, source_target_pairs={{0,1},{1,0},{2,3},{3,2},{4,5},{5,4},{6,7},{7,6},{8,9},{9,8},{10,11... | collective-permute-start | bytes 2433032 | tf_op jit(solution)/shard_map/ppermute | solution.py:224
  40.7 23.6 %collective-permute-start.11 = (bf16[64,4224]{1,0:T(8,128)(2,1)S(1)}, bf16[64,4224]{1,0:T(8,128)(2,1)S(1)}, u32[]{:S(2)}, u32[]{:S(2)}) collective-permute-start(bf16[64,4224]{1,0:T(8,128)(2,1)S(1)} %collective-permute-done.10.refs_2_), channel_id=1, source_target_pairs={{0,2},{1,3},{2,0},{3,1},{4,6},{5,7},{6,4},{7,5},{8,10},{9,11},{10,... | collective-permute-start | bytes 1622024 | tf_op jit(solution)/shard_map/ppermute | solution.py:224
  41.3 23.0 %collective-permute-start.12 = (bf16[64,4224]{1,0:T(8,128)(2,1)S(1)}, bf16[64,4224]{1,0:T(8,128)(2,1)S(1)}, u32[]{:S(2)}, u32[]{:S(2)}) collective-permute-start(bf16[64,4224]{1,0:T(8,128)(2,1)S(1)} %collective-permute-done.10.refs_2_), channel_id=1, source_target_pairs={{0,4},{1,5},{2,6},{3,7},{4,0},{5,1},{6,2},{7,3},{8,12},{9,13},{10,... | collective-permute-start | bytes 1622024 | tf_op jit(solution)/shard_map/ppermute | solution.py:224
  42.0 22.4 %collective-permute-start.7 = (bf16[2,48,2176]{2,1,0:T(8,128)(2,1)S(1)}, bf16[2,48,2176]{2,1,0:T(8,128)(2,1)S(1)}, u32[]{:S(2)}, u32[]{:S(2)}) collective-permute-start(bf16[2,48,2176]{2,1,0:T(8,128)(2,1)S(1)} %get-tuple-element.29), channel_id=1, source_target_pairs={{0,2},{1,3},{2,0},{3,1},{4,6},{5,7},{6,4},{7,5},{8,10},{9,11},{10,... | collective-permute-start | bytes 1253384 | tf_op jit(solution)/shard_map/ppermute | solution.py:224
  43.5 22.9 %collective-permute-start.6 = (bf16[2,48,2048]{2,1,0:T(8,128)(2,1)S(1)}, bf16[2,48,2048]{2,1,0:T(8,128)(2,1)S(1)}, u32[]{:S(2)}, u32[]{:S(2)}) collective-permute-start(bf16[2,48,2048]{2,1,0:T(8,128)(2,1)S(1)} %get-tuple-element.28), channel_id=1, source_target_pairs={{0,4},{1,5},{2,6},{3,7},{4,0},{5,1},{6,2},{7,3},{8,12},{9,13},{10,... | collective-permute-start | bytes 1179656 | tf_op jit(solution)/shard_map/ppermute | solution.py:224
  64.3 17.3 %collective-permute-start.9 = (bf16[2,48,2176]{2,1,0:T(8,128)(2,1)S(1)}, bf16[2,48,2176]{2,1,0:T(8,128)(2,1)S(1)}, u32[]{:S(2)}, u32[]{:S(2)}) collective-permute-start(bf16[2,48,2176]{2,1,0:T(8,128)(2,1)S(1)} %collective-permute-done.7.refs_1_), channel_id=1, source_target_pairs={{0,1},{1,0},{2,3},{3,2},{4,5},{5,4},{6,7},{7,6},{8,9},{9,8},{10,11... | collective-permute-start | bytes 1253384 | tf_op jit(solution)/shard_map/ppermute | solution.py:224
  65.8 15.8 %collective-permute-start.13 = (bf16[1,48,4224]{2,1,0:T(8,128)(2,1)S(1)}, bf16[1,48,4224]{2,1,0:T(8,128)(2,1)S(1)}, u32[]{:S(2)}, u32[]{:S(2)}) collective-permute-start(bf16[1,48,4224]{2,1,0:T(8,128)(2,1)S(1)} %get-tuple-element.31), channel_id=1, source_target_pairs={{0,1},{1,0},{2,3},{3,2},{4,5},{5,4},{6,7},{7,6},{8,9},{9,8},{10,11... | collective-permute-start | bytes 1216520 | tf_op jit(solution)/shard_map/ppermute | solution.py:224
  66.4 15.2 %collective-permute-start.8 = (bf16[2,48,2048]{2,1,0:T(8,128)(2,1)S(1)}, bf16[2,48,2048]{2,1,0:T(8,128)(2,1)S(1)}, u32[]{:S(2)}, u32[]{:S(2)}) collective-permute-start(bf16[2,48,2048]{2,1,0:T(8,128)(2,1)S(1)} %collective-permute-done.6.refs_0_), channel_id=1, source_target_pairs={{0,1},{1,0},{2,3},{3,2},{4,5},{5,4},{6,7},{7,6},{8,9},{9,8},{10,11... | collective-permute-start | bytes 1179656 | tf_op jit(solution)/shard_map/ppermute | solution.py:224
  66.5 28.3 %collective-permute-start = (bf16[64,4224]{1,0:T(8,128)(2,1)S(1)}, bf16[64,4224]{1,0:T(8,128)(2,1)S(1)}, u32[]{:S(2)}, u32[]{:S(2)}) collective-permute-start(bf16[64,4224]{1,0:T(8,128)(2,1)S(1)} %extend_rows.1.refs_0_), channel_id=1, source_target_pairs={{16,0},{17,1},{18,2},{19,3},{20,4},{21,5},{22,6},{23,7},{24,8},{25... | collective-permute-start | bytes 1622024 | tf_op jit(solution)/shard_map/ppermute | solution.py:228
  70.9 3.4 %copy-start.1 = (bf16[4096,1024]{1,0:T(8,128)(2,1)S(1)}, bf16[4096,1024]{1,0:T(8,128)(2,1)}, u32[]{:S(2)}) copy-start(bf16[4096,1024]{1,0:T(8,128)(2,1)} %copy-done) | copy-start | bytes 25165828
  74.3 3.4 %copy-start.3 = (bf16[4096,1024]{1,0:T(8,128)(2,1)S(1)}, bf16[4096,1024]{1,0:T(8,128)(2,1)}, u32[]{:S(2)}) copy-start(bf16[4096,1024]{1,0:T(8,128)(2,1)} %copy-done.2) | copy-start | bytes 25165828
  96.5 9.7 %collective-permute-start.21 = (bf16[1,96,4224]{2,1,0:T(8,128)(2,1)S(1)}, bf16[1,96,4224]{2,1,0:T(8,128)(2,1)S(1)}, u32[]{:S(2)}, u32[]{:S(2)}) collective-permute-start(bf16[1,96,4224]{2,1,0:T(8,128)(2,1)S(1)} %get-tuple-element.40), channel_id=1, source_target_pairs={{0,1},{1,0},{2,3},{3,2},{4,5},{5,4},{6,7},{7,6},{8,9},{9,8},{10,11... | collective-permute-start | bytes 2433032 | tf_op jit(solution)/shard_map/ppermute | solution.py:224
  96.6 7.5 %collective-permute-start.18 = (bf16[2,24,2176]{2,1,0:T(8,128)(2,1)S(1)}, bf16[2,24,2176]{2,1,0:T(8,128)(2,1)S(1)}, u32[]{:S(2)}, u32[]{:S(2)}) collective-permute-start(bf16[2,24,2176]{2,1,0:T(8,128)(2,1)S(1)} %get-tuple-element.38), channel_id=1, source_target_pairs={{0,2},{1,3},{2,0},{3,1},{4,6},{5,7},{6,4},{7,5},{8,10},{9,11},{10,... | collective-permute-start | bytes 626696 | tf_op jit(solution)/shard_map/ppermute | solution.py:224
  97.2 7.0 %collective-permute-start.17 = (bf16[2,24,2048]{2,1,0:T(8,128)(2,1)S(1)}, bf16[2,24,2048]{2,1,0:T(8,128)(2,1)S(1)}, u32[]{:S(2)}, u32[]{:S(2)}) collective-permute-start(bf16[2,24,2048]{2,1,0:T(8,128)(2,1)S(1)} %get-tuple-element.37), channel_id=1, source_target_pairs={{0,4},{1,5},{2,6},{3,7},{4,0},{5,1},{6,2},{7,3},{8,12},{9,13},{10,... | collective-permute-start | bytes 589832 | tf_op jit(solution)/shard_map/ppermute | solution.py:224
  104.1 2.0 %collective-permute-start.20 = (bf16[2,24,2176]{2,1,0:T(8,128)(2,1)S(1)}, bf16[2,24,2176]{2,1,0:T(8,128)(2,1)S(1)}, u32[]{:S(2)}, u32[]{:S(2)}) collective-permute-start(bf16[2,24,2176]{2,1,0:T(8,128)(2,1)S(1)} %collective-permute-done.18.refs_1_), channel_id=1, source_target_pairs={{0,1},{1,0},{2,3},{3,2},{4,5},{5,4},{6,7},{7,6},{8,9},{9,8},{10,11... | collective-permute-start | bytes 626696 | tf_op jit(solution)/shard_map/ppermute | solution.py:224
  104.2 2.0 %collective-permute-start.19 = (bf16[2,24,2048]{2,1,0:T(8,128)(2,1)S(1)}, bf16[2,24,2048]{2,1,0:T(8,128)(2,1)S(1)}, u32[]{:S(2)}, u32[]{:S(2)}) collective-permute-start(bf16[2,24,2048]{2,1,0:T(8,128)(2,1)S(1)} %collective-permute-done.17.refs_0_), channel_id=1, source_target_pairs={{0,1},{1,0},{2,3},{3,2},{4,5},{5,4},{6,7},{7,6},{8,9},{9,8},{10,11... | collective-permute-start | bytes 589832 | tf_op jit(solution)/shard_map/ppermute | solution.py:224
  104.7 14.2 %collective-permute-start.15 = (bf16[64,4224]{1,0:T(8,128)(2,1)S(1)}, bf16[64,4224]{1,0:T(8,128)(2,1)S(1)}, u32[]{:S(2)}, u32[]{:S(2)}) collective-permute-start(bf16[64,4224]{1,0:T(8,128)(2,1)S(1)} %collective-permute-done.refs_3_), channel_id=1, source_target_pairs={{0,2},{1,3},{2,0},{3,1},{4,6},{5,7},{6,4},{7,5},{8,10},{9,11},{10,... | collective-permute-start | bytes 1622024 | tf_op jit(solution)/shard_map/ppermute | solution.py:224
  105.6 14.4 %collective-permute-start.16 = (bf16[64,4224]{1,0:T(8,128)(2,1)S(1)}, bf16[64,4224]{1,0:T(8,128)(2,1)S(1)}, u32[]{:S(2)}, u32[]{:S(2)}) collective-permute-start(bf16[64,4224]{1,0:T(8,128)(2,1)S(1)} %collective-permute-done.refs_3_), channel_id=1, source_target_pairs={{0,4},{1,5},{2,6},{3,7},{4,0},{5,1},{6,2},{7,3},{8,12},{9,13},{10,... | collective-permute-start | bytes 1622024 | tf_op jit(solution)/shard_map/ppermute | solution.py:224
  121.5 6.5 %collective-permute-start.24 = (bf16[2,24,2176]{2,1,0:T(8,128)(2,1)S(1)}, bf16[2,24,2176]{2,1,0:T(8,128)(2,1)S(1)}, u32[]{:S(2)}, u32[]{:S(2)}) collective-permute-start(bf16[2,24,2176]{2,1,0:T(8,128)(2,1)S(1)} %get-tuple-element.47), channel_id=1, source_target_pairs={{0,2},{1,3},{2,0},{3,1},{4,6},{5,7},{6,4},{7,5},{8,10},{9,11},{10,... | collective-permute-start | bytes 626696 | tf_op jit(solution)/shard_map/ppermute | solution.py:224
  122.1 8.8 %collective-permute-start.22 = (bf16[1,48,4224]{2,1,0:T(8,128)(2,1)S(1)}, bf16[1,48,4224]{2,1,0:T(8,128)(2,1)S(1)}, u32[]{:S(2)}, u32[]{:S(2)}) collective-permute-start(bf16[1,48,4224]{2,1,0:T(8,128)(2,1)S(1)} %get-tuple-element.45), channel_id=1, source_target_pairs={{0,1},{1,0},{2,3},{3,2},{4,5},{5,4},{6,7},{7,6},{8,9},{9,8},{10,11... | collective-permute-start | bytes 1216520 | tf_op jit(solution)/shard_map/ppermute | solution.py:224
  122.1 7.3 %collective-permute-start.23 = (bf16[2,24,2048]{2,1,0:T(8,128)(2,1)S(1)}, bf16[2,24,2048]{2,1,0:T(8,128)(2,1)S(1)}, u32[]{:S(2)}, u32[]{:S(2)}) collective-permute-start(bf16[2,24,2048]{2,1,0:T(8,128)(2,1)S(1)} %get-tuple-element.46), channel_id=1, source_target_pairs={{0,4},{1,5},{2,6},{3,7},{4,0},{5,1},{6,2},{7,3},{8,12},{9,13},{10,... | collective-permute-start | bytes 589832 | tf_op jit(solution)/shard_map/ppermute | solution.py:224
  128.0 2.8 %collective-permute-start.26 = (bf16[2,24,2176]{2,1,0:T(8,128)(2,1)S(1)}, bf16[2,24,2176]{2,1,0:T(8,128)(2,1)S(1)}, u32[]{:S(2)}, u32[]{:S(2)}) collective-permute-start(bf16[2,24,2176]{2,1,0:T(8,128)(2,1)S(1)} %collective-permute-done.24.refs_3_), channel_id=1, source_target_pairs={{0,1},{1,0},{2,3},{3,2},{4,5},{5,4},{6,7},{7,6},{8,9},{9,8},{10,11... | collective-permute-start | bytes 626696 | tf_op jit(solution)/shard_map/ppermute | solution.py:224
  129.4 1.4 collective-permute-start.25

commit v2 on v1

--- a/solution.py
+++ b/solution.py
@@ -26,8 +26,16 @@
     return lax.dot_general(a, b, ((over[:1], over[1:]), ((), ())), preferred_element_type=jnp.float32)
 
 
-def extend_kernel(rank, top, tokens, grads, proj, routes, gates, docs, out):
+def extend_kernel(rank, top, tokens, *refs):
+    sources, out, held, sems = refs[:5], refs[5], refs[6:11], refs[11]
     width = tokens.shape[1]
+    copies = [pltpu.make_async_copy(a, b, sems.at[i]) for i, (a, b) in enumerate(zip(sources, held))]
+    copies.append(pltpu.make_async_copy(tokens, out.at[:, :width], sems.at[5]))
+    for copy in copies:
+        copy.start()
+    for copy in copies:
+        copy.wait()
+    grads, proj, routes, gates, docs = held
     small = jnp.float32
     projected = across(grads[...], proj[...], (1, 1)).astype(jnp.bfloat16)
     meta = dot(projected, place(rank, 0))
@@ -35,22 +43,26 @@
     meta += across(routes[...].astype(small).astype(jnp.bfloat16), place(top, rank + top), (0, 0))
     doc = jnp.concatenate([docs[...].astype(small)] * 8, axis=0).astype(jnp.bfloat16)
     meta += across(doc, place(8, rank + 2 * top), (0, 0))
-    out[:, :width] = tokens[...]
     out[:, width:] = meta.astype(jnp.bfloat16)
 
 
 def extend(tokens, out_grad, proj_out, routes, gate_probs, doc_ids):
     rows, width = tokens.shape
     body = functools.partial(extend_kernel, proj_out.shape[1], routes.shape[1])
+    operands = [tokens, out_grad, proj_out.T, routes.T, gate_probs.T, doc_ids.reshape(1, rows)]
     return pl.pallas_call(
         body,
         out_shape=jax.ShapeDtypeStruct((rows, width + LANES), jnp.bfloat16),
+        in_specs=[pl.BlockSpec(memory_space=pltpu.HBM)] * len(operands),
+        out_specs=pl.BlockSpec(memory_space=pltpu.VMEM),
+        scratch_shapes=[pltpu.VMEM(o.shape, o.dtype) for o in operands[1:]]
+        + [pltpu.SemaphoreType.DMA((len(operands),))],
         compiler_params=pltpu.CompilerParams(vmem_limit_bytes=16 * MIB),
         name="extend_rows",
-    )(tokens, out_grad, proj_out.T, routes.T, gate_probs.T, doc_ids.reshape(1, rows))
-
-
-def compact_kernel(capacity, top, rank, spans, parts, experts, after, *refs):
+    )(*[pltpu.with_memory_space_constraint(o, pltpu.HBM) for o in operands])
+
+
+def compact_kernel(capacity, top, rank, spans, parts, experts, *refs):
     count = len(refs) - len(parts)
     sources, outs = refs[:count], refs[count:]
     rows, total = sources[0].shape
@@ -93,7 +105,7 @@
                 ].astype(jnp.bfloat16)
 
 
-def compact(sources, experts, parts, spans, after, capacity, top, rank):
+def compact(sources, experts, parts, spans, capacity, top, rank):
     body = functools.partial(compact_kernel, capacity, top, rank, tuple(spans), tuple(parts))
     size = sum(s.size for s in sources)
     shapes = [
@@ -104,15 +116,14 @@
         body,
         out_shape=shapes,
         in_specs=[pl.BlockSpec(memory_space=pltpu.SMEM)]
-        + [pl.BlockSpec(memory_space=pltpu.VMEM)] * (1 + len(sources)),
+        + [pl.BlockSpec(memory_space=pltpu.VMEM)] * len(sources),
         out_specs=[pl.BlockSpec(memory_space=pltpu.VMEM)] * len(parts),
         compiler_params=pltpu.CompilerParams(vmem_limit_bytes=16 * MIB),
-        cost_estimate=pl.CostEstimate(flops=4 * 10**8, bytes_accessed=4 * size, transcendentals=0),
         name="compact_rows",
-    )(experts, after, *sources)
-
-
-def hold_kernel(gate_w, up_w, gate_out, up_out, done, sems):
+    )(experts, *sources)
+
+
+def hold_kernel(gate_w, up_w, gate_out, up_out, sems):
     copies = [
         pltpu.make_async_copy(gate_w.at[0], gate_out, sems.at[0]),
         pltpu.make_async_copy(up_w.at[0], up_out, sems.at[1]),
@@ -121,20 +132,17 @@
         copy.start()
     for copy in copies:
         copy.wait()
-    done[...] = jnp.zeros_like(done)
 
 
 def hold(w_gate, w_up):
     shape = w_gate.shape[1:]
     return pl.pallas_call(
         hold_kernel,
-        out_shape=[pltpu.VMEM(shape, jnp.bfloat16)] * 2
-        + [jax.ShapeDtypeStruct((8, LANES), jnp.float32)],
+        out_shape=[pltpu.VMEM(shape, jnp.bfloat16)] * 2,
         in_specs=[pl.BlockSpec(memory_space=pltpu.HBM)] * 2,
-        out_specs=[pl.BlockSpec(memory_space=pltpu.VMEM)] * 3,
+        out_specs=[pl.BlockSpec(memory_space=pltpu.VMEM)] * 2,
         scratch_shapes=[pltpu.SemaphoreType.DMA((2,))],
         compiler_params=pltpu.CompilerParams(vmem_limit_bytes=2 * MIB),
-        cost_estimate=pl.CostEstimate(flops=0, bytes_accessed=16 * MIB, transcendentals=0),
         name="hold_weights",
     )(*[pltpu.with_memory_space_constraint(w, pltpu.HBM) for w in (w_gate, w_up)])
 
@@ -202,11 +210,6 @@
             pltpu.VMEM((rows, hidden), jnp.bfloat16),
         ],
         compiler_params=pltpu.CompilerParams(vmem_limit_bytes=20 * MIB),
-        cost_estimate=pl.CostEstimate(
-            flops=4 * rows * width * hidden,
-            bytes_accessed=2 * rows * width,
-            transcendentals=rows * hidden,
-        ),
         name="sketch_rows",
     )(expert, *arrays, *weights, proj, total)
 
@@ -230,8 +233,9 @@
         )
 
     ext = extend(tokens, out_grad, proj_out, routes, gate_probs, doc_ids)
-    order = sorted(range(groups), key=lambda j: min(j, groups - j))
-    slots = [ext if j == 0 else turn(ext, j) for j in order]
+    slots = [ext]
+    for j in range(1, groups):
+        slots.append(turn(slots[-1], 1))
     bits = [1 << b for b in range(1, planes.bit_length() - 1)]
     last = sum(bits)
     masks = sorted(range(2, last, 2), key=lambda m: bin(m).count("1"))
@@ -240,49 +244,61 @@
     tiles = (width + LANES) // LANES
     cuts = [LANES * (tiles * i // len(bits)) for i in range(len(bits) + 1)]
     full = (0, width + LANES)
-    *weights, held = hold(w_gate, w_up)
+    weights = hold(w_gate, w_up)
     total = jnp.zeros((devices, rank * rank), jnp.float32)
     experts = jnp.stack([me, me ^ 1] + [me ^ hop ^ b for hop in hops for b in (0, 1)])
     own = me.reshape(1)
-    args = (held, capacity, top, rank)
+    args = (capacity, top, rank)
 
     def add(pieces):
         return sketch(pieces, own, weights, proj_hidden.T, total, top, rank)
 
-    phases = [range(groups - 2), [groups - 2], [groups - 1]]
-    waiting = []
-    for phase in phases:
-        n = len(phase)
-        if phase is phases[-1]:
-            slots[-1], total, *early = lax.optimization_barrier((slots[-1], total, *early))
-        columns = {0: [slots[i] for i in phase]}
+    def halves(arrived):
+        beside = [swap(f, 1) for f in arrived]
+        return [[(f, 0, cut) for f, cut in zip(arrived, cuts)]] + [
+            [(f, 1, cut) for f, cut in zip(beside, cuts)]
+        ]
+
+    def lanes(found):
+        return [[(found[0], 0, 0)], [(swap(found[1], 1), 0, 0)]]
+
+    def column(i):
+        slot = slots[i]
+        got = {0: slot}
         for mask in masks:
             low = mask & -mask
-            columns[mask] = [swap(s, low) for s in columns[mask ^ low]]
-        if phase is phases[-1]:
-            mine = compact(slots, experts, [(0,), (1,)], [(0, groups) + full] * 2, *args)
-            total = add(waiting + [[(mine[0], 0, 0)], [(swap(mine[1], 1), 0, 0)]])
-            columns, total = lax.optimization_barrier((columns, total))
+            got[mask] = swap(got[mask ^ low], low)
+        return [got[mask] for mask in masks]
+
+    def gather(sets):
+        n = len(sets)
         parts, spans = [(0,), (1,)], [(0, n * len(masks)) + full] * 2
         for k, i in enumerate(ends):
             parts.append((2 + 2 * k, 3 + 2 * k))
             spans.append((n * i, n * i + n, cuts[k], cuts[k + 1]))
-        sources = [s for mask in masks for s in columns[mask]]
+        sources = [s[m] for m in range(len(masks)) for s in sets]
         found = compact(sources, experts, parts, spans, *args)
-        arrived = [swap(f, hop) for f, hop in zip(found[2:], hops)]
-        beside = [swap(f, 1) for f in arrived]
-        far = [
-            [(f, 0, cuts[k]) for k, f in enumerate(arrived)],
-            [(f, 1, cuts[k]) for k, f in enumerate(beside)],
-        ]
-        near = [[(found[0], 0, 0)], [(swap(found[1], 1), 0, 0)]]
-        if phase is phases[-1]:
-            total = add(near + far)
-        else:
-            total = add(waiting + near)
-            if not waiting:
-                early = arrived
-            waiting = far
+        return found[:2], found[2:]
+
+    def send(found):
+        return [swap(f, hop) for f, hop in zip(found, hops)]
+
+    columns = [column(i) for i in range(groups - 2)]
+    near, far = gather(columns)
+    total = add(lanes(near))
+    slots[-1], far_first, total = lax.optimization_barrier((slots[-1], far, total))
+    far_first = send(far_first)
+    middle, total = lax.optimization_barrier((column(groups - 2), total))
+    near, far = gather([middle])
+    far_middle = send(far)
+    mine = compact(slots, experts, [(0,), (1,)], [(0, groups) + full] * 2, *args)
+    total = add(lanes(near) + lanes(mine))
+    final, total = lax.optimization_barrier((column(groups - 1), total))
+    near, far = gather([final])
+    far_last = send(far)
+    total = add(lanes(near) + halves(far_first))
+    far_last, total = lax.optimization_barrier((far_last, total))
+    total = add(halves(far_middle) + halves(far_last))
     owned = lax.all_to_all(total, AXES, split_axis=0, concat_axis=0, tiled=True)
     return owned[None]
 

time: 147 us -> 124 us (0.84)
  local copies, waits for them, and re-layouts: 19.3 us -> 0.92 us
  waiting for transfers between devices: 60.5 us -> 45.8 us
  starting transfers between devices: 25.1 us -> 32.7 us
  Pallas kernels: 30 us -> 31.9 us
    unnamed x22 -> x2, local copies, waits for them, and re-layouts: 18.3 us -> 0.01 us
    ppermute x3, waiting for transfers between devices: 17.7 us -> 8.75 us  [turn(): lax.ppermute(value, AXES, [(a * planes + b, c * planes + d) for (a, b), (...]
    ppermute x24, waiting for transfers between devices: 42.8 us -> 37.1 us  [swap(): return lax.ppermute(value, AXES, [(i, i ^ bits) for i in range(devices)])]
    ppermute x24, starting transfers between devices: 15.2 us -> 19.4 us  [swap(): return lax.ppermute(value, AXES, [(i, i ^ bits) for i in range(devices)])]
    ppermute x3, starting transfers between devices: 9.89 us -> 13.3 us  [turn(): lax.ppermute(value, AXES, [(a * planes + b, c * planes + d) for (a, b), (...]
  transfers between devices with their start and end apart: 27 -> 27, of which waited for: 9 -> 11; matrix products, arithmetic and copies ran while one was open for 0% -> 0% of each run, Pallas kernels for 16% -> 22%
where the time goes in v2:
time: 124 us
  waiting for transfers between devices  45.8 us (37%)
  starting transfers between devices  32.7 us (26%)
  Pallas kernels  31.9 us (26%)
  blocking collectives  12.7 us (10%)
    ppermute x24, waiting for transfers between devices, swap(): return lax.ppermute(value, AXES, [(i, i ^ bits) for i in range(devices)])  37.1 us
    ppermute x24, starting transfers between devices, swap(): return lax.ppermute(value, AXES, [(i, i ^ bits) for i in range(devices)])  19.4 us
    pallas_call x4, Pallas kernels, sketch(): pl.pallas_call(body, out_shape=jax.ShapeDtypeStruct(total.shape, jnp.floa...  17.1 us
    ppermute x3, starting transfers between devices, turn(): lax.ppermute(value, AXES, [(a * planes + b, c * planes + d) for (a, b), (...  13.3 us
    all_to_all x1, blocking collectives, on_device(): owned = lax.all_to_all(total, AXES, split_axis=0, concat_axis=0, tiled=True)  12.7 us
    ppermute x3, waiting for transfers between devices, turn(): lax.ppermute(value, AXES, [(a * planes + b, c * planes + d) for (a, b), (...  8.75 us
    pallas_call x4, Pallas kernels, compact(): pl.pallas_call(body, out_shape=shapes, in_specs=[pl.BlockSpec(memory_spac...  7.21 us
    pallas_call x1, Pallas kernels, hold(): pl.pallas_call(hold_kernel, out_shape=[pltpu.VMEM(shape, jnp.bfloat16)] *...  5.78 us
  transfers between devices with their start and end apart: 27, of which 11 were waited for; matrix products, arithmetic and copies ran while one was open for 0% of the time, Pallas kernels for 22%

profile of v2, /device:TPU:0, one launch (start us, length us, event | category | flops | bytes accessed | tf_op | source)
XLA Modules:
  0.0 124.1 jit_solution(11887267661562637846)
XLA Ops:
  0.0 1.8 %extend_rows.1.refs_0_ = bf16[64,4224]{1,0:T(8,128)(2,1)S(1)} custom-call(bf16[64,4096]{1,0:T(8,128)(2,1)} %tokens.1, bf16[64,4096]{1,0:T(8,128)(2,1)} %refs_0_.1, bf16[32,4096]{1,0:T(8,128)(2,1)} %bitcast.19, s32[8,64]{1,0:T(8,128)} %bitcast.20, bf16[8,64]{1,0:T(8,128)(2,1)} %bitcast.21, s32[1,64]{1,0:T(1,128)} %bitcast.22), custom_call_target="tpu_custom_call" | custom-call | tf_op jit(solution)/shard_map/extend_rows/pallas_call | solution.py:53
  1.8 5.1 %collective-permute-start = (bf16[64,4224]{1,0:T(8,128)(2,1)S(1)}, bf16[64,4224]{1,0:T(8,128)(2,1)S(1)}, u32[]{:S(2)}, u32[]{:S(2)}) collective-permute-start(bf16[64,4224]{1,0:T(8,128)(2,1)S(1)} %extend_rows.1.refs_0_), channel_id=1, source_target_pairs={{8,0},{9,1},{10,2},{11,3},{12,4},{13,5},{14,6},{15,7},{16,8},{17,9... | collective-permute-start | bytes 1622024 | tf_op jit(solution)/shard_map/ppermute | solution.py:231
  6.9 1.5 %collective-permute-start.5 = (bf16[64,4224]{1,0:T(8,128)(2,1)S(1)}, bf16[64,4224]{1,0:T(8,128)(2,1)S(1)}, u32[]{:S(2)}, u32[]{:S(2)}) collective-permute-start(bf16[64,4224]{1,0:T(8,128)(2,1)S(1)} %extend_rows.1.refs_0_), channel_id=1, source_target_pairs={{0,2},{1,3},{2,0},{3,1},{4,6},{5,7},{6,4},{7,5},{8,10},{9,11},{10,... | collective-permute-start | bytes 1622024 | tf_op jit(solution)/shard_map/ppermute | solution.py:227
  8.4 1.5 %collective-permute-start.7 = (bf16[64,4224]{1,0:T(8,128)(2,1)S(1)}, bf16[64,4224]{1,0:T(8,128)(2,1)S(1)}, u32[]{:S(2)}, u32[]{:S(2)}) collective-permute-start(bf16[64,4224]{1,0:T(8,128)(2,1)S(1)} %extend_rows.1.refs_0_), channel_id=1, source_target_pairs={{0,4},{1,5},{2,6},{3,7},{4,0},{5,1},{6,2},{7,3},{8,12},{9,13},{10,... | collective-permute-start | bytes 1622024 | tf_op jit(solution)/shard_map/ppermute | solution.py:227
  9.9 8.5 %collective-permute-done.refs_1_ = bf16[64,4224]{1,0:T(8,128)(2,1)S(1)} collective-permute-done((bf16[64,4224]{1,0:T(8,128)(2,1)S(1)}, bf16[64,4224]{1,0:T(8,128)(2,1)S(1)}, u32[]{:S(2)}, u32[]{:S(2)}) %collective-permute-start) | collective-permute-done | bytes 540704 | tf_op jit(solution)/shard_map/ppermute | solution.py:231
  18.4 1.5 %collective-permute-start.6 = (bf16[64,4224]{1,0:T(8,128)(2,1)S(1)}, bf16[64,4224]{1,0:T(8,128)(2,1)S(1)}, u32[]{:S(2)}, u32[]{:S(2)}) collective-permute-start(bf16[64,4224]{1,0:T(8,128)(2,1)S(1)} %collective-permute-done.refs_1_), channel_id=1, source_target_pairs={{0,2},{1,3},{2,0},{3,1},{4,6},{5,7},{6,4},{7,5},{8,10},{9,11},{10,... | collective-permute-start | bytes 1622024 | tf_op jit(solution)/shard_map/ppermute | solution.py:227
  19.9 1.5 %collective-permute-start.8 = (bf16[64,4224]{1,0:T(8,128)(2,1)S(1)}, bf16[64,4224]{1,0:T(8,128)(2,1)}, u32[]{:S(2)}, u32[]{:S(2)}) collective-permute-start(bf16[64,4224]{1,0:T(8,128)(2,1)S(1)} %collective-permute-done.refs_1_), channel_id=1, source_target_pairs={{0,4},{1,5},{2,6},{3,7},{4,0},{5,1},{6,2},{7,3},{8,12},{9,13},{10,... | collective-permute-start | bytes 1622024 | tf_op jit(solution)/shard_map/ppermute | solution.py:227
  21.5 4.3 %collective-permute-start.1 = (bf16[64,4224]{1,0:T(8,128)(2,1)S(1)}, bf16[64,4224]{1,0:T(8,128)(2,1)S(1)}, u32[]{:S(2)}, u32[]{:S(2)}) collective-permute-start(bf16[64,4224]{1,0:T(8,128)(2,1)S(1)} %collective-permute-done.refs_1_), channel_id=1, source_target_pairs={{8,0},{9,1},{10,2},{11,3},{12,4},{13,5},{14,6},{15,7},{16,8},{17,9... | collective-permute-start | bytes 1622024 | tf_op jit(solution)/shard_map/ppermute | solution.py:231
  25.8 0.1 stack.24.experts
  25.8 6.4 %collective-permute-done.6.refs_1_ = bf16[64,4224]{1,0:T(8,128)(2,1)S(1)} collective-permute-done((bf16[64,4224]{1,0:T(8,128)(2,1)S(1)}, bf16[64,4224]{1,0:T(8,128)(2,1)S(1)}, u32[]{:S(2)}, u32[]{:S(2)}) %collective-permute-start.6) | collective-permute-done | bytes 540704 | tf_op jit(solution)/shard_map/ppermute | solution.py:227
  32.2 1.3 %collective-permute-done.8.refs_3_ = bf16[64,4224]{1,0:T(8,128)(2,1)} collective-permute-done((bf16[64,4224]{1,0:T(8,128)(2,1)S(1)}, bf16[64,4224]{1,0:T(8,128)(2,1)}, u32[]{:S(2)}, u32[]{:S(2)}) %collective-permute-start.8) | collective-permute-done | bytes 540704 | tf_op jit(solution)/shard_map/ppermute | solution.py:227
  33.6 2.6 %compact_rows.4 = (bf16[1,96,4224]{2,1,0:T(8,128)(2,1)S(1)}, bf16[1,96,4224]{2,1,0:T(8,128)(2,1)S(1)}, bf16[2,48,2048]{2,1,0:T(8,128)(2,1)S(1)}, bf16[2,48,2176]{2,1,0:T(8,128)(2,1)S(1)}) custom-call(s32[6]{0:T(128)S(1)} %stack.24.experts, bf16[64,4224]{1,0:T(8,128)(2,1)S(1)} %collective-permute-done.5.refs_0_, ...), custom_call_target="tpu_custom_call" | custom-call | tf_op jit(solution)/shard_map/compact_rows/pallas_call | solution.py:115
  36.2 0.1 collective-permute-start.9
  36.3 3.9 %collective-permute-start.4 = (bf16[64,4224]{1,0:T(8,128)(2,1)S(1)}, bf16[64,4224]{1,0:T(8,128)(2,1)S(1)}, u32[]{:S(2)}, u32[]{:S(2)}) collective-permute-start(bf16[64,4224]{1,0:T(8,128)(2,1)S(1)} %collective-permute-done.1.refs_2_), channel_id=1, source_target_pairs={{8,0},{9,1},{10,2},{11,3},{12,4},{13,5},{14,6},{15,7},{16,8},{17,9... | collective-permute-start | bytes 1622024 | tf_op jit(solution)/shard_map/ppermute | solution.py:231
  40.1 0.5 collective-permute-start.2
  40.6 1.3 %collective-permute-start.3 = (bf16[64,4224]{1,0:T(8,128)(2,1)S(1)}, bf16[64,4224]{1,0:T(8,128)(2,1)S(1)}, u32[]{:S(2)}, u32[]{:S(2)}) collective-permute-start(bf16[64,4224]{1,0:T(8,128)(2,1)S(1)} %collective-permute-done.1.refs_2_), channel_id=1, source_target_pairs={{0,4},{1,5},{2,6},{3,7},{4,0},{5,1},{6,2},{7,3},{8,12},{9,13},{10,... | collective-permute-start | bytes 1622024 | tf_op jit(solution)/shard_map/ppermute | solution.py:227
  42.0 5.8 %hold_weights.1 = (bf16[4096,1024]{1,0:T(8,128)(2,1)S(1)}, bf16[4096,1024]{1,0:T(8,128)(2,1)S(1)}) custom-call(bf16[1,4096,1024]{2,1,0:T(8,128)(2,1)} %gate_w.1, bf16[1,4096,1024]{2,1,0:T(8,128)(2,1)} %up_w.1), custom_call_target="tpu_custom_call" | custom-call | tf_op jit(solution)/shard_map/hold_weights/pallas_call | solution.py:139
  47.8 4.0 %sketch_rows.4.refs_7_ = f32[32,1024]{1,0:T(8,128)S(1)} custom-call(s32[1]{0:T(128)} %bitcast.expert, bf16[1,96,4224]{2,1,0:T(8,128)(2,1)S(1)} %get-tuple-element.36.refs_0_, bf16[1,96,4224]{2,1,0:T(8,128)(2,1)S(1)} %collective-permute-done.9.refs_1_, bf16[4096,1024]{1,0:T(8,128)(2,1)S(1)} %get-tuple-element.38.refs_2_.refs_4_.refs_6_.refs_8_, ...), custom_call_target="tpu_custom_call" | custom-call | tf_op jit(solution)/shard_map/sketch_rows/pallas_call | solution.py:203
  51.8 0.2 collective-permute-done.4.refs_3_
  52.1 1.5 %collective-permute-start.21 = (bf16[2,48,2048]{2,1,0:T(8,128)(2,1)S(1)}, bf16[2,48,2048]{2,1,0:T(8,128)(2,1)S(1)}, u32[]{:S(2)}, u32[]{:S(2)}) collective-permute-start(bf16[2,48,2048]{2,1,0:T(8,128)(2,1)S(1)} %get-tuple-element.57), channel_id=1, source_target_pairs={{0,4},{1,5},{2,6},{3,7},{4,0},{5,1},{6,2},{7,3},{8,12},{9,13},{10,... | collective-permute-start | bytes 1179656 | tf_op jit(solution)/shard_map/ppermute | solution.py:227
  53.6 1.7 %compact_rows.6 = (bf16[1,96,4224]{2,1,0:T(8,128)(2,1)S(1)}, bf16[1,96,4224]{2,1,0:T(8,128)(2,1)S(1)}) custom-call(s32[6]{0:T(128)S(1)} %stack.24.experts, bf16[64,4224]{1,0:T(8,128)(2,1)S(1)} %extend_rows.1.refs_0_, bf16[64,4224]{1,0:T(8,128)(2,1)S(1)} %collective-permute-done.refs_1_, bf16[64,4224]{1,0:T(8,128)(2,1)S(1)} %collective-permute-done.1.refs_2_, ...), custom_call_target="tpu_custom_call" | custom-call | tf_op jit(solution)/shard_map/compact_rows/pallas_call | solution.py:115
  55.3 0.1 collective-permute-start.17
  55.4 1.4 %compact_rows.5 = (bf16[1,48,4224]{2,1,0:T(8,128)(2,1)S(1)}, bf16[1,48,4224]{2,1,0:T(8,128)(2,1)S(1)}, bf16[2,24,2048]{2,1,0:T(8,128)(2,1)S(1)}, bf16[2,24,2176]{2,1,0:T(8,128)(2,1)S(1)}) custom-call(s32[6]{0:T(128)S(1)} %stack.24.experts, bf16[64,4224]{1,0:T(8,128)(2,1)S(1)} %collective-permute-done.2.refs_0_, ...), custom_call_target="tpu_custom_call" | custom-call | tf_op jit(solution)/shard_map/compact_rows/pallas_call | solution.py:115
  56.9 0.5 collective-permute-start.16
  57.4 0.6 collective-permute-start.14
  58.0 2.2 %collective-permute-start.15 = (bf16[64,4224]{1,0:T(8,128)(2,1)S(1)}, bf16[64,4224]{1,0:T(8,128)(2,1)S(1)}, u32[]{:S(2)}, u32[]{:S(2)}) collective-permute-start(bf16[64,4224]{1,0:T(8,128)(2,1)S(1)} %collective-permute-done.4.refs_3_), channel_id=1, source_target_pairs={{0,4},{1,5},{2,6},{3,7},{4,0},{5,1},{6,2},{7,3},{8,12},{9,13},{10,... | collective-permute-start | bytes 1622024 | tf_op jit(solution)/shard_map/ppermute | solution.py:227
  60.3 3.9 %collective-permute-done.21.refs_2_ = bf16[2,48,2048]{2,1,0:T(8,128)(2,1)S(1)} collective-permute-done((bf16[2,48,2048]{2,1,0:T(8,128)(2,1)S(1)}, bf16[2,48,2048]{2,1,0:T(8,128)(2,1)S(1)}, u32[]{:S(2)}, u32[]{:S(2)}) %collective-permute-start.21) | collective-permute-done | bytes 393248 | tf_op jit(solution)/shard_map/ppermute | solution.py:227
  64.1 1.4 %collective-permute-start.22 = (bf16[2,48,2176]{2,1,0:T(8,128)(2,1)S(1)}, bf16[2,48,2176]{2,1,0:T(8,128)(2,1)S(1)}, u32[]{:S(2)}, u32[]{:S(2)}) collective-permute-start(bf16[2,48,2176]{2,1,0:T(8,128)(2,1)S(1)} %get-tuple-element.58), channel_id=1, source_target_pairs={{0,2},{1,3},{2,0},{3,1},{4,6},{5,7},{6,4},{7,5},{8,10},{9,11},{10,... | collective-permute-start | bytes 1253384 | tf_op jit(solution)/shard_map/ppermute | solution.py:227
  65.5 15.2 %collective-permute-done.22.refs_3_ = bf16[2,48,2176]{2,1,0:T(8,128)(2,1)S(1)} collective-permute-done((bf16[2,48,2176]{2,1,0:T(8,128)(2,1)S(1)}, bf16[2,48,2176]{2,1,0:T(8,128)(2,1)S(1)}, u32[]{:S(2)}, u32[]{:S(2)}) %collective-permute-start.22) | collective-permute-done | bytes 417824 | tf_op jit(solution)/shard_map/ppermute | solution.py:227
  80.7 5.8 %sketch_rows.5.refs_9_ = f32[32,1024]{1,0:T(8,128)S(1)} custom-call(s32[1]{0:T(128)} %bitcast.expert, bf16[1,48,4224]{2,1,0:T(8,128)(2,1)S(1)} %get-tuple-element.46.refs_0_, bf16[1,48,4224]{2,1,0:T(8,128)(2,1)S(1)} %collective-permute-done.16.refs_1_, bf16[1,96,4224]{2,1,0:T(8,128)(2,1)S(1)} %get-tuple-element.48.refs_2_, ...), custom_call_target="tpu_custom_call" | custom-call | tf_op jit(solution)/shard_map/sketch_rows/pallas_call | solution.py:203
  86.5 0.0 collective-permute-done.14.refs_0_
  86.5 1.4 %compact_rows.7 = (bf16[1,48,4224]{2,1,0:T(8,128)(2,1)S(1)}, bf16[1,48,4224]{2,1,0:T(8,128)(2,1)S(1)}, bf16[2,24,2048]{2,1,0:T(8,128)(2,1)S(1)}, bf16[2,24,2176]{2,1,0:T(8,128)(2,1)S(1)}) custom-call(s32[6]{0:T(128)S(1)} %stack.24.experts, bf16[64,4224]{1,0:T(8,128)(2,1)S(1)} %collective-permute-done.14.refs_0_, ...), custom_call_target="tpu_custom_call" | custom-call | tf_op jit(solution)/shard_map/compact_rows/pallas_call | solution.py:115
  88.0 0.6 collective-permute-start.20
  88.6 0.8 collective-permute-start.11
  89.4 1.2 collective-permute-start.19
  90.6 6.0 %collective-permute-done.11.refs_1_ = bf16[2,24,2176]{2,1,0:T(8,128)(2,1)S(1)} collective-permute-done((bf16[2,24,2176]{2,1,0:T(8,128)(2,1)S(1)}, bf16[2,24,2176]{2,1,0:T(8,128)(2,1)S(1)}, u32[]{:S(2)}, u32[]{:S(2)}) %collective-permute-start.11) | collective-permute-done | bytes 208928 | tf_op jit(solution)/shard_map/ppermute | solution.py:227
  96.6 1.4 %collective-permute-start.18 = (bf16[2,24,2048]{2,1,0:T(8,128)(2,1)S(1)}, bf16[2,24,2048]{2,1,0:T(8,128)(2,1)S(1)}, u32[]{:S(2)}, u32[]{:S(2)}) collective-permute-start(bf16[2,24,2048]{2,1,0:T(8,128)(2,1)S(1)} %get-tuple-element.53), channel_id=1, source_target_pairs={{0,4},{1,5},{2,6},{3,7},{4,0},{5,1},{6,2},{7,3},{8,12},{9,13},{10,... | collective-permute-start | bytes 589832 | tf_op jit(solution)/shard_map/ppermute | solution.py:227
  98.0 0.6 collective-permute-start.10
  98.6 4.3 %sketch_rows.6.refs_11_ = f32[32,1024]{1,0:T(8,128)S(1)} custom-call(s32[1]{0:T(128)} %bitcast.expert, bf16[1,48,4224]{2,1,0:T(8,128)(2,1)S(1)} %get-tuple-element.55.refs_0_, bf16[1,48,4224]{2,1,0:T(8,128)(2,1)S(1)} %collective-permute-done.20.refs_1_, bf16[2,48,2048]{2,1,0:T(8,128)(2,1)S(1)} %collective-permute-done.21.refs_2_, ...), custom_call_target="tpu_custom_call" | custom-call | tf_op jit(solution)/shard_map/sketch_rows/pallas_call | solution.py:203
  102.9 1.0 collective-permute-done.18.refs_4_
  103.9 2.1 %collective-permute-done.10.refs_0_ = bf16[2,24,2048]{2,1,0:T(8,128)(2,1)S(1)} collective-permute-done((bf16[2,24,2048]{2,1,0:T(8,128)(2,1)S(1)}, bf16[2,24,2048]{2,1,0:T(8,128)(2,1)S(1)}, u32[]{:S(2)}, u32[]{:S(2)}) %collective-permute-start.10) | collective-permute-done | bytes 196640 | tf_op jit(solution)/shard_map/ppermute | solution.py:227
  106.0 0.5 collective-permute-start.25
  106.5 0.9 collective-permute-done.12.refs_2_
  107.4 0.3 collective-permute-done.25.refs_6_
  107.7 2.9 %sketch_rows.7 = f32[32,1024]{1,0:T(8,128)S(1)} custom-call(s32[1]{0:T(128)} %bitcast.expert, bf16[2,24,2048]{2,1,0:T(8,128)(2,1)S(1)} %collective-permute-done.10.refs_0_, bf16[2,24,2176]{2,1,0:T(8,128)(2,1)S(1)} %collective-permute-done.11.refs_1_, bf16[2,24,2048]{2,1,0:T(8,128)(2,1)S(1)} %collective-permute-done.12.refs_2_, ...), custom_call_target="tpu_custom_call" | custom-call | tf_op jit(solution)/shard_map/sketch_rows/pallas_call | solution.py:203
  110.6 0.1 copy.10
  110.8 12.7 %all_to_all.9 = f32[32,1,1024]{2,1,0:T(1,128)S(1)} all-to-all(f32[32,1,1024]{2,1,0:T(1,128)S(1)} %copy.10), channel_id=1, replica_groups=mesh['expert'=4,'dp'=8] {'expert','dp'}, dimensions={0} | all-to-all | bytes 262144 | tf_op jit(solution)/shard_map/all_to_all | solution.py:302
  123.5 0.7 copy.11
  (23 shorter events, 0.1 us)
Async XLA Ops:
  1.8 16.6 %collective-permute-start = (bf16[64,4224]{1,0:T(8,128)(2,1)S(1)}, bf16[64,4224]{1,0:T(8,128)(2,1)S(1)}, u32[]{:S(2)}, u32[]{:S(2)}) collective-permute-start(bf16[64,4224]{1,0:T(8,128)(2,1)S(1)} %extend_rows.1.refs_0_), channel_id=1, source_target_pairs={{8,0},{9,1},{10,2},{11,3},{12,4},{13,5},{14,6},{15,7},{16,8},{17,9... | collective-permute-start | bytes 1622024 | tf_op jit(solution)/shard_map/ppermute | solution.py:231
  6.9 18.9 %collective-permute-start.5 = (bf16[64,4224]{1,0:T(8,128)(2,1)S(1)}, bf16[64,4224]{1,0:T(8,128)(2,1)S(1)}, u32[]{:S(2)}, u32[]{:S(2)}) collective-permute-start(bf16[64,4224]{1,0:T(8,128)(2,1)S(1)} %extend_rows.1.refs_0_), channel_id=1, source_target_pairs={{0,2},{1,3},{2,0},{3,1},{4,6},{5,7},{6,4},{7,5},{8,10},{9,11},{10,... | collective-permute-start | bytes 1622024 | tf_op jit(solution)/shard_map/ppermute | solution.py:227
  8.4 17.4 %collective-permute-start.7 = (bf16[64,4224]{1,0:T(8,128)(2,1)S(1)}, bf16[64,4224]{1,0:T(8,128)(2,1)S(1)}, u32[]{:S(2)}, u32[]{:S(2)}) collective-permute-start(bf16[64,4224]{1,0:T(8,128)(2,1)S(1)} %extend_rows.1.refs_0_), channel_id=1, source_target_pairs={{0,4},{1,5},{2,6},{3,7},{4,0},{5,1},{6,2},{7,3},{8,12},{9,13},{10,... | collective-permute-start | bytes 1622024 | tf_op jit(solution)/shard_map/ppermute | solution.py:227
  18.4 13.8 %collective-permute-start.6 = (bf16[64,4224]{1,0:T(8,128)(2,1)S(1)}, bf16[64,4224]{1,0:T(8,128)(2,1)S(1)}, u32[]{:S(2)}, u32[]{:S(2)}) collective-permute-start(bf16[64,4224]{1,0:T(8,128)(2,1)S(1)} %collective-permute-done.refs_1_), channel_id=1, source_target_pairs={{0,2},{1,3},{2,0},{3,1},{4,6},{5,7},{6,4},{7,5},{8,10},{9,11},{10,... | collective-permute-start | bytes 1622024 | tf_op jit(solution)/shard_map/ppermute | solution.py:227
  19.9 13.6 %collective-permute-start.8 = (bf16[64,4224]{1,0:T(8,128)(2,1)S(1)}, bf16[64,4224]{1,0:T(8,128)(2,1)}, u32[]{:S(2)}, u32[]{:S(2)}) collective-permute-start(bf16[64,4224]{1,0:T(8,128)(2,1)S(1)} %collective-permute-done.refs_1_), channel_id=1, source_target_pairs={{0,4},{1,5},{2,6},{3,7},{4,0},{5,1},{6,2},{7,3},{8,12},{9,13},{10,... | collective-permute-start | bytes 1622024 | tf_op jit(solution)/shard_map/ppermute | solution.py:227
  21.5 14.8 %collective-permute-start.1 = (bf16[64,4224]{1,0:T(8,128)(2,1)S(1)}, bf16[64,4224]{1,0:T(8,128)(2,1)S(1)}, u32[]{:S(2)}, u32[]{:S(2)}) collective-permute-start(bf16[64,4224]{1,0:T(8,128)(2,1)S(1)} %collective-permute-done.refs_1_), channel_id=1, source_target_pairs={{8,0},{9,1},{10,2},{11,3},{12,4},{13,5},{14,6},{15,7},{16,8},{17,9... | collective-permute-start | bytes 1622024 | tf_op jit(solution)/shard_map/ppermute | solution.py:231
  36.2 11.6 %copy-start = (bf16[1024,32]{0,1:T(8,128)(2,1)S(1)}, bf16[1024,32]{0,1:T(8,128)(2,1)}, u32[]{:S(2)}) copy-start(bf16[1024,32]{0,1:T(8,128)(2,1)} %param.16) | copy-start | bytes 196612
  36.2 11.6 %collective-permute-start.9 = (bf16[1,96,4224]{2,1,0:T(8,128)(2,1)S(1)}, bf16[1,96,4224]{2,1,0:T(8,128)(2,1)S(1)}, u32[]{:S(2)}, u32[]{:S(2)}) collective-permute-start(bf16[1,96,4224]{2,1,0:T(8,128)(2,1)S(1)} %get-tuple-element.37), channel_id=1, source_target_pairs={{0,1},{1,0},{2,3},{3,2},{4,5},{5,4},{6,7},{7,6},{8,9},{9,8},{10,11... | collective-permute-start | bytes 2433032 | tf_op jit(solution)/shard_map/ppermute | solution.py:227
  36.3 15.8 %collective-permute-start.4 = (bf16[64,4224]{1,0:T(8,128)(2,1)S(1)}, bf16[64,4224]{1,0:T(8,128)(2,1)S(1)}, u32[]{:S(2)}, u32[]{:S(2)}) collective-permute-start(bf16[64,4224]{1,0:T(8,128)(2,1)S(1)} %collective-permute-done.1.refs_2_), channel_id=1, source_target_pairs={{8,0},{9,1},{10,2},{11,3},{12,4},{13,5},{14,6},{15,7},{16,8},{17,9... | collective-permute-start | bytes 1622024 | tf_op jit(solution)/shard_map/ppermute | solution.py:231
  40.1 15.3 %collective-permute-start.2 = (bf16[64,4224]{1,0:T(8,128)(2,1)S(1)}, bf16[64,4224]{1,0:T(8,128)(2,1)S(1)}, u32[]{:S(2)}, u32[]{:S(2)}) collective-permute-start(bf16[64,4224]{1,0:T(8,128)(2,1)S(1)} %collective-permute-done.1.refs_2_), channel_id=1, source_target_pairs={{0,2},{1,3},{2,0},{3,1},{4,6},{5,7},{6,4},{7,5},{8,10},{9,11},{10,... | collective-permute-start | bytes 1622024 | tf_op jit(solution)/shard_map/ppermute | solution.py:227
  40.6 14.8 %collective-permute-start.3 = (bf16[64,4224]{1,0:T(8,128)(2,1)S(1)}, bf16[64,4224]{1,0:T(8,128)(2,1)S(1)}, u32[]{:S(2)}, u32[]{:S(2)}) collective-permute-start(bf16[64,4224]{1,0:T(8,128)(2,1)S(1)} %collective-permute-done.1.refs_2_), channel_id=1, source_target_pairs={{0,4},{1,5},{2,6},{3,7},{4,0},{5,1},{6,2},{7,3},{8,12},{9,13},{10,... | collective-permute-start | bytes 1622024 | tf_op jit(solution)/shard_map/ppermute | solution.py:227
  52.1 12.1 %collective-permute-start.21 = (bf16[2,48,2048]{2,1,0:T(8,128)(2,1)S(1)}, bf16[2,48,2048]{2,1,0:T(8,128)(2,1)S(1)}, u32[]{:S(2)}, u32[]{:S(2)}) collective-permute-start(bf16[2,48,2048]{2,1,0:T(8,128)(2,1)S(1)} %get-tuple-element.57), channel_id=1, source_target_pairs={{0,4},{1,5},{2,6},{3,7},{4,0},{5,1},{6,2},{7,3},{8,12},{9,13},{10,... | collective-permute-start | bytes 1179656 | tf_op jit(solution)/shard_map/ppermute | solution.py:227
  55.3 25.3 %collective-permute-start.17 = (bf16[1,96,4224]{2,1,0:T(8,128)(2,1)S(1)}, bf16[1,96,4224]{2,1,0:T(8,128)(2,1)S(1)}, u32[]{:S(2)}, u32[]{:S(2)}) collective-permute-start(bf16[1,96,4224]{2,1,0:T(8,128)(2,1)S(1)} %get-tuple-element.49), channel_id=1, source_target_pairs={{0,1},{1,0},{2,3},{3,2},{4,5},{5,4},{6,7},{7,6},{8,9},{9,8},{10,11... | collective-permute-start | bytes 2433032 | tf_op jit(solution)/shard_map/ppermute | solution.py:227
  56.9 8.6 %collective-permute-start.16 = (bf16[1,48,4224]{2,1,0:T(8,128)(2,1)S(1)}, bf16[1,48,4224]{2,1,0:T(8,128)(2,1)S(1)}, u32[]{:S(2)}, u32[]{:S(2)}) collective-permute-start(bf16[1,48,4224]{2,1,0:T(8,128)(2,1)S(1)} %get-tuple-element.47), channel_id=1, source_target_pairs={{0,1},{1,0},{2,3},{3,2},{4,5},{5,4},{6,7},{7,6},{8,9},{9,8},{10,11... | collective-permute-start | bytes 1216520 | tf_op jit(solution)/shard_map/ppermute | solution.py:227
  57.4 29.1 %collective-permute-start.14 = (bf16[64,4224]{1,0:T(8,128)(2,1)S(1)}, bf16[64,4224]{1,0:T(8,128)(2,1)S(1)}, u32[]{:S(2)}, u32[]{:S(2)}) collective-permute-start(bf16[64,4224]{1,0:T(8,128)(2,1)S(1)} %collective-permute-done.4.refs_3_), channel_id=1, source_target_pairs={{0,2},{1,3},{2,0},{3,1},{4,6},{5,7},{6,4},{7,5},{8,10},{9,11},{10,... | collective-permute-start | bytes 1622024 | tf_op jit(solution)/shard_map/ppermute | solution.py:227
  58.0 28.5 %collective-permute-start.15 = (bf16[64,4224]{1,0:T(8,128)(2,1)S(1)}, bf16[64,4224]{1,0:T(8,128)(2,1)S(1)}, u32[]{:S(2)}, u32[]{:S(2)}) collective-permute-start(bf16[64,4224]{1,0:T(8,128)(2,1)S(1)} %collective-permute-done.4.refs_3_), channel_id=1, source_target_pairs={{0,4},{1,5},{2,6},{3,7},{4,0},{5,1},{6,2},{7,3},{8,12},{9,13},{10,... | collective-permute-start | bytes 1622024 | tf_op jit(solution)/shard_map/ppermute | solution.py:227
  64.1 16.5 %collective-permute-start.22 = (bf16[2,48,2176]{2,1,0:T(8,128)(2,1)S(1)}, bf16[2,48,2176]{2,1,0:T(8,128)(2,1)S(1)}, u32[]{:S(2)}, u32[]{:S(2)}) collective-permute-start(bf16[2,48,2176]{2,1,0:T(8,128)(2,1)S(1)} %get-tuple-element.58), channel_id=1, source_target_pairs={{0,2},{1,3},{2,0},{3,1},{4,6},{5,7},{6,4},{7,5},{8,10},{9,11},{10,... | collective-permute-start | bytes 1253384 | tf_op jit(solution)/shard_map/ppermute | solution.py:227
  65.5 32.5 %collective-permute-start.23 = (bf16[2,48,2048]{2,1,0:T(8,128)(2,1)S(1)}, bf16[2,48,2048]{2,1,0:T(8,128)(2,1)S(1)}, u32[]{:S(2)}, u32[]{:S(2)}) collective-permute-start(bf16[2,48,2048]{2,1,0:T(8,128)(2,1)S(1)} %collective-permute-done.21.refs_2_), channel_id=1, source_target_pairs={{0,1},{1,0},{2,3},{3,2},{4,5},{5,4},{6,7},{7,6},{8,9},{9,8},{10,11... | collective-permute-start | bytes 1179656 | tf_op jit(solution)/shard_map/ppermute | solution.py:227
  80.7 17.9 %collective-permute-start.24 = (bf16[2,48,2176]{2,1,0:T(8,128)(2,1)S(1)}, bf16[2,48,2176]{2,1,0:T(8,128)(2,1)S(1)}, u32[]{:S(2)}, u32[]{:S(2)}) collective-permute-start(bf16[2,48,2176]{2,1,0:T(8,128)(2,1)S(1)} %collective-permute-done.22.refs_3_), channel_id=1, source_target_pairs={{0,1},{1,0},{2,3},{3,2},{4,5},{5,4},{6,7},{7,6},{8,9},{9,8},{10,11... | collective-permute-start | bytes 1253384 | tf_op jit(solution)/shard_map/ppermute | solution.py:227
  88.0 10.6 %collective-permute-start.20 = (bf16[1,48,4224]{2,1,0:T(8,128)(2,1)S(1)}, bf16[1,48,4224]{2,1,0:T(8,128)(2,1)S(1)}, u32[]{:S(2)}, u32[]{:S(2)}) collective-permute-start(bf16[1,48,4224]{2,1,0:T(8,128)(2,1)S(1)} %get-tuple-element.56), channel_id=1, source_target_pairs={{0,1},{1,0},{2,3},{3,2},{4,5},{5,4},{6,7},{7,6},{8,9},{9,8},{10,11... | collective-permute-start | bytes 1216520 | tf_op jit(solution)/shard_map/ppermute | solution.py:227
  88.6 8.0 %collective-permute-start.11 = (bf16[2,24,2176]{2,1,0:T(8,128)(2,1)S(1)}, bf16[2,24,2176]{2,1,0:T(8,128)(2,1)S(1)}, u32[]{:S(2)}, u32[]{:S(2)}) collective-permute-start(bf16[2,24,2176]{2,1,0:T(8,128)(2,1)S(1)} %get-tuple-element.44), channel_id=1, source_target_pairs={{0,2},{1,3},{2,0},{3,1},{4,6},{5,7},{6,4},{7,5},{8,10},{9,11},{10,... | collective-permute-start | bytes 626696 | tf_op jit(solution)/shard_map/ppermute | solution.py:227
  89.4 14.5 %collective-permute-start.19 = (bf16[2,24,2176]{2,1,0:T(8,128)(2,1)S(1)}, bf16[2,24,2176]{2,1,0:T(8,128)(2,1)S(1)}, u32[]{:S(2)}, u32[]{:S(2)}) collective-permute-start(bf16[2,24,2176]{2,1,0:T(8,128)(2,1)S(1)} %get-tuple-element.54), channel_id=1, source_target_pairs={{0,2},{1,3},{2,0},{3,1},{4,6},{5,7},{6,4},{7,5},{8,10},{9,11},{10,... | collective-permute-start | bytes 626696 | tf_op jit(solution)/shard_map/ppermute | solution.py:227
  96.6 7.3 %collective-permute-start.18 = (bf16[2,24,2048]{2,1,0:T(8,128)(2,1)S(1)}, bf16[2,24,2048]{2,1,0:T(8,128)(2,1)S(1)}, u32[]{:S(2)}, u32[]{:S(2)}) collective-permute-start(bf16[2,24,2048]{2,1,0:T(8,128)(2,1)S(1)} %get-tuple-element.53), channel_id=1, source_target_pairs={{0,4},{1,5},{2,6},{3,7},{4,0},{5,1},{6,2},{7,3},{8,12},{9,13},{10,... | collective-permute-start | bytes 589832 | tf_op jit(solution)/shard_map/ppermute | solution.py:227
  98.0 8.0 %collective-permute-start.10 = (bf16[2,24,2048]{2,1,0:T(8,128)(2,1)S(1)}, bf16[2,24,2048]{2,1,0:T(8,128)(2,1)S(1)}, u32[]{:S(2)}, u32[]{:S(2)}) collective-permute-start(bf16[2,24,2048]{2,1,0:T(8,128)(2,1)S(1)} %get-tuple-element.43), channel_id=1, source_target_pairs={{0,4},{1,5},{2,6},{3,7},{4,0},{5,1},{6,2},{7,3},{8,12},{9,13},{10,... | collective-permute-start | bytes 589832 | tf_op jit(solution)/shard_map/ppermute | solution.py:227
  98.6 8.8 %collective-permute-start.13 = (bf16[2,24,2176]{2,1,0:T(8,128)(2,1)S(1)}, bf16[2,24,2176]{2,1,0:T(8,128)(2,1)S(1)}, u32[]{:S(2)}, u32[]{:S(2)}) collective-permute-start(bf16[2,24,2176]{2,1,0:T(8,128)(2,1)S(1)} %collective-permute-done.11.refs_1_), channel_id=1, source_target_pairs={{0,1},{1,0},{2,3},{3,2},{4,5},{5,4},{6,7},{7,6},{8,9},{9,8},{10,11... | collective-permute-start | bytes 626696 | tf_op jit(solution)/shard_map/ppermute | solution.py:227
  103.9 3.8 %collective-permute-start.26 = (bf16[2,24,2176]{2,1,0:T(8,128)(2,1)S(1)}, bf16[2,24,2176]{2,1,0:T(8,128)(2,1)S(1)}, u32[]{:S(2)}, u32[]{:S(2)}) collective-permute-start(bf16[2,24,2176]{2,1,0:T(8,128)(2,1)S(1)} %collective-permute-done.19.refs_5_), channel_id=1, source_target_pairs={{0,1},{1,0},{2,3},{3,2},{4,5},{5,4},{6,7},{7,6},{8,9},{9,8},{10,11... | collective-permute-start | bytes 626696 | tf_op jit(solution)/shard_map/ppermute | solution.py:227
  106.0 1.4 %collective-permute-start.12 = (bf16[2,24,2048]{2,1,0:T(8,128)(2,1)S(1)}, bf16[2,24,2048]{2,1,0:T(8,128)(2,1)S(1)}, u32[]{:S(2)}, u32[]{:S(2)}) collective-permute-start(bf16[2,24,2048]{2,1,0:T(8,128)(2,1)S(1)} %collective-permute-done.10.refs_0_), channel_id=1, source_target_pairs={{0,1},{1,0},{2,3},{3,2},{4,5},{5,4},{6,7},{7,6},{8,9},{9,8},{10,11... | collective-permute-start | bytes 589832 | tf_op jit(solution)/shard_map/ppermute | solution.py:227
  106.0 1.7 %collective-permute-start.25 = (bf16[2,24,2048]{2,1,0:T(8,128)(2,1)S(1)}, bf16[2,24,2048]{2,1,0:T(8,128)(2,1)S(1)}, u32[]{:S(2)}, u32[]{:S(2)}) collective-permute-start(bf16[2,24,2048]{2,1,0:T(8,128)(2,1)S(1)} %collective-permute-done.18.refs_4_), channel_id=1, source_target_pairs={{0,1},{1,0},{2,3},{3,2},{4,5},{5,4},{6,7},{7,6},{8,9},{9,8},{10,11... | collective-permute-start | bytes 589832 | tf_op jit(solution)/shard_map/ppermute | solution.py:227

commit v3 on v2

--- a/solution.py
+++ b/solution.py
@@ -62,65 +62,64 @@
     )(*[pltpu.with_memory_space_constraint(o, pltpu.HBM) for o in operands])
 
 
-def compact_kernel(capacity, top, rank, spans, parts, experts, *refs):
-    count = len(refs) - len(parts)
-    sources, outs = refs[:count], refs[count:]
+def compact_kernel(capacity, top, rank, members, targets, *refs):
+    parts = 2 if members is None else 3
+    sources, outs = refs[:-parts], refs[-parts:]
+    count = len(sources)
     rows, total = sources[0].shape
     width = total - LANES
     meta = jnp.concatenate([s[:, width:] for s in sources], axis=0).astype(jnp.float32)
     lanes = lax.broadcasted_iota(jnp.int32, meta.shape, 1)
+    source = lax.broadcasted_iota(jnp.int32, meta.shape, 0) // rows
     is_route = (lanes >= rank + top) & (lanes < rank + 2 * top)
-    named_by = sorted({q for members in parts for q in members})
     hits = jnp.zeros(meta.shape, jnp.float32)
-    for q in named_by:
-        named = is_route & (meta == experts[q].astype(jnp.float32))
+    for q in range(2 * parts - 2):
+        named = is_route & (meta == targets[q].astype(jnp.float32))
         hit = jnp.sum(named.astype(jnp.float32), axis=1, keepdims=True)
         hits = jnp.where(lanes == q, hit, hits)
+    first = source
+    if members is not None:
+        hits = jnp.where((lanes < 2) | (source // members == targets[4]), hits, 0.0)
+        first = jnp.where(lanes < 2, source, source % members)
     every = count * rows
     here = lax.broadcasted_iota(jnp.int32, (every, every), 0)
     other = lax.broadcasted_iota(jnp.int32, (every, every), 1)
     earlier = ((other < here) & (other // rows == here // rows)).astype(jnp.bfloat16)
     before = dot(earlier, hits.astype(jnp.bfloat16))
-    first = (lax.broadcasted_iota(jnp.int32, meta.shape, 0) // rows * capacity).astype(jnp.float32)
-    slots = jnp.where(hits > 0, before + first, -1.0).T
+    slots = jnp.where(hits > 0, before + (first * capacity).astype(jnp.float32), -1.0).T
+    picks, spots = [], []
+    for q in range(2 * parts - 2):
+        picked = outs[min(q, 2)].shape[1]
+        spot = lax.broadcasted_iota(jnp.int32, (picked, every), 0).astype(jnp.float32)
+        picks.append((spot == slots[q : q + 1, :]).astype(jnp.bfloat16))
+        spots.append((outs[min(q, 2)], max(q - 2, 0), picked))
+    pick = jnp.concatenate(picks, axis=0)
     step = 4 * LANES
-    for out, members, (low, high, start, stop) in zip(outs, parts, spans):
-        picked = (high - low) * capacity
-        spot = lax.broadcasted_iota(jnp.int32, (picked, (high - low) * rows), 0) + low * capacity
-        spot = spot.astype(jnp.float32)
-        pick = jnp.concatenate(
-            [
-                (spot == slots[q : q + 1, low * rows : high * rows]).astype(jnp.bfloat16)
-                for q in members
-            ],
-            axis=0,
-        )
-        for at in range(start, stop, step):
-            end = min(at + step, stop)
-            block = jnp.concatenate([s[:, at:end] for s in sources[low:high]], axis=0)
-            found = dot(pick, block)
-            for i in range(len(members)):
-                out[i, :, at - start : end - start] = found[
-                    i * picked : (i + 1) * picked
-                ].astype(jnp.bfloat16)
-
-
-def compact(sources, experts, parts, spans, capacity, top, rank):
-    body = functools.partial(compact_kernel, capacity, top, rank, tuple(spans), tuple(parts))
-    size = sum(s.size for s in sources)
+    for at in range(0, total, step):
+        end = min(at + step, total)
+        found = dot(pick, jnp.concatenate([s[:, at:end] for s in sources], axis=0))
+        row = 0
+        for out, lead, picked in spots:
+            out[lead, :, at:end] = found[row : row + picked].astype(jnp.bfloat16)
+            row += picked
+
+
+def compact(sources, members, targets, capacity, top, rank):
+    body = functools.partial(compact_kernel, capacity, top, rank, members)
+    counts = [(1, len(sources))] * 2 + ([] if members is None else [(2, members)])
     shapes = [
-        jax.ShapeDtypeStruct((len(p), (high - low) * capacity, stop - start), jnp.bfloat16)
-        for p, (low, high, start, stop) in zip(parts, spans)
+        jax.ShapeDtypeStruct((lead, n * capacity, sources[0].shape[1]), jnp.bfloat16)
+        for lead, n in counts
     ]
     return pl.pallas_call(
         body,
         out_shape=shapes,
         in_specs=[pl.BlockSpec(memory_space=pltpu.SMEM)]
         + [pl.BlockSpec(memory_space=pltpu.VMEM)] * len(sources),
-        out_specs=[pl.BlockSpec(memory_space=pltpu.VMEM)] * len(parts),
+        out_specs=[pl.BlockSpec(memory_space=pltpu.VMEM)] * len(shapes),
         compiler_params=pltpu.CompilerParams(vmem_limit_bytes=16 * MIB),
         name="compact_rows",
-    )(experts, *sources)
+    )(targets, *sources)
 
 
 def hold_kernel(gate_w, up_w, gate_out, up_out, sems):
@@ -239,31 +238,26 @@
     bits = [1 << b for b in range(1, planes.bit_length() - 1)]
     last = sum(bits)
     masks = sorted(range(2, last, 2), key=lambda m: bin(m).count("1"))
-    ends = [i for i, m in enumerate(masks) if m ^ last in bits]
-    hops = [last ^ masks[i] for i in ends]
-    tiles = (width + LANES) // LANES
-    cuts = [LANES * (tiles * i // len(bits)) for i in range(len(bits) + 1)]
-    full = (0, width + LANES)
+    side = me & 1
+    hop = jnp.where(side == 0, bits[0], bits[1]).astype(jnp.int32)
+    ends = [masks.index(last ^ b) for b in bits[:2]]
+    chosen = jnp.where(side == 0, ends[0], ends[1]).astype(jnp.int32)
+    targets = jnp.stack([me, me ^ 1, me ^ hop, me ^ hop ^ 1, chosen])
     weights = hold(w_gate, w_up)
     total = jnp.zeros((devices, rank * rank), jnp.float32)
-    experts = jnp.stack([me, me ^ 1] + [me ^ hop ^ b for hop in hops for b in (0, 1)])
     own = me.reshape(1)
     args = (capacity, top, rank)
 
     def add(pieces):
         return sketch(pieces, own, weights, proj_hidden.T, total, top, rank)
 
-    def halves(arrived):
-        beside = [swap(f, 1) for f in arrived]
-        return [[(f, 0, cut) for f, cut in zip(arrived, cuts)]] + [
-            [(f, 1, cut) for f, cut in zip(beside, cuts)]
-        ]
-
     def lanes(found):
         return [[(found[0], 0, 0)], [(swap(found[1], 1), 0, 0)]]
 
-    def column(i):
-        slot = slots[i]
+    def far(arrived):
+        return [[(arrived, 0, 0)], [(swap(arrived, 1), 1, 0)]]
+
+    def column(slot):
         got = {0: slot}
         for mask in masks:
             low = mask & -mask
@@ -271,34 +265,21 @@
         return [got[mask] for mask in masks]
 
     def gather(sets):
-        n = len(sets)
-        parts, spans = [(0,), (1,)], [(0, n * len(masks)) + full] * 2
-        for k, i in enumerate(ends):
-            parts.append((2 + 2 * k, 3 + 2 * k))
-            spans.append((n * i, n * i + n, cuts[k], cuts[k + 1]))
-        sources = [s[m] for m in range(len(masks)) for s in sets]
-        found = compact(sources, experts, parts, spans, *args)
-        return found[:2], found[2:]
-
-    def send(found):
-        return [swap(f, hop) for f, hop in zip(found, hops)]
-
-    columns = [column(i) for i in range(groups - 2)]
-    near, far = gather(columns)
+        found = compact([s[m] for m in range(len(masks)) for s in sets], len(sets), targets, *args)
+        return found[:2], lax.ppermute(found[2], AXES, further)
+
+    further = [(i, i ^ bits[i & 1]) for i in range(devices)]
+    near, far_first = gather([column(slot) for slot in slots[:-2]])
     total = add(lanes(near))
-    slots[-1], far_first, total = lax.optimization_barrier((slots[-1], far, total))
-    far_first = send(far_first)
-    middle, total = lax.optimization_barrier((column(groups - 2), total))
-    near, far = gather([middle])
-    far_middle = send(far)
-    mine = compact(slots, experts, [(0,), (1,)], [(0, groups) + full] * 2, *args)
+    slots[-1], total = lax.optimization_barrier((slots[-1], total))
+    near, far_middle = gather([column(slots[-2])])
+    mine = compact(slots, None, targets, *args)
     total = add(lanes(near) + lanes(mine))
-    final, total = lax.optimization_barrier((column(groups - 1), total))
-    near, far = gather([final])
-    far_last = send(far)
-    total = add(lanes(near) + halves(far_first))
+    final, total = lax.optimization_barrier((column(slots[-1]), total))
+    near, far_last = gather([final])
+    total = add(lanes(near) + far(far_first))
     far_last, total = lax.optimization_barrier((far_last, total))
-    total = add(halves(far_middle) + halves(far_last))
+    total = add(far(far_middle) + far(far_last))
     owned = lax.all_to_all(total, AXES, split_axis=0, concat_axis=0, tiled=True)
     return owned[None]
 

time: 124 us -> 106 us (0.85)
  waiting for transfers between devices: 45.8 us -> 33.8 us
  starting transfers between devices: 32.7 us -> 29 us
  blocking collectives: 12.7 us -> 10.5 us
    ppermute x24 -> x15, waiting for transfers between devices: 37.1 us -> 23.8 us  [swap(): return lax.ppermute(value, AXES, [(i, i ^ bits) for i in range(devices)])]
    ppermute x24 -> x15, starting transfers between devices: 19.4 us -> 11.2 us  [swap(): return lax.ppermute(value, AXES, [(i, i ^ bits) for i in range(devices)])]
    ppermute x0 -> x3, starting transfers between devices: none -> 4.18 us  [gather(): return (found[:2], lax.ppermute(found[2], AXES, further))]
    all_to_all x1, blocking collectives: 12.7 us -> 10.5 us  [on_device(): owned = lax.all_to_all(total, AXES, split_axis=0, concat_axis=0, tiled=True)]
    ppermute x0 -> x3, waiting for transfers between devices: none -> 1.42 us  [gather(): return (found[:2], lax.ppermute(found[2], AXES, further))]
  transfers between devices with their start and end apart: 27 -> 21, of which waited for: 11 -> 6; matrix products, arithmetic and copies ran while one was open for 0% -> 0% of each run, Pallas kernels for 22% -> 25%
where the time goes in v3:
time: 106 us
  waiting for transfers between devices  33.8 us (32%)
  Pallas kernels  31.1 us (29%)
  starting transfers between devices  29 us (27%)
  blocking collectives  10.5 us (10%)
    ppermute x15, waiting for transfers between devices, swap(): return lax.ppermute(value, AXES, [(i, i ^ bits) for i in range(devices)])  23.8 us
    pallas_call x4, Pallas kernels, sketch(): pl.pallas_call(body, out_shape=jax.ShapeDtypeStruct(total.shape, jnp.floa...  17.1 us
    ppermute x3, starting transfers between devices, turn(): lax.ppermute(value, AXES, [(a * planes + b, c * planes + d) for (a, b), (...  13.7 us
    ppermute x15, starting transfers between devices, swap(): return lax.ppermute(value, AXES, [(i, i ^ bits) for i in range(devices)])  11.2 us
    all_to_all x1, blocking collectives, on_device(): owned = lax.all_to_all(total, AXES, split_axis=0, concat_axis=0, tiled=True)  10.5 us
    ppermute x3, waiting for transfers between devices, turn(): lax.ppermute(value, AXES, [(a * planes + b, c * planes + d) for (a, b), (...  8.54 us
    pallas_call x4, Pallas kernels, compact(): pl.pallas_call(body, out_shape=shapes, in_specs=[pl.BlockSpec(memory_spac...  6.49 us
    pallas_call x1, Pallas kernels, hold(): pl.pallas_call(hold_kernel, out_shape=[pltpu.VMEM(shape, jnp.bfloat16)] *...  5.78 us
  transfers between devices with their start and end apart: 21, of which 6 were waited for; matrix products, arithmetic and copies ran while one was open for 0% of the time, Pallas kernels for 25%

profile of v3, /device:TPU:0, one launch (start us, length us, event | category | flops | bytes accessed | tf_op | source)
XLA Modules:
  0.0 105.5 jit_solution(14855831744111663515)
XLA Ops:
  0.0 1.8 %extend_rows.1.refs_0_ = bf16[64,4224]{1,0:T(8,128)(2,1)S(1)} custom-call(bf16[64,4096]{1,0:T(8,128)(2,1)} %tokens.1, bf16[64,4096]{1,0:T(8,128)(2,1)} %refs_0_.1, bf16[32,4096]{1,0:T(8,128)(2,1)} %bitcast.18, s32[8,64]{1,0:T(8,128)} %bitcast.19, bf16[8,64]{1,0:T(8,128)(2,1)} %bitcast.20, s32[1,64]{1,0:T(1,128)} %bitcast.21), custom_call_target="tpu_custom_call" | custom-call | tf_op jit(solution)/shard_map/extend_rows/pallas_call | solution.py:53
  1.8 5.1 %collective-permute-start = (bf16[64,4224]{1,0:T(8,128)(2,1)S(1)}, bf16[64,4224]{1,0:T(8,128)(2,1)S(1)}, u32[]{:S(2)}, u32[]{:S(2)}) collective-permute-start(bf16[64,4224]{1,0:T(8,128)(2,1)S(1)} %extend_rows.1.refs_0_), channel_id=1, source_target_pairs={{8,0},{9,1},{10,2},{11,3},{12,4},{13,5},{14,6},{15,7},{16,8},{17,9... | collective-permute-start | bytes 1622024 | tf_op jit(solution)/shard_map/ppermute | solution.py:230
  6.9 1.5 %collective-permute-start.7 = (bf16[64,4224]{1,0:T(8,128)(2,1)S(1)}, bf16[64,4224]{1,0:T(8,128)(2,1)S(1)}, u32[]{:S(2)}, u32[]{:S(2)}) collective-permute-start(bf16[64,4224]{1,0:T(8,128)(2,1)S(1)} %extend_rows.1.refs_0_), channel_id=1, source_target_pairs={{0,2},{1,3},{2,0},{3,1},{4,6},{5,7},{6,4},{7,5},{8,10},{9,11},{10,... | collective-permute-start | bytes 1622024 | tf_op jit(solution)/shard_map/ppermute | solution.py:226
  8.4 1.5 %collective-permute-start.9 = (bf16[64,4224]{1,0:T(8,128)(2,1)S(1)}, bf16[64,4224]{1,0:T(8,128)(2,1)S(1)}, u32[]{:S(2)}, u32[]{:S(2)}) collective-permute-start(bf16[64,4224]{1,0:T(8,128)(2,1)S(1)} %extend_rows.1.refs_0_), channel_id=1, source_target_pairs={{0,4},{1,5},{2,6},{3,7},{4,0},{5,1},{6,2},{7,3},{8,12},{9,13},{10,... | collective-permute-start | bytes 1622024 | tf_op jit(solution)/shard_map/ppermute | solution.py:226
  9.9 8.5 %collective-permute-done.refs_1_ = bf16[64,4224]{1,0:T(8,128)(2,1)S(1)} collective-permute-done((bf16[64,4224]{1,0:T(8,128)(2,1)S(1)}, bf16[64,4224]{1,0:T(8,128)(2,1)S(1)}, u32[]{:S(2)}, u32[]{:S(2)}) %collective-permute-start) | collective-permute-done | bytes 540704 | tf_op jit(solution)/shard_map/ppermute | solution.py:230
  18.4 1.5 %collective-permute-start.10 = (bf16[64,4224]{1,0:T(8,128)(2,1)S(1)}, bf16[64,4224]{1,0:T(8,128)(2,1)S(1)}, u32[]{:S(2)}, u32[]{:S(2)}) collective-permute-start(bf16[64,4224]{1,0:T(8,128)(2,1)S(1)} %collective-permute-done.refs_1_), channel_id=1, source_target_pairs={{0,4},{1,5},{2,6},{3,7},{4,0},{5,1},{6,2},{7,3},{8,12},{9,13},{10,... | collective-permute-start | bytes 1622024 | tf_op jit(solution)/shard_map/ppermute | solution.py:226
  20.0 1.5 %collective-permute-start.8 = (bf16[64,4224]{1,0:T(8,128)(2,1)S(1)}, bf16[64,4224]{1,0:T(8,128)(2,1)}, u32[]{:S(2)}, u32[]{:S(2)}) collective-permute-start(bf16[64,4224]{1,0:T(8,128)(2,1)S(1)} %collective-permute-done.refs_1_), channel_id=1, source_target_pairs={{0,2},{1,3},{2,0},{3,1},{4,6},{5,7},{6,4},{7,5},{8,10},{9,11},{10,... | collective-permute-start | bytes 1622024 | tf_op jit(solution)/shard_map/ppermute | solution.py:226
  21.5 4.3 %collective-permute-start.1 = (bf16[64,4224]{1,0:T(8,128)(2,1)S(1)}, bf16[64,4224]{1,0:T(8,128)(2,1)S(1)}, u32[]{:S(2)}, u32[]{:S(2)}) collective-permute-start(bf16[64,4224]{1,0:T(8,128)(2,1)S(1)} %collective-permute-done.refs_1_), channel_id=1, source_target_pairs={{8,0},{9,1},{10,2},{11,3},{12,4},{13,5},{14,6},{15,7},{16,8},{17,9... | collective-permute-start | bytes 1622024 | tf_op jit(solution)/shard_map/ppermute | solution.py:230
  25.8 0.1 stack.20.targets
  25.8 0.0 collective-permute-done.7.refs_0_
  25.8 0.0 collective-permute-done.9.refs_2_
  25.8 7.6 %collective-permute-done.10.refs_3_ = bf16[64,4224]{1,0:T(8,128)(2,1)S(1)} collective-permute-done((bf16[64,4224]{1,0:T(8,128)(2,1)S(1)}, bf16[64,4224]{1,0:T(8,128)(2,1)S(1)}, u32[]{:S(2)}, u32[]{:S(2)}) %collective-permute-start.10) | collective-permute-done | bytes 540704 | tf_op jit(solution)/shard_map/ppermute | solution.py:226
  33.5 2.3 %compact_rows.5 = (bf16[1,96,4224]{2,1,0:T(8,128)(2,1)S(1)}, bf16[1,96,4224]{2,1,0:T(8,128)(2,1)S(1)}, bf16[2,48,4224]{2,1,0:T(8,128)(2,1)S(1)}) custom-call(s32[5]{0:T(128)S(1)} %stack.20.targets, bf16[64,4224]{1,0:T(8,128)(2,1)S(1)} %collective-permute-done.7.refs_0_, bf16[64,4224]{1,0:T(8,128)(2,1)} %collective-permute-done.8.refs_1_, ...), custom_call_target="tpu_custom_call" | custom-call | tf_op jit(solution)/shard_map/compact_rows/pallas_call | solution.py:114
  35.8 0.1 collective-permute-start.11
  35.8 0.0 collective-permute-done.1.refs_2_
  35.9 4.3 %collective-permute-start.6 = (bf16[64,4224]{1,0:T(8,128)(2,1)S(1)}, bf16[64,4224]{1,0:T(8,128)(2,1)S(1)}, u32[]{:S(2)}, u32[]{:S(2)}) collective-permute-start(bf16[64,4224]{1,0:T(8,128)(2,1)S(1)} %collective-permute-done.1.refs_2_), channel_id=1, source_target_pairs={{8,0},{9,1},{10,2},{11,3},{12,4},{13,5},{14,6},{15,7},{16,8},{17,9... | collective-permute-start | bytes 1622024 | tf_op jit(solution)/shard_map/ppermute | solution.py:230
  40.1 1.0 collective-permute-start.18
  41.2 1.0 collective-permute-start.2
  42.2 0.5 collective-permute-start.3
  42.7 5.8 %hold_weights.1 = (bf16[4096,1024]{1,0:T(8,128)(2,1)S(1)}, bf16[4096,1024]{1,0:T(8,128)(2,1)S(1)}) custom-call(bf16[1,4096,1024]{2,1,0:T(8,128)(2,1)} %gate_w.1, bf16[1,4096,1024]{2,1,0:T(8,128)(2,1)} %up_w.1), custom_call_target="tpu_custom_call" | custom-call | tf_op jit(solution)/shard_map/hold_weights/pallas_call | solution.py:138
  48.5 0.0 collective-permute-done.11.refs_1_
  48.5 4.0 %sketch_rows.4.refs_7_ = f32[32,1024]{1,0:T(8,128)S(1)} custom-call(s32[1]{0:T(128)} %bitcast.expert, bf16[1,96,4224]{2,1,0:T(8,128)(2,1)S(1)} %get-tuple-element.26.refs_0_, bf16[1,96,4224]{2,1,0:T(8,128)(2,1)S(1)} %collective-permute-done.11.refs_1_, bf16[4096,1024]{1,0:T(8,128)(2,1)S(1)} %get-tuple-element.28.refs_2_.refs_4_, ...), custom_call_target="tpu_custom_call" | custom-call | tf_op jit(solution)/shard_map/sketch_rows/pallas_call | solution.py:202
  52.5 0.0 collective-permute-done.6.refs_3_
  52.5 1.5 %compact_rows.6 = (bf16[1,96,4224]{2,1,0:T(8,128)(2,1)S(1)}, bf16[1,96,4224]{2,1,0:T(8,128)(2,1)S(1)}) custom-call(s32[5]{0:T(128)S(1)} %stack.20.targets, bf16[64,4224]{1,0:T(8,128)(2,1)S(1)} %extend_rows.1.refs_0_, bf16[64,4224]{1,0:T(8,128)(2,1)S(1)} %collective-permute-done.refs_1_, bf16[64,4224]{1,0:T(8,128)(2,1)S(1)} %collective-permute-done.1.refs_2_, ...), custom_call_target="tpu_custom_call" | custom-call | tf_op jit(solution)/shard_map/compact_rows/pallas_call | solution.py:114
  54.1 0.1 collective-permute-start.15
  54.1 1.1 %collective-permute-start.12 = (bf16[64,4224]{1,0:T(8,128)(2,1)S(1)}, bf16[64,4224]{1,0:T(8,128)(2,1)S(1)}, u32[]{:S(2)}, u32[]{:S(2)}) collective-permute-start(bf16[64,4224]{1,0:T(8,128)(2,1)S(1)} %collective-permute-done.6.refs_3_), channel_id=1, source_target_pairs={{0,2},{1,3},{2,0},{3,1},{4,6},{5,7},{6,4},{7,5},{8,10},{9,11},{10,... | collective-permute-start | bytes 1622024 | tf_op jit(solution)/shard_map/ppermute | solution.py:226
  55.2 13.2 %collective-permute-done.2.refs_0_ = bf16[64,4224]{1,0:T(8,128)(2,1)S(1)} collective-permute-done((bf16[64,4224]{1,0:T(8,128)(2,1)S(1)}, bf16[64,4224]{1,0:T(8,128)(2,1)S(1)}, u32[]{:S(2)}, u32[]{:S(2)}) %collective-permute-start.2) | collective-permute-done | bytes 540704 | tf_op jit(solution)/shard_map/ppermute | solution.py:226
  68.5 1.5 %collective-permute-start.13 = (bf16[64,4224]{1,0:T(8,128)(2,1)S(1)}, bf16[64,4224]{1,0:T(8,128)(2,1)S(1)}, u32[]{:S(2)}, u32[]{:S(2)}) collective-permute-start(bf16[64,4224]{1,0:T(8,128)(2,1)S(1)} %collective-permute-done.6.refs_3_), channel_id=1, source_target_pairs={{0,4},{1,5},{2,6},{3,7},{4,0},{5,1},{6,2},{7,3},{8,12},{9,13},{10,... | collective-permute-start | bytes 1622024 | tf_op jit(solution)/shard_map/ppermute | solution.py:226
  70.0 1.3 %compact_rows.4 = (bf16[1,48,4224]{2,1,0:T(8,128)(2,1)S(1)}, bf16[1,48,4224]{2,1,0:T(8,128)(2,1)S(1)}, bf16[2,24,4224]{2,1,0:T(8,128)(2,1)S(1)}) custom-call(s32[5]{0:T(128)S(1)} %stack.20.targets, bf16[64,4224]{1,0:T(8,128)(2,1)S(1)} %collective-permute-done.2.refs_0_, bf16[64,4224]{1,0:T(8,128)(2,1)S(1)} %collective-permute-done.3.refs_1_), custom_call_target="tpu_custom_call" | custom-call | tf_op jit(solution)/shard_map/compact_rows/pallas_call | solution.py:114
  71.3 0.1 collective-permute-start.14
  71.4 0.5 collective-permute-start.19
  71.9 1.2 %collective-permute-done.14.refs_1_ = bf16[1,48,4224]{2,1,0:T(8,128)(2,1)S(1)} collective-permute-done((bf16[1,48,4224]{2,1,0:T(8,128)(2,1)S(1)}, bf16[1,48,4224]{2,1,0:T(8,128)(2,1)S(1)}, u32[]{:S(2)}, u32[]{:S(2)}) %collective-permute-start.14) | collective-permute-done | bytes 405536 | tf_op jit(solution)/shard_map/ppermute | solution.py:226
  73.1 1.1 %collective-permute-start.4 = (bf16[2,24,4224]{2,1,0:T(8,128)(2,1)S(1)}, bf16[2,24,4224]{2,1,0:T(8,128)(2,1)S(1)}, u32[]{:S(2)}, u32[]{:S(2)}) collective-permute-start(bf16[2,24,4224]{2,1,0:T(8,128)(2,1)S(1)} %get-tuple-element.25), channel_id=1, source_target_pairs={{0,2},{1,5},{2,0},{3,7},{4,6},{5,1},{6,4},{7,3},{8,10},{9,13},{10,... | collective-permute-start | bytes 1216520 | tf_op jit(solution)/shard_map/ppermute | solution.py:269
  74.3 5.8 %sketch_rows.5.refs_7_ = f32[32,1024]{1,0:T(8,128)S(1)} custom-call(s32[1]{0:T(128)} %bitcast.expert, bf16[1,48,4224]{2,1,0:T(8,128)(2,1)S(1)} %get-tuple-element.31.refs_0_, bf16[1,48,4224]{2,1,0:T(8,128)(2,1)S(1)} %collective-permute-done.14.refs_1_, bf16[1,96,4224]{2,1,0:T(8,128)(2,1)S(1)} %get-tuple-element.33.refs_2_, ...), custom_call_target="tpu_custom_call" | custom-call | tf_op jit(solution)/shard_map/sketch_rows/pallas_call | solution.py:202
  80.1 0.0 collective-permute-done.12.refs_0_
  80.1 0.0 collective-permute-done.13.refs_1_
  80.1 1.3 %compact_rows.7 = (bf16[1,48,4224]{2,1,0:T(8,128)(2,1)S(1)}, bf16[1,48,4224]{2,1,0:T(8,128)(2,1)S(1)}, bf16[2,24,4224]{2,1,0:T(8,128)(2,1)S(1)}) custom-call(s32[5]{0:T(128)S(1)} %stack.20.targets, bf16[64,4224]{1,0:T(8,128)(2,1)S(1)} %collective-permute-done.12.refs_0_, bf16[64,4224]{1,0:T(8,128)(2,1)S(1)} %collective-permute-done.13.refs_1_), custom_call_target="tpu_custom_call" | custom-call | tf_op jit(solution)/shard_map/compact_rows/pallas_call | solution.py:114
  81.5 0.1 collective-permute-start.17
  81.6 2.0 %collective-permute-start.16 = (bf16[2,24,4224]{2,1,0:T(8,128)(2,1)S(1)}, bf16[2,24,4224]{2,1,0:T(8,128)(2,1)S(1)}, u32[]{:S(2)}, u32[]{:S(2)}) collective-permute-start(bf16[2,24,4224]{2,1,0:T(8,128)(2,1)S(1)} %get-tuple-element.38), channel_id=1, source_target_pairs={{0,2},{1,5},{2,0},{3,7},{4,6},{5,1},{6,4},{7,3},{8,10},{9,13},{10,... | collective-permute-start | bytes 1216520 | tf_op jit(solution)/shard_map/ppermute | solution.py:269
  83.6 0.3 collective-permute-start.5
  83.9 4.2 %sketch_rows.6.refs_7_ = f32[32,1024]{1,0:T(8,128)S(1)} custom-call(s32[1]{0:T(128)} %bitcast.expert, bf16[1,48,4224]{2,1,0:T(8,128)(2,1)S(1)} %get-tuple-element.39.refs_0_, bf16[1,48,4224]{2,1,0:T(8,128)(2,1)S(1)} %collective-permute-done.17.refs_1_, bf16[2,48,4224]{2,1,0:T(8,128)(2,1)S(1)} %collective-permute-done.18.refs_2_, ...), custom_call_target="tpu_custom_call" | custom-call | tf_op jit(solution)/shard_map/sketch_rows/pallas_call | solution.py:202
  88.1 1.4 %collective-permute-done.16.refs_2_ = bf16[2,24,4224]{2,1,0:T(8,128)(2,1)S(1)} collective-permute-done((bf16[2,24,4224]{2,1,0:T(8,128)(2,1)S(1)}, bf16[2,24,4224]{2,1,0:T(8,128)(2,1)S(1)}, u32[]{:S(2)}, u32[]{:S(2)}) %collective-permute-start.16) | collective-permute-done | bytes 405536 | tf_op jit(solution)/shard_map/ppermute | solution.py:269
  89.5 0.0 collective-permute-done.5.refs_1_
  89.5 1.7 %collective-permute-done.20.refs_3_ = bf16[2,24,4224]{2,1,0:T(8,128)(2,1)S(1)} collective-permute-done((bf16[2,24,4224]{2,1,0:T(8,128)(2,1)S(1)}, bf16[2,24,4224]{2,1,0:T(8,128)(2,1)S(1)}, u32[]{:S(2)}, u32[]{:S(2)}) %collective-permute-start.20) | collective-permute-done | bytes 405536 | tf_op jit(solution)/shard_map/ppermute | solution.py:226
  91.3 2.9 %sketch_rows.7 = f32[32,1024]{1,0:T(8,128)S(1)} custom-call(s32[1]{0:T(128)} %bitcast.expert, bf16[2,24,4224]{2,1,0:T(8,128)(2,1)S(1)} %collective-permute-done.4.refs_0_, bf16[2,24,4224]{2,1,0:T(8,128)(2,1)S(1)} %collective-permute-done.5.refs_1_, bf16[2,24,4224]{2,1,0:T(8,128)(2,1)S(1)} %collective-permute-done.16.refs_2_, ...), custom_call_target="tpu_custom_call" | custom-call | tf_op jit(solution)/shard_map/sketch_rows/pallas_call | solution.py:202
  94.2 0.1 copy.10
  94.4 10.5 %all_to_all.9 = f32[32,1,1024]{2,1,0:T(1,128)S(1)} all-to-all(f32[32,1,1024]{2,1,0:T(1,128)S(1)} %copy.10), channel_id=1, replica_groups=mesh['expert'=4,'dp'=8] {'expert','dp'}, dimensions={0} | all-to-all | bytes 262144 | tf_op jit(solution)/shard_map/all_to_all | solution.py:283
  104.9 0.7 copy.11
  (11 shorter events, 0.0 us)
Async XLA Ops:
  1.8 16.6 %collective-permute-start = (bf16[64,4224]{1,0:T(8,128)(2,1)S(1)}, bf16[64,4224]{1,0:T(8,128)(2,1)S(1)}, u32[]{:S(2)}, u32[]{:S(2)}) collective-permute-start(bf16[64,4224]{1,0:T(8,128)(2,1)S(1)} %extend_rows.1.refs_0_), channel_id=1, source_target_pairs={{8,0},{9,1},{10,2},{11,3},{12,4},{13,5},{14,6},{15,7},{16,8},{17,9... | collective-permute-start | bytes 1622024 | tf_op jit(solution)/shard_map/ppermute | solution.py:230
  6.9 18.9 %collective-permute-start.7 = (bf16[64,4224]{1,0:T(8,128)(2,1)S(1)}, bf16[64,4224]{1,0:T(8,128)(2,1)S(1)}, u32[]{:S(2)}, u32[]{:S(2)}) collective-permute-start(bf16[64,4224]{1,0:T(8,128)(2,1)S(1)} %extend_rows.1.refs_0_), channel_id=1, source_target_pairs={{0,2},{1,3},{2,0},{3,1},{4,6},{5,7},{6,4},{7,5},{8,10},{9,11},{10,... | collective-permute-start | bytes 1622024 | tf_op jit(solution)/shard_map/ppermute | solution.py:226
  8.4 17.4 %collective-permute-start.9 = (bf16[64,4224]{1,0:T(8,128)(2,1)S(1)}, bf16[64,4224]{1,0:T(8,128)(2,1)S(1)}, u32[]{:S(2)}, u32[]{:S(2)}) collective-permute-start(bf16[64,4224]{1,0:T(8,128)(2,1)S(1)} %extend_rows.1.refs_0_), channel_id=1, source_target_pairs={{0,4},{1,5},{2,6},{3,7},{4,0},{5,1},{6,2},{7,3},{8,12},{9,13},{10,... | collective-permute-start | bytes 1622024 | tf_op jit(solution)/shard_map/ppermute | solution.py:226
  18.4 15.0 %collective-permute-start.10 = (bf16[64,4224]{1,0:T(8,128)(2,1)S(1)}, bf16[64,4224]{1,0:T(8,128)(2,1)S(1)}, u32[]{:S(2)}, u32[]{:S(2)}) collective-permute-start(bf16[64,4224]{1,0:T(8,128)(2,1)S(1)} %collective-permute-done.refs_1_), channel_id=1, source_target_pairs={{0,4},{1,5},{2,6},{3,7},{4,0},{5,1},{6,2},{7,3},{8,12},{9,13},{10,... | collective-permute-start | bytes 1622024 | tf_op jit(solution)/shard_map/ppermute | solution.py:226
  20.0 13.5 %collective-permute-start.8 = (bf16[64,4224]{1,0:T(8,128)(2,1)S(1)}, bf16[64,4224]{1,0:T(8,128)(2,1)}, u32[]{:S(2)}, u32[]{:S(2)}) collective-permute-start(bf16[64,4224]{1,0:T(8,128)(2,1)S(1)} %collective-permute-done.refs_1_), channel_id=1, source_target_pairs={{0,2},{1,3},{2,0},{3,1},{4,6},{5,7},{6,4},{7,5},{8,10},{9,11},{10,... | collective-permute-start | bytes 1622024 | tf_op jit(solution)/shard_map/ppermute | solution.py:226
  21.5 14.4 %collective-permute-start.1 = (bf16[64,4224]{1,0:T(8,128)(2,1)S(1)}, bf16[64,4224]{1,0:T(8,128)(2,1)S(1)}, u32[]{:S(2)}, u32[]{:S(2)}) collective-permute-start(bf16[64,4224]{1,0:T(8,128)(2,1)S(1)} %collective-permute-done.refs_1_), channel_id=1, source_target_pairs={{8,0},{9,1},{10,2},{11,3},{12,4},{13,5},{14,6},{15,7},{16,8},{17,9... | collective-permute-start | bytes 1622024 | tf_op jit(solution)/shard_map/ppermute | solution.py:230
  35.8 12.7 %collective-permute-start.11 = (bf16[1,96,4224]{2,1,0:T(8,128)(2,1)S(1)}, bf16[1,96,4224]{2,1,0:T(8,128)(2,1)S(1)}, u32[]{:S(2)}, u32[]{:S(2)}) collective-permute-start(bf16[1,96,4224]{2,1,0:T(8,128)(2,1)S(1)} %get-tuple-element.27), channel_id=1, source_target_pairs={{0,1},{1,0},{2,3},{3,2},{4,5},{5,4},{6,7},{7,6},{8,9},{9,8},{10,11... | collective-permute-start | bytes 2433032 | tf_op jit(solution)/shard_map/ppermute | solution.py:226
  35.9 16.7 %collective-permute-start.6 = (bf16[64,4224]{1,0:T(8,128)(2,1)S(1)}, bf16[64,4224]{1,0:T(8,128)(2,1)S(1)}, u32[]{:S(2)}, u32[]{:S(2)}) collective-permute-start(bf16[64,4224]{1,0:T(8,128)(2,1)S(1)} %collective-permute-done.1.refs_2_), channel_id=1, source_target_pairs={{8,0},{9,1},{10,2},{11,3},{12,4},{13,5},{14,6},{15,7},{16,8},{17,9... | collective-permute-start | bytes 1622024 | tf_op jit(solution)/shard_map/ppermute | solution.py:230
  40.1 8.3 %copy-start = (bf16[1024,32]{0,1:T(8,128)(2,1)S(1)}, bf16[1024,32]{0,1:T(8,128)(2,1)}, u32[]{:S(2)}) copy-start(bf16[1024,32]{0,1:T(8,128)(2,1)} %param.16) | copy-start | bytes 196612
  40.1 31.3 %collective-permute-start.18 = (bf16[2,48,4224]{2,1,0:T(8,128)(2,1)S(1)}, bf16[2,48,4224]{2,1,0:T(8,128)(2,1)S(1)}, u32[]{:S(2)}, u32[]{:S(2)}) collective-permute-start(bf16[2,48,4224]{2,1,0:T(8,128)(2,1)S(1)} %get-tuple-element.41), channel_id=1, source_target_pairs={{0,2},{1,5},{2,0},{3,7},{4,6},{5,1},{6,4},{7,3},{8,10},{9,13},{10,... | collective-permute-start | bytes 2433032 | tf_op jit(solution)/shard_map/ppermute | solution.py:269
  41.2 27.3 %collective-permute-start.2 = (bf16[64,4224]{1,0:T(8,128)(2,1)S(1)}, bf16[64,4224]{1,0:T(8,128)(2,1)S(1)}, u32[]{:S(2)}, u32[]{:S(2)}) collective-permute-start(bf16[64,4224]{1,0:T(8,128)(2,1)S(1)} %collective-permute-done.1.refs_2_), channel_id=1, source_target_pairs={{0,2},{1,3},{2,0},{3,1},{4,6},{5,7},{6,4},{7,5},{8,10},{9,11},{10,... | collective-permute-start | bytes 1622024 | tf_op jit(solution)/shard_map/ppermute | solution.py:226
  42.2 27.8 %collective-permute-start.3 = (bf16[64,4224]{1,0:T(8,128)(2,1)S(1)}, bf16[64,4224]{1,0:T(8,128)(2,1)S(1)}, u32[]{:S(2)}, u32[]{:S(2)}) collective-permute-start(bf16[64,4224]{1,0:T(8,128)(2,1)S(1)} %collective-permute-done.1.refs_2_), channel_id=1, source_target_pairs={{0,4},{1,5},{2,6},{3,7},{4,0},{5,1},{6,2},{7,3},{8,12},{9,13},{10,... | collective-permute-start | bytes 1622024 | tf_op jit(solution)/shard_map/ppermute | solution.py:226
  54.1 20.2 %collective-permute-start.15 = (bf16[1,96,4224]{2,1,0:T(8,128)(2,1)S(1)}, bf16[1,96,4224]{2,1,0:T(8,128)(2,1)S(1)}, u32[]{:S(2)}, u32[]{:S(2)}) collective-permute-start(bf16[1,96,4224]{2,1,0:T(8,128)(2,1)S(1)} %get-tuple-element.34), channel_id=1, source_target_pairs={{0,1},{1,0},{2,3},{3,2},{4,5},{5,4},{6,7},{7,6},{8,9},{9,8},{10,11... | collective-permute-start | bytes 2433032 | tf_op jit(solution)/shard_map/ppermute | solution.py:226
  54.1 26.0 %collective-permute-start.12 = (bf16[64,4224]{1,0:T(8,128)(2,1)S(1)}, bf16[64,4224]{1,0:T(8,128)(2,1)S(1)}, u32[]{:S(2)}, u32[]{:S(2)}) collective-permute-start(bf16[64,4224]{1,0:T(8,128)(2,1)S(1)} %collective-permute-done.6.refs_3_), channel_id=1, source_target_pairs={{0,2},{1,3},{2,0},{3,1},{4,6},{5,7},{6,4},{7,5},{8,10},{9,11},{10,... | collective-permute-start | bytes 1622024 | tf_op jit(solution)/shard_map/ppermute | solution.py:226
  68.5 11.6 %collective-permute-start.13 = (bf16[64,4224]{1,0:T(8,128)(2,1)S(1)}, bf16[64,4224]{1,0:T(8,128)(2,1)S(1)}, u32[]{:S(2)}, u32[]{:S(2)}) collective-permute-start(bf16[64,4224]{1,0:T(8,128)(2,1)S(1)} %collective-permute-done.6.refs_3_), channel_id=1, source_target_pairs={{0,4},{1,5},{2,6},{3,7},{4,0},{5,1},{6,2},{7,3},{8,12},{9,13},{10,... | collective-permute-start | bytes 1622024 | tf_op jit(solution)/shard_map/ppermute | solution.py:226
  71.3 1.8 %collective-permute-start.14 = (bf16[1,48,4224]{2,1,0:T(8,128)(2,1)S(1)}, bf16[1,48,4224]{2,1,0:T(8,128)(2,1)S(1)}, u32[]{:S(2)}, u32[]{:S(2)}) collective-permute-start(bf16[1,48,4224]{2,1,0:T(8,128)(2,1)S(1)} %get-tuple-element.32), channel_id=1, source_target_pairs={{0,1},{1,0},{2,3},{3,2},{4,5},{5,4},{6,7},{7,6},{8,9},{9,8},{10,11... | collective-permute-start | bytes 1216520 | tf_op jit(solution)/shard_map/ppermute | solution.py:226
  71.4 12.4 %collective-permute-start.19 = (bf16[2,48,4224]{2,1,0:T(8,128)(2,1)S(1)}, bf16[2,48,4224]{2,1,0:T(8,128)(2,1)S(1)}, u32[]{:S(2)}, u32[]{:S(2)}) collective-permute-start(bf16[2,48,4224]{2,1,0:T(8,128)(2,1)S(1)} %collective-permute-done.18.refs_2_), channel_id=1, source_target_pairs={{0,1},{1,0},{2,3},{3,2},{4,5},{5,4},{6,7},{7,6},{8,9},{9,8},{10,11... | collective-permute-start | bytes 2433032 | tf_op jit(solution)/shard_map/ppermute | solution.py:226
  73.1 10.4 %collective-permute-start.4 = (bf16[2,24,4224]{2,1,0:T(8,128)(2,1)S(1)}, bf16[2,24,4224]{2,1,0:T(8,128)(2,1)S(1)}, u32[]{:S(2)}, u32[]{:S(2)}) collective-permute-start(bf16[2,24,4224]{2,1,0:T(8,128)(2,1)S(1)} %get-tuple-element.25), channel_id=1, source_target_pairs={{0,2},{1,5},{2,0},{3,7},{4,6},{5,1},{6,4},{7,3},{8,10},{9,13},{10,... | collective-permute-start | bytes 1216520 | tf_op jit(solution)/shard_map/ppermute | solution.py:269
  81.5 2.4 %collective-permute-start.17 = (bf16[1,48,4224]{2,1,0:T(8,128)(2,1)S(1)}, bf16[1,48,4224]{2,1,0:T(8,128)(2,1)S(1)}, u32[]{:S(2)}, u32[]{:S(2)}) collective-permute-start(bf16[1,48,4224]{2,1,0:T(8,128)(2,1)S(1)} %get-tuple-element.40), channel_id=1, source_target_pairs={{0,1},{1,0},{2,3},{3,2},{4,5},{5,4},{6,7},{7,6},{8,9},{9,8},{10,11... | collective-permute-start | bytes 1216520 | tf_op jit(solution)/shard_map/ppermute | solution.py:226
  81.6 8.0 %collective-permute-start.16 = (bf16[2,24,4224]{2,1,0:T(8,128)(2,1)S(1)}, bf16[2,24,4224]{2,1,0:T(8,128)(2,1)S(1)}, u32[]{:S(2)}, u32[]{:S(2)}) collective-permute-start(bf16[2,24,4224]{2,1,0:T(8,128)(2,1)S(1)} %get-tuple-element.38), channel_id=1, source_target_pairs={{0,2},{1,5},{2,0},{3,7},{4,6},{5,1},{6,4},{7,3},{8,10},{9,13},{10,... | collective-permute-start | bytes 1216520 | tf_op jit(solution)/shard_map/ppermute | solution.py:269
  83.6 6.0 %collective-permute-start.5 = (bf16[2,24,4224]{2,1,0:T(8,128)(2,1)S(1)}, bf16[2,24,4224]{2,1,0:T(8,128)(2,1)S(1)}, u32[]{:S(2)}, u32[]{:S(2)}) collective-permute-start(bf16[2,24,4224]{2,1,0:T(8,128)(2,1)S(1)} %collective-permute-done.4.refs_0_), channel_id=1, source_target_pairs={{0,1},{1,0},{2,3},{3,2},{4,5},{5,4},{6,7},{7,6},{8,9},{9,8},{10,11... | collective-permute-start | bytes 1216520 | tf_op jit(solution)/shard_map/ppermute | solution.py:226
  89.5 1.7 %collective-permute-start.20 = (bf16[2,24,4224]{2,1,0:T(8,128)(2,1)S(1)}, bf16[2,24,4224]{2,1,0:T(8,128)(2,1)S(1)}, u32[]{:S(2)}, u32[]{:S(2)}) collective-permute-start(bf16[2,24,4224]{2,1,0:T(8,128)(2,1)S(1)} %collective-permute-done.16.refs_2_), channel_id=1, source_target_pairs={{0,1},{1,0},{2,3},{3,2},{4,5},{5,4},{6,7},{7,6},{8,9},{9,8},{10,11... | collective-permute-start | bytes 1216520 | tf_op jit(solution)/shard_map/ppermute | solution.py:226

commit v4 on v3

--- a/solution.py
+++ b/solution.py
@@ -10,6 +10,7 @@
 AXES = ("expert", "dp")
 LANES = 128
 MIB = 1 << 20
+LIGHT = pl.CostEstimate(flops=1, bytes_accessed=1, transcendentals=0)
 
 
 def place(width, first):
@@ -57,67 +58,56 @@
         out_specs=pl.BlockSpec(memory_space=pltpu.VMEM),
         scratch_shapes=[pltpu.VMEM(o.shape, o.dtype) for o in operands[1:]]
         + [pltpu.SemaphoreType.DMA((len(operands),))],
-        compiler_params=pltpu.CompilerParams(vmem_limit_bytes=16 * MIB),
+        compiler_params=pltpu.CompilerParams(vmem_limit_bytes=4 * MIB),
         name="extend_rows",
     )(*[pltpu.with_memory_space_constraint(o, pltpu.HBM) for o in operands])
 
 
-def compact_kernel(capacity, top, rank, members, targets, *refs):
-    parts = 2 if members is None else 3
-    sources, outs = refs[:-parts], refs[-parts:]
+def compact_kernel(capacity, top, rank, targets, *refs):
+    sources, outs = refs[:-3], refs[-3:]
     count = len(sources)
     rows, total = sources[0].shape
     width = total - LANES
     meta = jnp.concatenate([s[:, width:] for s in sources], axis=0).astype(jnp.float32)
     lanes = lax.broadcasted_iota(jnp.int32, meta.shape, 1)
-    source = lax.broadcasted_iota(jnp.int32, meta.shape, 0) // rows
     is_route = (lanes >= rank + top) & (lanes < rank + 2 * top)
     hits = jnp.zeros(meta.shape, jnp.float32)
-    for q in range(2 * parts - 2):
+    for q in range(4):
         named = is_route & (meta == targets[q].astype(jnp.float32))
         hit = jnp.sum(named.astype(jnp.float32), axis=1, keepdims=True)
         hits = jnp.where(lanes == q, hit, hits)
-    first = source
-    if members is not None:
-        hits = jnp.where((lanes < 2) | (source // members == targets[4]), hits, 0.0)
-        first = jnp.where(lanes < 2, source, source % members)
     every = count * rows
     here = lax.broadcasted_iota(jnp.int32, (every, every), 0)
     other = lax.broadcasted_iota(jnp.int32, (every, every), 1)
     earlier = ((other < here) & (other // rows == here // rows)).astype(jnp.bfloat16)
     before = dot(earlier, hits.astype(jnp.bfloat16))
-    slots = jnp.where(hits > 0, before + (first * capacity).astype(jnp.float32), -1.0).T
-    picks, spots = [], []
-    for q in range(2 * parts - 2):
-        picked = outs[min(q, 2)].shape[1]
-        spot = lax.broadcasted_iota(jnp.int32, (picked, every), 0).astype(jnp.float32)
-        picks.append((spot == slots[q : q + 1, :]).astype(jnp.bfloat16))
-        spots.append((outs[min(q, 2)], max(q - 2, 0), picked))
-    pick = jnp.concatenate(picks, axis=0)
+    first = lax.broadcasted_iota(jnp.int32, meta.shape, 0) // rows * capacity
+    slots = jnp.where(hits > 0, before + first.astype(jnp.float32), -1.0).T
+    picked = count * capacity
+    spot = lax.broadcasted_iota(jnp.int32, (picked, every), 0).astype(jnp.float32)
+    pick = jnp.concatenate(
+        [(spot == slots[q : q + 1, :]).astype(jnp.bfloat16) for q in range(4)], axis=0
+    )
     step = 4 * LANES
     for at in range(0, total, step):
         end = min(at + step, total)
         found = dot(pick, jnp.concatenate([s[:, at:end] for s in sources], axis=0))
-        row = 0
-        for out, lead, picked in spots:
-            out[lead, :, at:end] = found[row : row + picked].astype(jnp.bfloat16)
-            row += picked
-
-
-def compact(sources, members, targets, capacity, top, rank):
-    body = functools.partial(compact_kernel, capacity, top, rank, members)
-    counts = [(1, len(sources))] * 2 + ([] if members is None else [(2, members)])
-    shapes = [
-        jax.ShapeDtypeStruct((lead, n * capacity, sources[0].shape[1]), jnp.bfloat16)
-        for lead, n in counts
-    ]
+        for q in range(4):
+            part = found[q * picked : (q + 1) * picked].astype(jnp.bfloat16)
+            outs[min(q, 2)][max(q - 2, 0), :, at:end] = part
+
+
+def compact(sources, targets, capacity, top, rank):
+    body = functools.partial(compact_kernel, capacity, top, rank)
+    rows, width = len(sources) * capacity, sources[0].shape[1]
     return pl.pallas_call(
         body,
-        out_shape=shapes,
+        out_shape=[jax.ShapeDtypeStruct((n, rows, width), jnp.bfloat16) for n in (1, 1, 2)],
         in_specs=[pl.BlockSpec(memory_space=pltpu.SMEM)]
         + [pl.BlockSpec(memory_space=pltpu.VMEM)] * len(sources),
-        out_specs=[pl.BlockSpec(memory_space=pltpu.VMEM)] * len(shapes),
-        compiler_params=pltpu.CompilerParams(vmem_limit_bytes=16 * MIB),
+        out_specs=[pl.BlockSpec(memory_space=pltpu.VMEM)] * 3,
+        compiler_params=pltpu.CompilerParams(vmem_limit_bytes=8 * MIB),
+        cost_estimate=LIGHT,
         name="compact_rows",
     )(targets, *sources)
 
@@ -142,6 +132,7 @@
         out_specs=[pl.BlockSpec(memory_space=pltpu.VMEM)] * 2,
         scratch_shapes=[pltpu.SemaphoreType.DMA((2,))],
         compiler_params=pltpu.CompilerParams(vmem_limit_bytes=2 * MIB),
+        cost_estimate=LIGHT,
         name="hold_weights",
     )(*[pltpu.with_memory_space_constraint(w, pltpu.HBM) for w in (w_gate, w_up)])
 
@@ -208,7 +199,8 @@
             pltpu.VMEM((rows, width + LANES), jnp.bfloat16),
             pltpu.VMEM((rows, hidden), jnp.bfloat16),
         ],
-        compiler_params=pltpu.CompilerParams(vmem_limit_bytes=20 * MIB),
+        compiler_params=pltpu.CompilerParams(vmem_limit_bytes=14 * MIB),
+        cost_estimate=LIGHT,
         name="sketch_rows",
     )(expert, *arrays, *weights, proj, total)
 
@@ -222,8 +214,8 @@
     capacity = max(2, 3 * row_count * top // (2 * devices))
     me = lax.axis_index(AXES).astype(jnp.int32)
 
-    def swap(value, bits):
-        return lax.ppermute(value, AXES, [(i, i ^ bits) for i in range(devices)])
+    def swap(value, hops):
+        return lax.ppermute(value, AXES, [(i, i ^ hops[i & 1]) for i in range(devices)])
 
     def turn(value, by):
         pairs = [(((g + by) % groups, p), (g, p)) for g in range(groups) for p in range(planes)]
@@ -233,53 +225,57 @@
 
     ext = extend(tokens, out_grad, proj_out, routes, gate_probs, doc_ids)
     slots = [ext]
-    for j in range(1, groups):
+    for j in range(1, groups - 1):
         slots.append(turn(slots[-1], 1))
+    slots.insert(groups - 2, turn(ext, groups - 1))
     bits = [1 << b for b in range(1, planes.bit_length() - 1)]
-    last = sum(bits)
-    masks = sorted(range(2, last, 2), key=lambda m: bin(m).count("1"))
-    side = me & 1
-    hop = jnp.where(side == 0, bits[0], bits[1]).astype(jnp.int32)
-    ends = [masks.index(last ^ b) for b in bits[:2]]
-    chosen = jnp.where(side == 0, ends[0], ends[1]).astype(jnp.int32)
-    targets = jnp.stack([me, me ^ 1, me ^ hop, me ^ hop ^ 1, chosen])
+    shared = [[b for b in bits if b != bits[core]] for core in (0, 1)]
+    side = jnp.where(me & 1 == 0, bits[0], bits[1]).astype(jnp.int32)
+    targets = jnp.stack([me, me ^ 1, me ^ side, me ^ side ^ 1])
     weights = hold(w_gate, w_up)
     total = jnp.zeros((devices, rank * rank), jnp.float32)
     own = me.reshape(1)
     args = (capacity, top, rank)
 
-    def add(pieces):
+    def sketch_of(total, pieces):
         return sketch(pieces, own, weights, proj_hidden.T, total, top, rank)
 
-    def lanes(found):
-        return [[(found[0], 0, 0)], [(swap(found[1], 1), 0, 0)]]
-
-    def far(arrived):
-        return [[(arrived, 0, 0)], [(swap(arrived, 1), 1, 0)]]
-
-    def column(slot):
-        got = {0: slot}
-        for mask in masks:
-            low = mask & -mask
-            got[mask] = swap(got[mask ^ low], low)
-        return [got[mask] for mask in masks]
-
-    def gather(sets):
-        found = compact([s[m] for m in range(len(masks)) for s in sets], len(sets), targets, *args)
-        return found[:2], lax.ppermute(found[2], AXES, further)
-
-    further = [(i, i ^ bits[i & 1]) for i in range(devices)]
-    near, far_first = gather([column(slot) for slot in slots[:-2]])
-    total = add(lanes(near))
-    slots[-1], total = lax.optimization_barrier((slots[-1], total))
-    near, far_middle = gather([column(slots[-2])])
-    mine = compact(slots, None, targets, *args)
-    total = add(lanes(near) + lanes(mine))
-    final, total = lax.optimization_barrier((column(slots[-1]), total))
-    near, far_last = gather([final])
-    total = add(lanes(near) + far(far_first))
-    far_last, total = lax.optimization_barrier((far_last, total))
-    total = add(far(far_middle) + far(far_last))
+    def gather(slot):
+        sources = [slot]
+        for hops in zip(*shared):
+            sources += [swap(s, hops) for s in sources]
+        return sources
+
+    def spread(sources):
+        own, other, further = compact(sources, targets, *args)
+        return [own, swap(other, (1, 1))], swap(further, bits)
+
+    def near(*pairs):
+        return [[(array, 0, 0)] for pair in pairs for array in pair]
+
+    def far(*arrays):
+        return [
+            [piece] for a in arrays for piece in ((a, 0, 0), (swap(a, (1, 1)), 1, 0))
+        ]
+
+    tied = lax.optimization_barrier
+    near_now, far_now = spread(gather(slots[0]))
+    near_kept, far_kept, far_now = [], [far_now], None
+    for j in range(1, groups):
+        sources, coming = gather(slots[j]), slots[j + 1 : j + 2]
+        group = (near_now, far_kept, sources, coming, [total] if far_kept else [])
+        near_now, far_kept, sources, slots[j + 1 : j + 2], kept = tied(group)
+        near_kept += near_now
+        near_now, far_next = spread(sources)
+        if far_kept:
+            total = sketch_of(kept[0], near(near_kept) + far(*far_kept))
+            near_kept = []
+        far_kept = [] if far_now is None else [far_now]
+        far_now = far_next
+    near_now, far_kept = tied((near_now, far_kept))
+    total = sketch_of(total, near(near_kept, near_now) + far(*far_kept))
+    far_now, total = tied((far_now, total))
+    total = sketch_of(total, far(far_now))
     owned = lax.all_to_all(total, AXES, split_axis=0, concat_axis=0, tiled=True)
     return owned[None]
 

time: 106 us -> 97.7 us (0.922)
  starting transfers between devices: 29 us -> 21.3 us
  blocking collectives: 10.5 us -> 12.7 us
  waiting for transfers between devices: 33.8 us -> 31.7 us
    ppermute x18 -> x16, waiting for transfers between devices: 25.3 us -> 13.9 us  [swap(): lax.ppermute(value, AXES, [(i, i ^ hops[i & 1]) for i in range(devices)])]
    ppermute x3, waiting for transfers between devices: 8.54 us -> 17.8 us  [turn(): lax.ppermute(value, AXES, [(a * planes + b, c * planes + d) for (a, b), (...]
    ppermute x3, starting transfers between devices: 13.7 us -> 9.47 us  [turn(): lax.ppermute(value, AXES, [(a * planes + b, c * planes + d) for (a, b), (...]
    ppermute x18 -> x16, starting transfers between devices: 15.4 us -> 11.9 us  [swap(): lax.ppermute(value, AXES, [(i, i ^ hops[i & 1]) for i in range(devices)])]
    all_to_all x1, blocking collectives: 10.5 us -> 12.7 us  [on_device(): owned = lax.all_to_all(total, AXES, split_axis=0, concat_axis=0, tiled=True)]
  transfers between devices with their start and end apart: 21 -> 19, of which waited for: 6 -> 10; matrix products, arithmetic and copies ran while one was open for 0% -> 0% of each run, Pallas kernels for 25% -> 26%
where the time goes in v4:
time: 97.7 us; the launch traced here: 97.5 us
  waiting for transfers between devices  31.7 us (32%)
  Pallas kernels  30.7 us (31%)
  starting transfers between devices  21.3 us (22%)
  blocking collectives  12.7 us (13%)
    ppermute x3, waiting for transfers between devices, turn(): lax.ppermute(value, AXES, [(a * planes + b, c * planes + d) for (a, b), (...  17.8 us
    pallas_call x4, Pallas kernels, sketch(): pl.pallas_call(body, out_shape=jax.ShapeDtypeStruct(total.shape, jnp.floa...  17.4 us
    ppermute x16, waiting for transfers between devices, swap(): lax.ppermute(value, AXES, [(i, i ^ hops[i & 1]) for i in range(devices)])  13.9 us
    all_to_all x1, blocking collectives, on_device(): owned = lax.all_to_all(total, AXES, split_axis=0, concat_axis=0, tiled=True)  12.7 us
    ppermute x16, starting transfers between devices, swap(): lax.ppermute(value, AXES, [(i, i ^ hops[i & 1]) for i in range(devices)])  11.9 us
    ppermute x3, starting transfers between devices, turn(): lax.ppermute(value, AXES, [(a * planes + b, c * planes + d) for (a, b), (...  9.47 us
    pallas_call x1, Pallas kernels, hold(): pl.pallas_call(hold_kernel, out_shape=[pltpu.VMEM(shape, jnp.bfloat16)] *...  5.78 us
    pallas_call x4, Pallas kernels, compact(): pl.pallas_call(body, out_shape=[jax.ShapeDtypeStruct((n, rows, width), jn...  5.73 us
  transfers between devices with their start and end apart: 19, of which 10 were waited for; matrix products, arithmetic and copies ran while one was open for 0% of the time, Pallas kernels for 26%

profile of v4, /device:TPU:0, one launch (start us, length us, event | category | flops | bytes accessed | tf_op | source)
XLA Modules:
  0.0 97.5 jit_solution(13459696998485884088)
XLA Ops:
  0.0 1.8 %extend_rows.1.refs_0_ = bf16[64,4224]{1,0:T(8,128)(2,1)S(1)} custom-call(bf16[64,4096]{1,0:T(8,128)(2,1)} %tokens.1, bf16[64,4096]{1,0:T(8,128)(2,1)} %refs_0_.1, bf16[32,4096]{1,0:T(8,128)(2,1)} %bitcast.17, s32[8,64]{1,0:T(8,128)} %bitcast.18, bf16[8,64]{1,0:T(8,128)(2,1)} %bitcast.19, s32[1,64]{1,0:T(1,128)} %bitcast.20), custom_call_target="tpu_custom_call" | custom-call | tf_op jit(solution)/shard_map/extend_rows/pallas_call | solution.py:54
  1.8 3.0 %collective-permute-start = (bf16[64,4224]{1,0:T(8,128)(2,1)S(1)}, bf16[64,4224]{1,0:T(8,128)(2,1)S(1)}, u32[]{:S(2)}, u32[]{:S(2)}) collective-permute-start(bf16[64,4224]{1,0:T(8,128)(2,1)S(1)} %extend_rows.1.refs_0_), channel_id=1, source_target_pairs={{0,4},{1,3},{2,6},{3,1},{4,0},{5,7},{6,2},{7,5},{8,12},{9,11},{10,... | collective-permute-start | bytes 1622024 | tf_op jit(solution)/shard_map/ppermute | solution.py:218
  4.8 3.6 %collective-permute-start.3 = (bf16[64,4224]{1,0:T(8,128)(2,1)S(1)}, bf16[64,4224]{1,0:T(8,128)(2,1)S(1)}, u32[]{:S(2)}, u32[]{:S(2)}) collective-permute-start(bf16[64,4224]{1,0:T(8,128)(2,1)S(1)} %extend_rows.1.refs_0_), channel_id=1, source_target_pairs={{8,0},{9,1},{10,2},{11,3},{12,4},{13,5},{14,6},{15,7},{16,8},{17,9... | collective-permute-start | bytes 1622024 | tf_op jit(solution)/shard_map/ppermute | solution.py:222
  8.5 0.1 pad_add_fusion.targets
  8.5 3.6 %collective-permute-done.refs_1_ = bf16[64,4224]{1,0:T(8,128)(2,1)S(1)} collective-permute-done((bf16[64,4224]{1,0:T(8,128)(2,1)S(1)}, bf16[64,4224]{1,0:T(8,128)(2,1)S(1)}, u32[]{:S(2)}, u32[]{:S(2)}) %collective-permute-start) | collective-permute-done | bytes 540704 | tf_op jit(solution)/shard_map/ppermute | solution.py:218
  12.2 1.4 %compact_rows.4 = (bf16[1,48,4224]{2,1,0:T(8,128)(2,1)S(1)}, bf16[1,48,4224]{2,1,0:T(8,128)(2,1)S(1)}, bf16[2,48,4224]{2,1,0:T(8,128)(2,1)S(1)}) custom-call(s32[4]{0:T(128)S(1)} %pad_add_fusion.targets, bf16[64,4224]{1,0:T(8,128)(2,1)S(1)} %extend_rows.1.refs_0_, bf16[64,4224]{1,0:T(8,128)(2,1)S(1)} %collective-permute-done.refs_1_), custom_call_target="tpu_custom_call" | custom-call | flops 1 | bytes 1 | tf_op jit(solution)/shard_map/compact_rows/pallas_call | solution.py:103
  13.6 2.1 %collective-permute-start.2 = (bf16[2,48,4224]{2,1,0:T(8,128)(2,1)S(1)}, bf16[2,48,4224]{2,1,0:T(8,128)(2,1)S(1)}, u32[]{:S(2)}, u32[]{:S(2)}) collective-permute-start(bf16[2,48,4224]{2,1,0:T(8,128)(2,1)S(1)} %get-tuple-element.44), channel_id=1, source_target_pairs={{0,2},{1,5},{2,0},{3,7},{4,6},{5,1},{6,4},{7,3},{8,10},{9,13},{10,... | collective-permute-start | bytes 2433032 | tf_op jit(solution)/shard_map/ppermute | solution.py:218
  15.7 1.6 %collective-permute-start.5 = (bf16[64,4224]{1,0:T(8,128)(2,1)S(1)}, bf16[64,4224]{1,0:T(8,128)(2,1)S(1)}, u32[]{:S(2)}, u32[]{:S(2)}) collective-permute-start(bf16[64,4224]{1,0:T(8,128)(2,1)S(1)} %extend_rows.1.refs_0_), channel_id=1, source_target_pairs={{24,0},{25,1},{26,2},{27,3},{28,4},{29,5},{30,6},{31,7},{0,8},{1,9... | collective-permute-start | bytes 1622024 | tf_op jit(solution)/shard_map/ppermute | solution.py:222
  17.3 4.0 %collective-permute-done.3.refs_0_ = bf16[64,4224]{1,0:T(8,128)(2,1)S(1)} collective-permute-done((bf16[64,4224]{1,0:T(8,128)(2,1)S(1)}, bf16[64,4224]{1,0:T(8,128)(2,1)S(1)}, u32[]{:S(2)}, u32[]{:S(2)}) %collective-permute-start.3) | collective-permute-done | bytes 540704 | tf_op jit(solution)/shard_map/ppermute | solution.py:222
  21.2 0.4 collective-permute-start.4
  21.6 0.0 collective-permute-start.1
  21.6 4.3 %collective-permute-start.8 = (bf16[64,4224]{1,0:T(8,128)(2,1)S(1)}, bf16[64,4224]{1,0:T(8,128)(2,1)S(1)}, u32[]{:S(2)}, u32[]{:S(2)}) collective-permute-start(bf16[64,4224]{1,0:T(8,128)(2,1)S(1)} %collective-permute-done.3.refs_0_), channel_id=1, source_target_pairs={{8,0},{9,1},{10,2},{11,3},{12,4},{13,5},{14,6},{15,7},{16,8},{17,9... | collective-permute-start | bytes 1622024 | tf_op jit(solution)/shard_map/ppermute | solution.py:222
  25.9 7.8 %collective-permute-done.5.refs_0_ = bf16[64,4224]{1,0:T(8,128)(2,1)S(1)} collective-permute-done((bf16[64,4224]{1,0:T(8,128)(2,1)S(1)}, bf16[64,4224]{1,0:T(8,128)(2,1)S(1)}, u32[]{:S(2)}, u32[]{:S(2)}) %collective-permute-start.5) | collective-permute-done | bytes 540704 | tf_op jit(solution)/shard_map/ppermute | solution.py:222
  33.7 0.0 collective-permute-done.1.refs_1_
  33.7 0.6 collective-permute-start.7
  34.3 1.4 %compact_rows.5 = (bf16[1,48,4224]{2,1,0:T(8,128)(2,1)S(1)}, bf16[1,48,4224]{2,1,0:T(8,128)(2,1)S(1)}, bf16[2,48,4224]{2,1,0:T(8,128)(2,1)S(1)}) custom-call(s32[4]{0:T(128)S(1)} %pad_add_fusion.targets, bf16[64,4224]{1,0:T(8,128)(2,1)S(1)} %collective-permute-done.3.refs_0_, bf16[64,4224]{1,0:T(8,128)(2,1)S(1)} %collective-permute-done.4.refs_1_), custom_call_target="tpu_custom_call" | custom-call | flops 1 | bytes 1 | tf_op jit(solution)/shard_map/compact_rows/pallas_call | solution.py:103
  35.8 0.1 collective-permute-start.6
  35.9 0.5 collective-permute-start.12
  36.4 1.5 %collective-permute-start.10 = (bf16[2,48,4224]{2,1,0:T(8,128)(2,1)S(1)}, bf16[2,48,4224]{2,1,0:T(8,128)(2,1)S(1)}, u32[]{:S(2)}, u32[]{:S(2)}) collective-permute-start(bf16[2,48,4224]{2,1,0:T(8,128)(2,1)S(1)} %get-tuple-element.54), channel_id=1, source_target_pairs={{0,2},{1,5},{2,0},{3,7},{4,6},{5,1},{6,4},{7,3},{8,10},{9,13},{10,... | collective-permute-start | bytes 2433032 | tf_op jit(solution)/shard_map/ppermute | solution.py:218
  37.8 6.0 %collective-permute-done.8.refs_0_ = bf16[64,4224]{1,0:T(8,128)(2,1)S(1)} collective-permute-done((bf16[64,4224]{1,0:T(8,128)(2,1)S(1)}, bf16[64,4224]{1,0:T(8,128)(2,1)S(1)}, u32[]{:S(2)}, u32[]{:S(2)}) %collective-permute-start.8) | collective-permute-done | bytes 540704 | tf_op jit(solution)/shard_map/ppermute | solution.py:222
  43.8 3.4 %collective-permute-done.7.refs_1_ = bf16[64,4224]{1,0:T(8,128)(2,1)S(1)} collective-permute-done((bf16[64,4224]{1,0:T(8,128)(2,1)S(1)}, bf16[64,4224]{1,0:T(8,128)(2,1)S(1)}, u32[]{:S(2)}, u32[]{:S(2)}) %collective-permute-start.7) | collective-permute-done | bytes 540704 | tf_op jit(solution)/shard_map/ppermute | solution.py:218
  47.2 1.4 %compact_rows.6 = (bf16[1,48,4224]{2,1,0:T(8,128)(2,1)S(1)}, bf16[1,48,4224]{2,1,0:T(8,128)(2,1)S(1)}, bf16[2,48,4224]{2,1,0:T(8,128)(2,1)S(1)}) custom-call(s32[4]{0:T(128)S(1)} %pad_add_fusion.targets, bf16[64,4224]{1,0:T(8,128)(2,1)S(1)} %collective-permute-done.5.refs_0_, bf16[64,4224]{1,0:T(8,128)(2,1)S(1)} %collective-permute-done.7.refs_1_), custom_call_target="tpu_custom_call" | custom-call | flops 1 | bytes 1 | tf_op jit(solution)/shard_map/compact_rows/pallas_call | solution.py:103
  48.6 0.1 collective-permute-start.9
  48.7 0.0 copy-start
  48.7 2.1 %collective-permute-start.15 = (bf16[2,48,4224]{2,1,0:T(8,128)(2,1)S(1)}, bf16[2,48,4224]{2,1,0:T(8,128)(2,1)S(1)}, u32[]{:S(2)}, u32[]{:S(2)}) collective-permute-start(bf16[2,48,4224]{2,1,0:T(8,128)(2,1)S(1)} %get-tuple-element.67), channel_id=1, source_target_pairs={{0,2},{1,5},{2,0},{3,7},{4,6},{5,1},{6,4},{7,3},{8,10},{9,13},{10,... | collective-permute-start | bytes 2433032 | tf_op jit(solution)/shard_map/ppermute | solution.py:218
  50.8 5.8 %hold_weights.1 = (bf16[4096,1024]{1,0:T(8,128)(2,1)S(1)}, bf16[4096,1024]{1,0:T(8,128)(2,1)S(1)}) custom-call(bf16[1,4096,1024]{2,1,0:T(8,128)(2,1)} %gate_w.1, bf16[1,4096,1024]{2,1,0:T(8,128)(2,1)} %up_w.1), custom_call_target="tpu_custom_call" | custom-call | flops 1 | bytes 1 | tf_op jit(solution)/shard_map/hold_weights/pallas_call | solution.py:128
  56.6 0.0 collective-permute-done.12.refs_3_
  56.7 4.0 %sketch_rows.4.refs_9_ = f32[32,1024]{1,0:T(8,128)S(1)} custom-call(s32[1]{0:T(128)} %bitcast.expert, bf16[1,48,4224]{2,1,0:T(8,128)(2,1)S(1)} %get-tuple-element.56.refs_0_, bf16[1,48,4224]{2,1,0:T(8,128)(2,1)S(1)} %collective-permute-done.1.refs_1_, bf16[2,48,4224]{2,1,0:T(8,128)(2,1)S(1)} %collective-permute-done.2.refs_2_, ...), custom_call_target="tpu_custom_call" | custom-call | flops 1 | bytes 1 | tf_op jit(solution)/shard_map/sketch_rows/pallas_call | solution.py:193
  60.7 0.0 collective-permute-done.10.refs_4_
  60.7 1.7 %collective-permute-done.11.refs_1_ = bf16[64,4224]{1,0:T(8,128)(2,1)S(1)} collective-permute-done((bf16[64,4224]{1,0:T(8,128)(2,1)S(1)}, bf16[64,4224]{1,0:T(8,128)(2,1)S(1)}, u32[]{:S(2)}, u32[]{:S(2)}) %collective-permute-start.11) | collective-permute-done | bytes 540704 | tf_op jit(solution)/shard_map/ppermute | solution.py:218
  62.4 1.4 %compact_rows.7 = (bf16[1,48,4224]{2,1,0:T(8,128)(2,1)S(1)}, bf16[1,48,4224]{2,1,0:T(8,128)(2,1)S(1)}, bf16[2,48,4224]{2,1,0:T(8,128)(2,1)S(1)}) custom-call(s32[4]{0:T(128)S(1)} %pad_add_fusion.targets, bf16[64,4224]{1,0:T(8,128)(2,1)S(1)} %collective-permute-done.8.refs_0_, bf16[64,4224]{1,0:T(8,128)(2,1)S(1)} %collective-permute-done.11.refs_1_), custom_call_target="tpu_custom_call" | custom-call | flops 1 | bytes 1 | tf_op jit(solution)/shard_map/compact_rows/pallas_call | solution.py:103
  63.9 0.1 collective-permute-start.14
  63.9 0.5 collective-permute-start.17
  64.4 0.0 collective-permute-done.15.refs_2_
  64.4 1.2 %collective-permute-done.14.refs_1_ = bf16[1,48,4224]{2,1,0:T(8,128)(2,1)S(1)} collective-permute-done((bf16[1,48,4224]{2,1,0:T(8,128)(2,1)S(1)}, bf16[1,48,4224]{2,1,0:T(8,128)(2,1)S(1)}, u32[]{:S(2)}, u32[]{:S(2)}) %collective-permute-start.14) | collective-permute-done | bytes 405536 | tf_op jit(solution)/shard_map/ppermute | solution.py:218
  65.7 0.5 collective-permute-start.16
  66.1 0.5 collective-permute-start.13
  66.7 0.1 collective-permute-done.17.refs_5_
  66.8 5.9 %sketch_rows.5.refs_7_ = f32[32,1024]{1,0:T(8,128)S(1)} custom-call(s32[1]{0:T(128)} %bitcast.expert, bf16[1,48,4224]{2,1,0:T(8,128)(2,1)S(1)} %get-tuple-element.71.refs_0_, bf16[1,48,4224]{2,1,0:T(8,128)(2,1)S(1)} %collective-permute-done.6.refs_1_, bf16[1,48,4224]{2,1,0:T(8,128)(2,1)S(1)} %get-tuple-element.73.refs_2_, ...), custom_call_target="tpu_custom_call" | custom-call | flops 1 | bytes 1 | tf_op jit(solution)/shard_map/sketch_rows/pallas_call | solution.py:193
  72.7 0.0 collective-permute-done.16.refs_3_
  72.7 4.2 %sketch_rows.6.refs_5_ = f32[32,1024]{1,0:T(8,128)S(1)} custom-call(s32[1]{0:T(128)} %bitcast.expert, bf16[1,48,4224]{2,1,0:T(8,128)(2,1)S(1)} %get-tuple-element.68.refs_0_, bf16[1,48,4224]{2,1,0:T(8,128)(2,1)S(1)} %collective-permute-done.14.refs_1_, bf16[2,48,4224]{2,1,0:T(8,128)(2,1)S(1)} %collective-permute-done.15.refs_2_, ...), custom_call_target="tpu_custom_call" | custom-call | flops 1 | bytes 1 | tf_op jit(solution)/shard_map/sketch_rows/pallas_call | solution.py:193
  76.9 1.5 %collective-permute-done.13.refs_0_ = bf16[2,48,4224]{2,1,0:T(8,128)(2,1)S(1)} collective-permute-done((bf16[2,48,4224]{2,1,0:T(8,128)(2,1)S(1)}, bf16[2,48,4224]{2,1,0:T(8,128)(2,1)S(1)}, u32[]{:S(2)}, u32[]{:S(2)}) %collective-permute-start.13) | collective-permute-done | bytes 811040 | tf_op jit(solution)/shard_map/ppermute | solution.py:218
  78.4 0.0 collective-permute-start.18
  78.4 2.3 %collective-permute-done.18.refs_1_ = bf16[2,48,4224]{2,1,0:T(8,128)(2,1)S(1)} collective-permute-done((bf16[2,48,4224]{2,1,0:T(8,128)(2,1)S(1)}, bf16[2,48,4224]{2,1,0:T(8,128)(2,1)S(1)}, u32[]{:S(2)}, u32[]{:S(2)}) %collective-permute-start.18) | collective-permute-done | bytes 811040 | tf_op jit(solution)/shard_map/ppermute | solution.py:218
  80.7 3.3 %sketch_rows.7 = f32[32,1024]{1,0:T(8,128)S(1)} custom-call(s32[1]{0:T(128)} %bitcast.expert, bf16[2,48,4224]{2,1,0:T(8,128)(2,1)S(1)} %collective-permute-done.13.refs_0_, bf16[2,48,4224]{2,1,0:T(8,128)(2,1)S(1)} %collective-permute-done.18.refs_1_, bf16[4096,1024]{1,0:T(8,128)(2,1)S(1)} %get-tuple-element.59.refs_4_.refs_6_.refs_2_, ...), custom_call_target="tpu_custom_call" | custom-call | flops 1 | bytes 1 | tf_op jit(solution)/shard_map/sketch_rows/pallas_call | solution.py:193
  84.0 0.1 copy.10
  84.1 12.7 %all_to_all.9 = f32[32,1,1024]{2,1,0:T(1,128)S(1)} all-to-all(f32[32,1,1024]{2,1,0:T(1,128)S(1)} %copy.10), channel_id=1, replica_groups=mesh['expert'=4,'dp'=8] {'expert','dp'}, dimensions={0} | all-to-all | bytes 262144 | tf_op jit(solution)/shard_map/all_to_all | solution.py:279
  96.9 0.7 copy.11
  (7 shorter events, 0.0 us)
Async XLA Ops:
  1.8 10.4 %collective-permute-start = (bf16[64,4224]{1,0:T(8,128)(2,1)S(1)}, bf16[64,4224]{1,0:T(8,128)(2,1)S(1)}, u32[]{:S(2)}, u32[]{:S(2)}) collective-permute-start(bf16[64,4224]{1,0:T(8,128)(2,1)S(1)} %extend_rows.1.refs_0_), channel_id=1, source_target_pairs={{0,4},{1,3},{2,6},{3,1},{4,0},{5,7},{6,2},{7,5},{8,12},{9,11},{10,... | collective-permute-start | bytes 1622024 | tf_op jit(solution)/shard_map/ppermute | solution.py:218
  4.8 16.4 %collective-permute-start.3 = (bf16[64,4224]{1,0:T(8,128)(2,1)S(1)}, bf16[64,4224]{1,0:T(8,128)(2,1)S(1)}, u32[]{:S(2)}, u32[]{:S(2)}) collective-permute-start(bf16[64,4224]{1,0:T(8,128)(2,1)S(1)} %extend_rows.1.refs_0_), channel_id=1, source_target_pairs={{8,0},{9,1},{10,2},{11,3},{12,4},{13,5},{14,6},{15,7},{16,8},{17,9... | collective-permute-start | bytes 1622024 | tf_op jit(solution)/shard_map/ppermute | solution.py:222
  13.6 20.1 %collective-permute-start.2 = (bf16[2,48,4224]{2,1,0:T(8,128)(2,1)S(1)}, bf16[2,48,4224]{2,1,0:T(8,128)(2,1)S(1)}, u32[]{:S(2)}, u32[]{:S(2)}) collective-permute-start(bf16[2,48,4224]{2,1,0:T(8,128)(2,1)S(1)} %get-tuple-element.44), channel_id=1, source_target_pairs={{0,2},{1,5},{2,0},{3,7},{4,6},{5,1},{6,4},{7,3},{8,10},{9,13},{10,... | collective-permute-start | bytes 2433032 | tf_op jit(solution)/shard_map/ppermute | solution.py:218
  15.7 18.0 %collective-permute-start.5 = (bf16[64,4224]{1,0:T(8,128)(2,1)S(1)}, bf16[64,4224]{1,0:T(8,128)(2,1)S(1)}, u32[]{:S(2)}, u32[]{:S(2)}) collective-permute-start(bf16[64,4224]{1,0:T(8,128)(2,1)S(1)} %extend_rows.1.refs_0_), channel_id=1, source_target_pairs={{24,0},{25,1},{26,2},{27,3},{28,4},{29,5},{30,6},{31,7},{0,8},{1,9... | collective-permute-start | bytes 1622024 | tf_op jit(solution)/shard_map/ppermute | solution.py:222
  21.2 12.5 %collective-permute-start.4 = (bf16[64,4224]{1,0:T(8,128)(2,1)S(1)}, bf16[64,4224]{1,0:T(8,128)(2,1)S(1)}, u32[]{:S(2)}, u32[]{:S(2)}) collective-permute-start(bf16[64,4224]{1,0:T(8,128)(2,1)S(1)} %collective-permute-done.3.refs_0_), channel_id=1, source_target_pairs={{0,4},{1,3},{2,6},{3,1},{4,0},{5,7},{6,2},{7,5},{8,12},{9,11},{10,... | collective-permute-start | bytes 1622024 | tf_op jit(solution)/shard_map/ppermute | solution.py:218
  21.6 12.1 %collective-permute-start.1 = (bf16[1,48,4224]{2,1,0:T(8,128)(2,1)S(1)}, bf16[1,48,4224]{2,1,0:T(8,128)(2,1)S(1)}, u32[]{:S(2)}, u32[]{:S(2)}) collective-permute-start(bf16[1,48,4224]{2,1,0:T(8,128)(2,1)S(1)} %get-tuple-element.43), channel_id=1, source_target_pairs={{0,1},{1,0},{2,3},{3,2},{4,5},{5,4},{6,7},{7,6},{8,9},{9,8},{10,11... | collective-permute-start | bytes 1216520 | tf_op jit(solution)/shard_map/ppermute | solution.py:218
  21.6 22.2 %collective-permute-start.8 = (bf16[64,4224]{1,0:T(8,128)(2,1)S(1)}, bf16[64,4224]{1,0:T(8,128)(2,1)S(1)}, u32[]{:S(2)}, u32[]{:S(2)}) collective-permute-start(bf16[64,4224]{1,0:T(8,128)(2,1)S(1)} %collective-permute-done.3.refs_0_), channel_id=1, source_target_pairs={{8,0},{9,1},{10,2},{11,3},{12,4},{13,5},{14,6},{15,7},{16,8},{17,9... | collective-permute-start | bytes 1622024 | tf_op jit(solution)/shard_map/ppermute | solution.py:222
  33.7 13.5 %collective-permute-start.7 = (bf16[64,4224]{1,0:T(8,128)(2,1)S(1)}, bf16[64,4224]{1,0:T(8,128)(2,1)S(1)}, u32[]{:S(2)}, u32[]{:S(2)}) collective-permute-start(bf16[64,4224]{1,0:T(8,128)(2,1)S(1)} %collective-permute-done.5.refs_0_), channel_id=1, source_target_pairs={{0,4},{1,3},{2,6},{3,1},{4,0},{5,7},{6,2},{7,5},{8,12},{9,11},{10,... | collective-permute-start | bytes 1622024 | tf_op jit(solution)/shard_map/ppermute | solution.py:218
  35.8 8.0 %collective-permute-start.6 = (bf16[1,48,4224]{2,1,0:T(8,128)(2,1)S(1)}, bf16[1,48,4224]{2,1,0:T(8,128)(2,1)S(1)}, u32[]{:S(2)}, u32[]{:S(2)}) collective-permute-start(bf16[1,48,4224]{2,1,0:T(8,128)(2,1)S(1)} %get-tuple-element.48), channel_id=1, source_target_pairs={{0,1},{1,0},{2,3},{3,2},{4,5},{5,4},{6,7},{7,6},{8,9},{9,8},{10,11... | collective-permute-start | bytes 1216520 | tf_op jit(solution)/shard_map/ppermute | solution.py:218
  35.9 20.8 %collective-permute-start.12 = (bf16[2,48,4224]{2,1,0:T(8,128)(2,1)S(1)}, bf16[2,48,4224]{2,1,0:T(8,128)(2,1)S(1)}, u32[]{:S(2)}, u32[]{:S(2)}) collective-permute-start(bf16[2,48,4224]{2,1,0:T(8,128)(2,1)S(1)} %collective-permute-done.2.refs_2_), channel_id=1, source_target_pairs={{0,1},{1,0},{2,3},{3,2},{4,5},{5,4},{6,7},{7,6},{8,9},{9,8},{10,11... | collective-permute-start | bytes 2433032 | tf_op jit(solution)/shard_map/ppermute | solution.py:218
  36.4 24.4 %collective-permute-start.10 = (bf16[2,48,4224]{2,1,0:T(8,128)(2,1)S(1)}, bf16[2,48,4224]{2,1,0:T(8,128)(2,1)S(1)}, u32[]{:S(2)}, u32[]{:S(2)}) collective-permute-start(bf16[2,48,4224]{2,1,0:T(8,128)(2,1)S(1)} %get-tuple-element.54), channel_id=1, source_target_pairs={{0,2},{1,5},{2,0},{3,7},{4,6},{5,1},{6,4},{7,3},{8,10},{9,13},{10,... | collective-permute-start | bytes 2433032 | tf_op jit(solution)/shard_map/ppermute | solution.py:218
  47.2 15.2 %collective-permute-start.11 = (bf16[64,4224]{1,0:T(8,128)(2,1)S(1)}, bf16[64,4224]{1,0:T(8,128)(2,1)S(1)}, u32[]{:S(2)}, u32[]{:S(2)}) collective-permute-start(bf16[64,4224]{1,0:T(8,128)(2,1)S(1)} %collective-permute-done.8.refs_0_), channel_id=1, source_target_pairs={{0,4},{1,3},{2,6},{3,1},{4,0},{5,7},{6,2},{7,5},{8,12},{9,11},{10,... | collective-permute-start | bytes 1622024 | tf_op jit(solution)/shard_map/ppermute | solution.py:218
  48.6 12.1 %collective-permute-start.9 = (bf16[1,48,4224]{2,1,0:T(8,128)(2,1)S(1)}, bf16[1,48,4224]{2,1,0:T(8,128)(2,1)S(1)}, u32[]{:S(2)}, u32[]{:S(2)}) collective-permute-start(bf16[1,48,4224]{2,1,0:T(8,128)(2,1)S(1)} %get-tuple-element.53), channel_id=1, source_target_pairs={{0,1},{1,0},{2,3},{3,2},{4,5},{5,4},{6,7},{7,6},{8,9},{9,8},{10,11... | collective-permute-start | bytes 1216520 | tf_op jit(solution)/shard_map/ppermute | solution.py:218
  48.7 7.9 %copy-start = (bf16[1024,32]{0,1:T(8,128)(2,1)S(1)}, bf16[1024,32]{0,1:T(8,128)(2,1)}, u32[]{:S(2)}) copy-start(bf16[1024,32]{0,1:T(8,128)(2,1)} %param.16) | copy-start | bytes 196612
  48.7 15.7 %collective-permute-start.15 = (bf16[2,48,4224]{2,1,0:T(8,128)(2,1)S(1)}, bf16[2,48,4224]{2,1,0:T(8,128)(2,1)S(1)}, u32[]{:S(2)}, u32[]{:S(2)}) collective-permute-start(bf16[2,48,4224]{2,1,0:T(8,128)(2,1)S(1)} %get-tuple-element.67), channel_id=1, source_target_pairs={{0,2},{1,5},{2,0},{3,7},{4,6},{5,1},{6,4},{7,3},{8,10},{9,13},{10,... | collective-permute-start | bytes 2433032 | tf_op jit(solution)/shard_map/ppermute | solution.py:218
  63.9 1.8 %collective-permute-start.14 = (bf16[1,48,4224]{2,1,0:T(8,128)(2,1)S(1)}, bf16[1,48,4224]{2,1,0:T(8,128)(2,1)S(1)}, u32[]{:S(2)}, u32[]{:S(2)}) collective-permute-start(bf16[1,48,4224]{2,1,0:T(8,128)(2,1)S(1)} %get-tuple-element.66), channel_id=1, source_target_pairs={{0,1},{1,0},{2,3},{3,2},{4,5},{5,4},{6,7},{7,6},{8,9},{9,8},{10,11... | collective-permute-start | bytes 1216520 | tf_op jit(solution)/shard_map/ppermute | solution.py:218
  63.9 2.9 %collective-permute-start.17 = (bf16[2,48,4224]{2,1,0:T(8,128)(2,1)S(1)}, bf16[2,48,4224]{2,1,0:T(8,128)(2,1)S(1)}, u32[]{:S(2)}, u32[]{:S(2)}) collective-permute-start(bf16[2,48,4224]{2,1,0:T(8,128)(2,1)S(1)} %collective-permute-done.10.refs_4_), channel_id=1, source_target_pairs={{0,1},{1,0},{2,3},{3,2},{4,5},{5,4},{6,7},{7,6},{8,9},{9,8},{10,11... | collective-permute-start | bytes 2433032 | tf_op jit(solution)/shard_map/ppermute | solution.py:218
  65.7 7.0 %collective-permute-start.16 = (bf16[2,48,4224]{2,1,0:T(8,128)(2,1)S(1)}, bf16[2,48,4224]{2,1,0:T(8,128)(2,1)S(1)}, u32[]{:S(2)}, u32[]{:S(2)}) collective-permute-start(bf16[2,48,4224]{2,1,0:T(8,128)(2,1)S(1)} %collective-permute-done.15.refs_2_), channel_id=1, source_target_pairs={{0,1},{1,0},{2,3},{3,2},{4,5},{5,4},{6,7},{7,6},{8,9},{9,8},{10,11... | collective-permute-start | bytes 2433032 | tf_op jit(solution)/shard_map/ppermute | solution.py:218
  66.1 12.3 %collective-permute-start.13 = (bf16[2,48,4224]{2,1,0:T(8,128)(2,1)S(1)}, bf16[2,48,4224]{2,1,0:T(8,128)(2,1)S(1)}, u32[]{:S(2)}, u32[]{:S(2)}) collective-permute-start(bf16[2,48,4224]{2,1,0:T(8,128)(2,1)S(1)} %get-tuple-element.64), channel_id=1, source_target_pairs={{0,2},{1,5},{2,0},{3,7},{4,6},{5,1},{6,4},{7,3},{8,10},{9,13},{10,... | collective-permute-start | bytes 2433032 | tf_op jit(solution)/shard_map/ppermute | solution.py:218
  78.4 2.3 %collective-permute-start.18 = (bf16[2,48,4224]{2,1,0:T(8,128)(2,1)S(1)}, bf16[2,48,4224]{2,1,0:T(8,128)(2,1)S(1)}, u32[]{:S(2)}, u32[]{:S(2)}) collective-permute-start(bf16[2,48,4224]{2,1,0:T(8,128)(2,1)S(1)} %collective-permute-done.13.refs_0_), channel_id=1, source_target_pairs={{0,1},{1,0},{2,3},{3,2},{4,5},{5,4},{6,7},{7,6},{8,9},{9,8},{10,11... | collective-permute-start | bytes 2433032 | tf_op jit(solution)/shard_map/ppermute | solution.py:218

commit v5 on v4

--- a/solution.py
+++ b/solution.py
@@ -63,8 +63,9 @@
     )(*[pltpu.with_memory_space_constraint(o, pltpu.HBM) for o in operands])
 
 
-def compact_kernel(capacity, top, rank, targets, *refs):
-    sources, outs = refs[:-3], refs[-3:]
+def compact_kernel(spots, capacity, top, rank, targets, after, *refs):
+    parts = 1 + spots[-1][0]
+    sources, outs = refs[:-parts], refs[-parts:]
     count = len(sources)
     rows, total = sources[0].shape
     width = total - LANES
@@ -92,27 +93,28 @@
     for at in range(0, total, step):
         end = min(at + step, total)
         found = dot(pick, jnp.concatenate([s[:, at:end] for s in sources], axis=0))
-        for q in range(4):
+        for q, (out, lead) in enumerate(spots):
             part = found[q * picked : (q + 1) * picked].astype(jnp.bfloat16)
-            outs[min(q, 2)][max(q - 2, 0), :, at:end] = part
-
-
-def compact(sources, targets, capacity, top, rank):
-    body = functools.partial(compact_kernel, capacity, top, rank)
+            outs[out][lead, :, at:end] = part
+
+
+def compact(sources, targets, after, leads, capacity, top, rank):
+    spots = tuple((i, lead) for i, n in enumerate(leads) for lead in range(n))
+    body = functools.partial(compact_kernel, spots, capacity, top, rank)
     rows, width = len(sources) * capacity, sources[0].shape[1]
     return pl.pallas_call(
         body,
-        out_shape=[jax.ShapeDtypeStruct((n, rows, width), jnp.bfloat16) for n in (1, 1, 2)],
-        in_specs=[pl.BlockSpec(memory_space=pltpu.SMEM)]
+        out_shape=[jax.ShapeDtypeStruct((n, rows, width), jnp.bfloat16) for n in leads],
+        in_specs=[pl.BlockSpec(memory_space=pltpu.SMEM)] * 2
         + [pl.BlockSpec(memory_space=pltpu.VMEM)] * len(sources),
-        out_specs=[pl.BlockSpec(memory_space=pltpu.VMEM)] * 3,
+        out_specs=[pl.BlockSpec(memory_space=pltpu.VMEM)] * len(leads),
         compiler_params=pltpu.CompilerParams(vmem_limit_bytes=8 * MIB),
         cost_estimate=LIGHT,
         name="compact_rows",
-    )(targets, *sources)
-
-
-def hold_kernel(gate_w, up_w, gate_out, up_out, sems):
+    )(targets, after, *sources)
+
+
+def hold_kernel(gate_w, up_w, gate_out, up_out, done, sems):
     copies = [
         pltpu.make_async_copy(gate_w.at[0], gate_out, sems.at[0]),
         pltpu.make_async_copy(up_w.at[0], up_out, sems.at[1]),
@@ -121,15 +123,17 @@
         copy.start()
     for copy in copies:
         copy.wait()
+    done[0] = 0
 
 
 def hold(w_gate, w_up):
     shape = w_gate.shape[1:]
     return pl.pallas_call(
         hold_kernel,
-        out_shape=[pltpu.VMEM(shape, jnp.bfloat16)] * 2,
+        out_shape=[pltpu.VMEM(shape, jnp.bfloat16)] * 2 + [jax.ShapeDtypeStruct((1,), jnp.int32)],
         in_specs=[pl.BlockSpec(memory_space=pltpu.HBM)] * 2,
-        out_specs=[pl.BlockSpec(memory_space=pltpu.VMEM)] * 2,
+        out_specs=[pl.BlockSpec(memory_space=pltpu.VMEM)] * 2
+        + [pl.BlockSpec(memory_space=pltpu.SMEM)],
         scratch_shapes=[pltpu.SemaphoreType.DMA((2,))],
         compiler_params=pltpu.CompilerParams(vmem_limit_bytes=2 * MIB),
         cost_estimate=LIGHT,
@@ -232,13 +236,13 @@
     shared = [[b for b in bits if b != bits[core]] for core in (0, 1)]
     side = jnp.where(me & 1 == 0, bits[0], bits[1]).astype(jnp.int32)
     targets = jnp.stack([me, me ^ 1, me ^ side, me ^ side ^ 1])
-    weights = hold(w_gate, w_up)
+    *weights, held = hold(w_gate, w_up)
     total = jnp.zeros((devices, rank * rank), jnp.float32)
-    own = me.reshape(1)
+    own_id = me.reshape(1)
     args = (capacity, top, rank)
 
     def sketch_of(total, pieces):
-        return sketch(pieces, own, weights, proj_hidden.T, total, top, rank)
+        return sketch(pieces, own_id, weights, proj_hidden.T, total, top, rank)
 
     def gather(slot):
         sources = [slot]
@@ -246,36 +250,49 @@
             sources += [swap(s, hops) for s in sources]
         return sources
 
-    def spread(sources):
-        own, other, further = compact(sources, targets, *args)
+    def spread(sources, after=own_id):
+        own, other, further = compact(sources, targets, after, (1, 1, 2), *args)
         return [own, swap(other, (1, 1))], swap(further, bits)
+
+    def spread_apart(sources):
+        own, other, same, crossed = compact(sources, targets, own_id, (1, 1, 1, 1), *args)
+        return [own, swap(other, (1, 1))], [swap(same, bits), swap(crossed, [b ^ 1 for b in bits])]
 
     def near(*pairs):
         return [[(array, 0, 0)] for pair in pairs for array in pair]
 
-    def far(*arrays):
-        return [
-            [piece] for a in arrays for piece in ((a, 0, 0), (swap(a, (1, 1)), 1, 0))
-        ]
+    def across_core(array):
+        return [array, swap(array, (1, 1))]
+
+    def far(*pairs):
+        return [[piece] for a, b in pairs for piece in ((a, 0, 0), (b, 1, 0))]
 
     tied = lax.optimization_barrier
     near_now, far_now = spread(gather(slots[0]))
     near_kept, far_kept, far_now = [], [far_now], None
     for j in range(1, groups):
         sources, coming = gather(slots[j]), slots[j + 1 : j + 2]
-        group = (near_now, far_kept, sources, coming, [total] if far_kept else [])
+        if j == groups - 1:
+            total = sketch_of(total, near(near_kept, near_now) + far(*map(across_core, far_old)))
+            near_kept, near_now = [], []
+        group = (near_now, far_kept, sources, coming, [total] if j != 2 else [held])
         near_now, far_kept, sources, slots[j + 1 : j + 2], kept = tied(group)
         near_kept += near_now
-        near_now, far_next = spread(sources)
-        if far_kept:
-            total = sketch_of(kept[0], near(near_kept) + far(*far_kept))
-            near_kept = []
-        far_kept = [] if far_now is None else [far_now]
+        if j == groups - 1:
+            near_now, far_next = spread_apart(sources)
+            total = kept[0]
+        else:
+            near_now, far_next = spread(sources, kept[0] if j == 2 else own_id)
+        if j == 1:
+            far_old = far_kept
+            far_kept = []
+        elif far_now is not None:
+            far_kept = far_kept + [far_now]
         far_now = far_next
     near_now, far_kept = tied((near_now, far_kept))
-    total = sketch_of(total, near(near_kept, near_now) + far(*far_kept))
+    total = sketch_of(total, near(near_kept, near_now) + far(*map(across_core, far_kept)))
     far_now, total = tied((far_now, total))
-    total = sketch_of(total, far(far_now))
+    total = sketch_of(total, near(far_now))
     owned = lax.all_to_all(total, AXES, split_axis=0, concat_axis=0, tiled=True)
     return owned[None]
 

time: 97.7 us -> 94.9 us (0.971)
  waiting for transfers between devices: 31.7 us -> 27.6 us
    ppermute x3, waiting for transfers between devices: 17.8 us -> 11.8 us  [turn(): lax.ppermute(value, AXES, [(a * planes + b, c * planes + d) for (a, b), (...]
    ppermute x16, waiting for transfers between devices: 13.9 us -> 15.8 us  [swap(): lax.ppermute(value, AXES, [(i, i ^ hops[i & 1]) for i in range(devices)])]
    pallas_call x4 -> x3, Pallas kernels: 17.4 us -> 16.8 us  [sketch(): pl.pallas_call(body, out_shape=jax.ShapeDtypeStruct(total.shape, jnp.floa...]
  transfers between devices with their start and end apart: 19 -> 19, of which waited for: 10 -> 9; matrix products, arithmetic and copies ran while one was open for 0% -> 0% of each run, Pallas kernels for 26% -> 28%
where the time goes in v5:
time: 94.9 us; the launch traced here: 94.8 us
  Pallas kernels  31.3 us (33%)
  waiting for transfers between devices  27.6 us (29%)
  starting transfers between devices  22.1 us (23%)
  blocking collectives  12.7 us (13%)
    pallas_call x3, Pallas kernels, sketch(): pl.pallas_call(body, out_shape=jax.ShapeDtypeStruct(total.shape, jnp.floa...  16.8 us
    ppermute x16, waiting for transfers between devices, swap(): lax.ppermute(value, AXES, [(i, i ^ hops[i & 1]) for i in range(devices)])  15.8 us
    all_to_all x1, blocking collectives, on_device(): owned = lax.all_to_all(total, AXES, split_axis=0, concat_axis=0, tiled=True)  12.7 us
    ppermute x16, starting transfers between devices, swap(): lax.ppermute(value, AXES, [(i, i ^ hops[i & 1]) for i in range(devices)])  12.7 us
    ppermute x3, waiting for transfers between devices, turn(): lax.ppermute(value, AXES, [(a * planes + b, c * planes + d) for (a, b), (...  11.8 us
    ppermute x3, starting transfers between devices, turn(): lax.ppermute(value, AXES, [(a * planes + b, c * planes + d) for (a, b), (...  9.47 us
    pallas_call x4, Pallas kernels, compact(): pl.pallas_call(body, out_shape=[jax.ShapeDtypeStruct((n, rows, width), jn...  6.37 us
    pallas_call x1, Pallas kernels, hold(): pl.pallas_call(hold_kernel, out_shape=[pltpu.VMEM(shape, jnp.bfloat16)] *...  6.3 us
  transfers between devices with their start and end apart: 19, of which 9 were waited for; matrix products, arithmetic and copies ran while one was open for 0% of the time, Pallas kernels for 28%

profile of v5, /device:TPU:0, one launch (start us, length us, event | category | flops | bytes accessed | tf_op | source)
XLA Modules:
  0.0 94.8 jit_solution(17261339707317242893)
XLA Ops:
  0.0 1.8 %extend_rows.1.refs_0_ = bf16[64,4224]{1,0:T(8,128)(2,1)S(1)} custom-call(bf16[64,4096]{1,0:T(8,128)(2,1)} %tokens.1, bf16[64,4096]{1,0:T(8,128)(2,1)} %refs_0_.1, bf16[32,4096]{1,0:T(8,128)(2,1)} %bitcast.16, s32[8,64]{1,0:T(8,128)} %bitcast.17, bf16[8,64]{1,0:T(8,128)(2,1)} %bitcast.18, s32[1,64]{1,0:T(1,128)} %bitcast.19), custom_call_target="tpu_custom_call" | custom-call | tf_op jit(solution)/shard_map/extend_rows/pallas_call | solution.py:54
  1.8 3.0 %collective-permute-start = (bf16[64,4224]{1,0:T(8,128)(2,1)S(1)}, bf16[64,4224]{1,0:T(8,128)(2,1)S(1)}, u32[]{:S(2)}, u32[]{:S(2)}) collective-permute-start(bf16[64,4224]{1,0:T(8,128)(2,1)S(1)} %extend_rows.1.refs_0_), channel_id=1, source_target_pairs={{0,4},{1,3},{2,6},{3,1},{4,0},{5,7},{6,2},{7,5},{8,12},{9,11},{10,... | collective-permute-start | bytes 1622024 | tf_op jit(solution)/shard_map/ppermute | solution.py:222
  4.8 3.6 %collective-permute-start.3 = (bf16[64,4224]{1,0:T(8,128)(2,1)S(1)}, bf16[64,4224]{1,0:T(8,128)(2,1)S(1)}, u32[]{:S(2)}, u32[]{:S(2)}) collective-permute-start(bf16[64,4224]{1,0:T(8,128)(2,1)S(1)} %extend_rows.1.refs_0_), channel_id=1, source_target_pairs={{8,0},{9,1},{10,2},{11,3},{12,4},{13,5},{14,6},{15,7},{16,8},{17,9... | collective-permute-start | bytes 1622024 | tf_op jit(solution)/shard_map/ppermute | solution.py:226
  8.5 0.1 pad_add_fusion.targets
  8.5 3.6 %collective-permute-done.refs_1_ = bf16[64,4224]{1,0:T(8,128)(2,1)S(1)} collective-permute-done((bf16[64,4224]{1,0:T(8,128)(2,1)S(1)}, bf16[64,4224]{1,0:T(8,128)(2,1)S(1)}, u32[]{:S(2)}, u32[]{:S(2)}) %collective-permute-start) | collective-permute-done | bytes 540704 | tf_op jit(solution)/shard_map/ppermute | solution.py:222
  12.2 1.4 %compact_rows.4 = (bf16[1,48,4224]{2,1,0:T(8,128)(2,1)S(1)}, bf16[1,48,4224]{2,1,0:T(8,128)(2,1)S(1)}, bf16[2,48,4224]{2,1,0:T(8,128)(2,1)S(1)}) custom-call(s32[4]{0:T(128)S(1)} %pad_add_fusion.targets, s32[1]{0:T(128)} %bitcast.after.expert, bf16[64,4224]{1,0:T(8,128)(2,1)S(1)} %extend_rows.1.refs_0_, bf16[64,4224]{1,0:T(8,128)(2,1)S(1)} %collective-permute-done.refs_1_), custom_call_target="tpu_custom_call" | custom-call | flops 1 | bytes 1 | tf_op jit(solution)/shard_map/compact_rows/pallas_call | solution.py:105
  13.6 2.1 %collective-permute-start.2 = (bf16[2,48,4224]{2,1,0:T(8,128)(2,1)S(1)}, bf16[2,48,4224]{2,1,0:T(8,128)(2,1)S(1)}, u32[]{:S(2)}, u32[]{:S(2)}) collective-permute-start(bf16[2,48,4224]{2,1,0:T(8,128)(2,1)S(1)} %get-tuple-element.46), channel_id=1, source_target_pairs={{0,2},{1,5},{2,0},{3,7},{4,6},{5,1},{6,4},{7,3},{8,10},{9,13},{10,... | collective-permute-start | bytes 2433032 | tf_op jit(solution)/shard_map/ppermute | solution.py:222
  15.7 1.6 %collective-permute-start.5 = (bf16[64,4224]{1,0:T(8,128)(2,1)S(1)}, bf16[64,4224]{1,0:T(8,128)(2,1)S(1)}, u32[]{:S(2)}, u32[]{:S(2)}) collective-permute-start(bf16[64,4224]{1,0:T(8,128)(2,1)S(1)} %extend_rows.1.refs_0_), channel_id=1, source_target_pairs={{24,0},{25,1},{26,2},{27,3},{28,4},{29,5},{30,6},{31,7},{0,8},{1,9... | collective-permute-start | bytes 1622024 | tf_op jit(solution)/shard_map/ppermute | solution.py:226
  17.3 4.0 %collective-permute-done.3.refs_0_ = bf16[64,4224]{1,0:T(8,128)(2,1)S(1)} collective-permute-done((bf16[64,4224]{1,0:T(8,128)(2,1)S(1)}, bf16[64,4224]{1,0:T(8,128)(2,1)S(1)}, u32[]{:S(2)}, u32[]{:S(2)}) %collective-permute-start.3) | collective-permute-done | bytes 540704 | tf_op jit(solution)/shard_map/ppermute | solution.py:226
  21.2 0.4 collective-permute-start.4
  21.6 0.0 collective-permute-start.1
  21.6 4.3 %collective-permute-start.9 = (bf16[64,4224]{1,0:T(8,128)(2,1)S(1)}, bf16[64,4224]{1,0:T(8,128)(2,1)S(1)}, u32[]{:S(2)}, u32[]{:S(2)}) collective-permute-start(bf16[64,4224]{1,0:T(8,128)(2,1)S(1)} %collective-permute-done.3.refs_0_), channel_id=1, source_target_pairs={{8,0},{9,1},{10,2},{11,3},{12,4},{13,5},{14,6},{15,7},{16,8},{17,9... | collective-permute-start | bytes 1622024 | tf_op jit(solution)/shard_map/ppermute | solution.py:226
  25.9 7.8 %collective-permute-done.5.refs_0_ = bf16[64,4224]{1,0:T(8,128)(2,1)S(1)} collective-permute-done((bf16[64,4224]{1,0:T(8,128)(2,1)S(1)}, bf16[64,4224]{1,0:T(8,128)(2,1)S(1)}, u32[]{:S(2)}, u32[]{:S(2)}) %collective-permute-start.5) | collective-permute-done | bytes 540704 | tf_op jit(solution)/shard_map/ppermute | solution.py:226
  33.7 0.0 collective-permute-done.1.refs_1_
  33.7 0.0 collective-permute-done.4.refs_1_
  33.7 0.6 collective-permute-start.8
  34.3 1.4 %compact_rows.5 = (bf16[1,48,4224]{2,1,0:T(8,128)(2,1)S(1)}, bf16[1,48,4224]{2,1,0:T(8,128)(2,1)S(1)}, bf16[2,48,4224]{2,1,0:T(8,128)(2,1)S(1)}) custom-call(s32[4]{0:T(128)S(1)} %pad_add_fusion.targets, s32[1]{0:T(128)} %bitcast.after.expert, bf16[64,4224]{1,0:T(8,128)(2,1)S(1)} %collective-permute-done.3.refs_0_, ...), custom_call_target="tpu_custom_call" | custom-call | flops 1 | bytes 1 | tf_op jit(solution)/shard_map/compact_rows/pallas_call | solution.py:105
  35.8 0.1 collective-permute-start.7
  35.9 0.5 collective-permute-start.12
  36.4 1.5 %collective-permute-start.6 = (bf16[2,48,4224]{2,1,0:T(8,128)(2,1)S(1)}, bf16[2,48,4224]{2,1,0:T(8,128)(2,1)S(1)}, u32[]{:S(2)}, u32[]{:S(2)}) collective-permute-start(bf16[2,48,4224]{2,1,0:T(8,128)(2,1)S(1)} %get-tuple-element.49), channel_id=1, source_target_pairs={{0,2},{1,5},{2,0},{3,7},{4,6},{5,1},{6,4},{7,3},{8,10},{9,13},{10,... | collective-permute-start | bytes 2433032 | tf_op jit(solution)/shard_map/ppermute | solution.py:222
  37.8 6.3 %hold_weights.1 = (bf16[4096,1024]{1,0:T(8,128)(2,1)S(1)}, bf16[4096,1024]{1,0:T(8,128)(2,1)S(1)}, s32[1]{0:T(128)}) custom-call(bf16[1,4096,1024]{2,1,0:T(8,128)(2,1)} %gate_w.1, bf16[1,4096,1024]{2,1,0:T(8,128)(2,1)} %up_w.1), custom_call_target="tpu_custom_call" | custom-call | flops 1 | bytes 1 | tf_op jit(solution)/shard_map/hold_weights/pallas_call | solution.py:131
  44.1 0.0 collective-permute-done.9.refs_0_
  44.2 3.0 %collective-permute-done.8.refs_1_ = bf16[64,4224]{1,0:T(8,128)(2,1)S(1)} collective-permute-done((bf16[64,4224]{1,0:T(8,128)(2,1)S(1)}, bf16[64,4224]{1,0:T(8,128)(2,1)S(1)}, u32[]{:S(2)}, u32[]{:S(2)}) %collective-permute-start.8) | collective-permute-done | bytes 540704 | tf_op jit(solution)/shard_map/ppermute | solution.py:222
  47.2 2.1 %compact_rows.6 = (bf16[1,48,4224]{2,1,0:T(8,128)(2,1)S(1)}, bf16[1,48,4224]{2,1,0:T(8,128)(2,1)S(1)}, bf16[2,48,4224]{2,1,0:T(8,128)(2,1)S(1)}) custom-call(s32[4]{0:T(128)S(1)} %pad_add_fusion.targets, s32[1]{0:T(128)} %get-tuple-element.59.after, bf16[64,4224]{1,0:T(8,128)(2,1)S(1)} %collective-permute-done.5.refs_0_, ...), custom_call_target="tpu_custom_call" | custom-call | flops 1 | bytes 1 | tf_op jit(solution)/shard_map/compact_rows/pallas_call | solution.py:105
  49.3 0.1 collective-permute-start.11
  49.4 2.1 %collective-permute-start.16 = (bf16[2,48,4224]{2,1,0:T(8,128)(2,1)S(1)}, bf16[2,48,4224]{2,1,0:T(8,128)(2,1)S(1)}, u32[]{:S(2)}, u32[]{:S(2)}) collective-permute-start(bf16[2,48,4224]{2,1,0:T(8,128)(2,1)S(1)} %get-tuple-element.74), channel_id=1, source_target_pairs={{0,2},{1,5},{2,0},{3,7},{4,6},{5,1},{6,4},{7,3},{8,10},{9,13},{10,... | collective-permute-start | bytes 2433032 | tf_op jit(solution)/shard_map/ppermute | solution.py:222
  51.4 0.0 collective-permute-done.12.refs_7_
  51.4 0.0 collective-permute-done.11.refs_5_
  51.5 7.7 %sketch_rows.3.refs_9_ = f32[32,1024]{1,0:T(8,128)S(1)} custom-call(s32[1]{0:T(128)} %bitcast.after.expert, bf16[1,48,4224]{2,1,0:T(8,128)(2,1)S(1)} %get-tuple-element.55.refs_0_, bf16[1,48,4224]{2,1,0:T(8,128)(2,1)S(1)} %collective-permute-done.1.refs_1_, bf16[1,48,4224]{2,1,0:T(8,128)(2,1)S(1)} %get-tuple-element.57.refs_2_, ...), custom_call_target="tpu_custom_call" | custom-call | flops 1 | bytes 1 | tf_op jit(solution)/shard_map/sketch_rows/pallas_call | solution.py:197
  59.1 0.0 collective-permute-done.6.refs_2_
  59.2 3.3 %collective-permute-done.10.refs_1_ = bf16[64,4224]{1,0:T(8,128)(2,1)S(1)} collective-permute-done((bf16[64,4224]{1,0:T(8,128)(2,1)S(1)}, bf16[64,4224]{1,0:T(8,128)(2,1)S(1)}, u32[]{:S(2)}, u32[]{:S(2)}) %collective-permute-start.10) | collective-permute-done | bytes 540704 | tf_op jit(solution)/shard_map/ppermute | solution.py:222
  62.4 1.4 %compact_rows.7 = (bf16[1,48,4224]{2,1,0:T(8,128)(2,1)S(1)}, bf16[1,48,4224]{2,1,0:T(8,128)(2,1)S(1)}, bf16[1,48,4224]{2,1,0:T(8,128)(2,1)S(1)}, bf16[1,48,4224]{2,1,0:T(8,128)(2,1)S(1)}) custom-call(s32[4]{0:T(128)S(1)} %pad_add_fusion.targets, s32[1]{0:T(128)} %bitcast.after.expert, bf16[64,4224]{1,0:T(8,128)(2,1)S(1)} %collective-permute-done.9.refs_0_, ...), custom_call_target="tpu_custom_call" | custom-call | flops 1 | bytes 1 | tf_op jit(solution)/shard_map/compact_rows/pallas_call | solution.py:105
  63.9 0.1 collective-permute-start.15
  63.9 0.0 collective-permute-done.16.refs_4_
  63.9 1.7 %collective-permute-done.15.refs_1_ = bf16[1,48,4224]{2,1,0:T(8,128)(2,1)S(1)} collective-permute-done((bf16[1,48,4224]{2,1,0:T(8,128)(2,1)S(1)}, bf16[1,48,4224]{2,1,0:T(8,128)(2,1)S(1)}, u32[]{:S(2)}, u32[]{:S(2)}) %collective-permute-start.15) | collective-permute-done | bytes 405536 | tf_op jit(solution)/shard_map/ppermute | solution.py:222
  65.7 0.5 collective-permute-start.17
  66.1 0.0 collective-permute-start.18
  66.2 0.5 collective-permute-start.13
  66.7 1.3 %collective-permute-start.14 = (bf16[1,48,4224]{2,1,0:T(8,128)(2,1)S(1)}, bf16[1,48,4224]{2,1,0:T(8,128)(2,1)S(1)}, u32[]{:S(2)}, u32[]{:S(2)}) collective-permute-start(bf16[1,48,4224]{2,1,0:T(8,128)(2,1)S(1)} %get-tuple-element.70), channel_id=1, source_target_pairs={{0,3},{1,4},{2,1},{3,6},{4,7},{5,0},{6,5},{7,2},{8,11},{9,12},{10,... | collective-permute-start | bytes 1216520 | tf_op jit(solution)/shard_map/ppermute | solution.py:222
  68.0 0.1 collective-permute-done.17.refs_3_
  68.1 1.2 %collective-permute-done.18.refs_5_ = bf16[2,48,4224]{2,1,0:T(8,128)(2,1)S(1)} collective-permute-done((bf16[2,48,4224]{2,1,0:T(8,128)(2,1)S(1)}, bf16[2,48,4224]{2,1,0:T(8,128)(2,1)S(1)}, u32[]{:S(2)}, u32[]{:S(2)}) %collective-permute-start.18) | collective-permute-done | bytes 811040 | tf_op jit(solution)/shard_map/ppermute | solution.py:222
  69.3 5.9 %sketch_rows.4.refs_5_ = f32[32,1024]{1,0:T(8,128)S(1)} custom-call(s32[1]{0:T(128)} %bitcast.after.expert, bf16[1,48,4224]{2,1,0:T(8,128)(2,1)S(1)} %get-tuple-element.75.refs_0_, bf16[1,48,4224]{2,1,0:T(8,128)(2,1)S(1)} %collective-permute-done.15.refs_1_, bf16[2,48,4224]{2,1,0:T(8,128)(2,1)S(1)} %collective-permute-done.6.refs_2_, ...), custom_call_target="tpu_custom_call" | custom-call | flops 1 | bytes 1 | tf_op jit(solution)/shard_map/sketch_rows/pallas_call | solution.py:197
  75.1 0.0 collective-permute-done.13.refs_0_
  75.1 2.8 %collective-permute-done.14.refs_1_ = bf16[1,48,4224]{2,1,0:T(8,128)(2,1)S(1)} collective-permute-done((bf16[1,48,4224]{2,1,0:T(8,128)(2,1)S(1)}, bf16[1,48,4224]{2,1,0:T(8,128)(2,1)S(1)}, u32[]{:S(2)}, u32[]{:S(2)}) %collective-permute-start.14) | collective-permute-done | bytes 405536 | tf_op jit(solution)/shard_map/ppermute | solution.py:222
  77.9 3.3 %sketch_rows.5 = f32[32,1024]{1,0:T(8,128)S(1)} custom-call(s32[1]{0:T(128)} %bitcast.after.expert, bf16[1,48,4224]{2,1,0:T(8,128)(2,1)S(1)} %collective-permute-done.13.refs_0_, bf16[1,48,4224]{2,1,0:T(8,128)(2,1)S(1)} %collective-permute-done.14.refs_1_, bf16[4096,1024]{1,0:T(8,128)(2,1)S(1)} %get-tuple-element.65.refs_8_.refs_6_.refs_2_, ...), custom_call_target="tpu_custom_call" | custom-call | flops 1 | bytes 1 | tf_op jit(solution)/shard_map/sketch_rows/pallas_call | solution.py:197
  81.2 0.1 copy.10
  81.4 12.7 %all_to_all.9 = f32[32,1,1024]{2,1,0:T(1,128)S(1)} all-to-all(f32[32,1,1024]{2,1,0:T(1,128)S(1)} %copy.10), channel_id=1, replica_groups=mesh['expert'=4,'dp'=8] {'expert','dp'}, dimensions={0} | all-to-all | bytes 262144 | tf_op jit(solution)/shard_map/all_to_all | solution.py:296
  94.1 0.7 copy.11
  (6 shorter events, 0.0 us)
Async XLA Ops:
  1.8 10.4 %collective-permute-start = (bf16[64,4224]{1,0:T(8,128)(2,1)S(1)}, bf16[64,4224]{1,0:T(8,128)(2,1)S(1)}, u32[]{:S(2)}, u32[]{:S(2)}) collective-permute-start(bf16[64,4224]{1,0:T(8,128)(2,1)S(1)} %extend_rows.1.refs_0_), channel_id=1, source_target_pairs={{0,4},{1,3},{2,6},{3,1},{4,0},{5,7},{6,2},{7,5},{8,12},{9,11},{10,... | collective-permute-start | bytes 1622024 | tf_op jit(solution)/shard_map/ppermute | solution.py:222
  4.8 16.4 %collective-permute-start.3 = (bf16[64,4224]{1,0:T(8,128)(2,1)S(1)}, bf16[64,4224]{1,0:T(8,128)(2,1)S(1)}, u32[]{:S(2)}, u32[]{:S(2)}) collective-permute-start(bf16[64,4224]{1,0:T(8,128)(2,1)S(1)} %extend_rows.1.refs_0_), channel_id=1, source_target_pairs={{8,0},{9,1},{10,2},{11,3},{12,4},{13,5},{14,6},{15,7},{16,8},{17,9... | collective-permute-start | bytes 1622024 | tf_op jit(solution)/shard_map/ppermute | solution.py:226
  13.6 20.1 %collective-permute-start.2 = (bf16[2,48,4224]{2,1,0:T(8,128)(2,1)S(1)}, bf16[2,48,4224]{2,1,0:T(8,128)(2,1)S(1)}, u32[]{:S(2)}, u32[]{:S(2)}) collective-permute-start(bf16[2,48,4224]{2,1,0:T(8,128)(2,1)S(1)} %get-tuple-element.46), channel_id=1, source_target_pairs={{0,2},{1,5},{2,0},{3,7},{4,6},{5,1},{6,4},{7,3},{8,10},{9,13},{10,... | collective-permute-start | bytes 2433032 | tf_op jit(solution)/shard_map/ppermute | solution.py:222
  15.7 18.0 %collective-permute-start.5 = (bf16[64,4224]{1,0:T(8,128)(2,1)S(1)}, bf16[64,4224]{1,0:T(8,128)(2,1)S(1)}, u32[]{:S(2)}, u32[]{:S(2)}) collective-permute-start(bf16[64,4224]{1,0:T(8,128)(2,1)S(1)} %extend_rows.1.refs_0_), channel_id=1, source_target_pairs={{24,0},{25,1},{26,2},{27,3},{28,4},{29,5},{30,6},{31,7},{0,8},{1,9... | collective-permute-start | bytes 1622024 | tf_op jit(solution)/shard_map/ppermute | solution.py:226
  21.2 12.5 %collective-permute-start.4 = (bf16[64,4224]{1,0:T(8,128)(2,1)S(1)}, bf16[64,4224]{1,0:T(8,128)(2,1)S(1)}, u32[]{:S(2)}, u32[]{:S(2)}) collective-permute-start(bf16[64,4224]{1,0:T(8,128)(2,1)S(1)} %collective-permute-done.3.refs_0_), channel_id=1, source_target_pairs={{0,4},{1,3},{2,6},{3,1},{4,0},{5,7},{6,2},{7,5},{8,12},{9,11},{10,... | collective-permute-start | bytes 1622024 | tf_op jit(solution)/shard_map/ppermute | solution.py:222
  21.6 12.1 %collective-permute-start.1 = (bf16[1,48,4224]{2,1,0:T(8,128)(2,1)S(1)}, bf16[1,48,4224]{2,1,0:T(8,128)(2,1)S(1)}, u32[]{:S(2)}, u32[]{:S(2)}) collective-permute-start(bf16[1,48,4224]{2,1,0:T(8,128)(2,1)S(1)} %get-tuple-element.45), channel_id=1, source_target_pairs={{0,1},{1,0},{2,3},{3,2},{4,5},{5,4},{6,7},{7,6},{8,9},{9,8},{10,11... | collective-permute-start | bytes 1216520 | tf_op jit(solution)/shard_map/ppermute | solution.py:222
  21.6 22.6 %collective-permute-start.9 = (bf16[64,4224]{1,0:T(8,128)(2,1)S(1)}, bf16[64,4224]{1,0:T(8,128)(2,1)S(1)}, u32[]{:S(2)}, u32[]{:S(2)}) collective-permute-start(bf16[64,4224]{1,0:T(8,128)(2,1)S(1)} %collective-permute-done.3.refs_0_), channel_id=1, source_target_pairs={{8,0},{9,1},{10,2},{11,3},{12,4},{13,5},{14,6},{15,7},{16,8},{17,9... | collective-permute-start | bytes 1622024 | tf_op jit(solution)/shard_map/ppermute | solution.py:226
  33.7 13.5 %collective-permute-start.8 = (bf16[64,4224]{1,0:T(8,128)(2,1)S(1)}, bf16[64,4224]{1,0:T(8,128)(2,1)S(1)}, u32[]{:S(2)}, u32[]{:S(2)}) collective-permute-start(bf16[64,4224]{1,0:T(8,128)(2,1)S(1)} %collective-permute-done.5.refs_0_), channel_id=1, source_target_pairs={{0,4},{1,3},{2,6},{3,1},{4,0},{5,7},{6,2},{7,5},{8,12},{9,11},{10,... | collective-permute-start | bytes 1622024 | tf_op jit(solution)/shard_map/ppermute | solution.py:222
  35.8 8.4 %collective-permute-start.7 = (bf16[1,48,4224]{2,1,0:T(8,128)(2,1)S(1)}, bf16[1,48,4224]{2,1,0:T(8,128)(2,1)S(1)}, u32[]{:S(2)}, u32[]{:S(2)}) collective-permute-start(bf16[1,48,4224]{2,1,0:T(8,128)(2,1)S(1)} %get-tuple-element.51), channel_id=1, source_target_pairs={{0,1},{1,0},{2,3},{3,2},{4,5},{5,4},{6,7},{7,6},{8,9},{9,8},{10,11... | collective-permute-start | bytes 1216520 | tf_op jit(solution)/shard_map/ppermute | solution.py:222
  35.9 15.6 %collective-permute-start.12 = (bf16[2,48,4224]{2,1,0:T(8,128)(2,1)S(1)}, bf16[2,48,4224]{2,1,0:T(8,128)(2,1)S(1)}, u32[]{:S(2)}, u32[]{:S(2)}) collective-permute-start(bf16[2,48,4224]{2,1,0:T(8,128)(2,1)S(1)} %collective-permute-done.2.refs_6_), channel_id=1, source_target_pairs={{0,1},{1,0},{2,3},{3,2},{4,5},{5,4},{6,7},{7,6},{8,9},{9,8},{10,11... | collective-permute-start | bytes 2433032 | tf_op jit(solution)/shard_map/ppermute | solution.py:222
  36.4 15.1 %copy-start = (bf16[1024,32]{0,1:T(8,128)(2,1)S(1)}, bf16[1024,32]{0,1:T(8,128)(2,1)}, u32[]{:S(2)}) copy-start(bf16[1024,32]{0,1:T(8,128)(2,1)} %param.16) | copy-start | bytes 196612
  36.4 22.8 %collective-permute-start.6 = (bf16[2,48,4224]{2,1,0:T(8,128)(2,1)S(1)}, bf16[2,48,4224]{2,1,0:T(8,128)(2,1)S(1)}, u32[]{:S(2)}, u32[]{:S(2)}) collective-permute-start(bf16[2,48,4224]{2,1,0:T(8,128)(2,1)S(1)} %get-tuple-element.49), channel_id=1, source_target_pairs={{0,2},{1,5},{2,0},{3,7},{4,6},{5,1},{6,4},{7,3},{8,10},{9,13},{10,... | collective-permute-start | bytes 2433032 | tf_op jit(solution)/shard_map/ppermute | solution.py:222
  47.2 15.2 %collective-permute-start.10 = (bf16[64,4224]{1,0:T(8,128)(2,1)S(1)}, bf16[64,4224]{1,0:T(8,128)(2,1)S(1)}, u32[]{:S(2)}, u32[]{:S(2)}) collective-permute-start(bf16[64,4224]{1,0:T(8,128)(2,1)S(1)} %collective-permute-done.9.refs_0_), channel_id=1, source_target_pairs={{0,4},{1,3},{2,6},{3,1},{4,0},{5,7},{6,2},{7,5},{8,12},{9,11},{10,... | collective-permute-start | bytes 1622024 | tf_op jit(solution)/shard_map/ppermute | solution.py:222
  49.3 2.2 %collective-permute-start.11 = (bf16[1,48,4224]{2,1,0:T(8,128)(2,1)S(1)}, bf16[1,48,4224]{2,1,0:T(8,128)(2,1)S(1)}, u32[]{:S(2)}, u32[]{:S(2)}) collective-permute-start(bf16[1,48,4224]{2,1,0:T(8,128)(2,1)S(1)} %get-tuple-element.63), channel_id=1, source_target_pairs={{0,1},{1,0},{2,3},{3,2},{4,5},{5,4},{6,7},{7,6},{8,9},{9,8},{10,11... | collective-permute-start | bytes 1216520 | tf_op jit(solution)/shard_map/ppermute | solution.py:222
  49.4 14.6 %collective-permute-start.16 = (bf16[2,48,4224]{2,1,0:T(8,128)(2,1)S(1)}, bf16[2,48,4224]{2,1,0:T(8,128)(2,1)S(1)}, u32[]{:S(2)}, u32[]{:S(2)}) collective-permute-start(bf16[2,48,4224]{2,1,0:T(8,128)(2,1)S(1)} %get-tuple-element.74), channel_id=1, source_target_pairs={{0,2},{1,5},{2,0},{3,7},{4,6},{5,1},{6,4},{7,3},{8,10},{9,13},{10,... | collective-permute-start | bytes 2433032 | tf_op jit(solution)/shard_map/ppermute | solution.py:222
  63.9 1.8 %collective-permute-start.15 = (bf16[1,48,4224]{2,1,0:T(8,128)(2,1)S(1)}, bf16[1,48,4224]{2,1,0:T(8,128)(2,1)S(1)}, u32[]{:S(2)}, u32[]{:S(2)}) collective-permute-start(bf16[1,48,4224]{2,1,0:T(8,128)(2,1)S(1)} %get-tuple-element.72), channel_id=1, source_target_pairs={{0,1},{1,0},{2,3},{3,2},{4,5},{5,4},{6,7},{7,6},{8,9},{9,8},{10,11... | collective-permute-start | bytes 1216520 | tf_op jit(solution)/shard_map/ppermute | solution.py:222
  65.7 2.4 %collective-permute-start.17 = (bf16[2,48,4224]{2,1,0:T(8,128)(2,1)S(1)}, bf16[2,48,4224]{2,1,0:T(8,128)(2,1)S(1)}, u32[]{:S(2)}, u32[]{:S(2)}) collective-permute-start(bf16[2,48,4224]{2,1,0:T(8,128)(2,1)S(1)} %collective-permute-done.6.refs_2_), channel_id=1, source_target_pairs={{0,1},{1,0},{2,3},{3,2},{4,5},{5,4},{6,7},{7,6},{8,9},{9,8},{10,11... | collective-permute-start | bytes 2433032 | tf_op jit(solution)/shard_map/ppermute | solution.py:222
  66.1 3.1 %collective-permute-start.18 = (bf16[2,48,4224]{2,1,0:T(8,128)(2,1)S(1)}, bf16[2,48,4224]{2,1,0:T(8,128)(2,1)S(1)}, u32[]{:S(2)}, u32[]{:S(2)}) collective-permute-start(bf16[2,48,4224]{2,1,0:T(8,128)(2,1)S(1)} %collective-permute-done.16.refs_4_), channel_id=1, source_target_pairs={{0,1},{1,0},{2,3},{3,2},{4,5},{5,4},{6,7},{7,6},{8,9},{9,8},{10,11... | collective-permute-start | bytes 2433032 | tf_op jit(solution)/shard_map/ppermute | solution.py:222
  66.2 8.9 %collective-permute-start.13 = (bf16[1,48,4224]{2,1,0:T(8,128)(2,1)S(1)}, bf16[1,48,4224]{2,1,0:T(8,128)(2,1)S(1)}, u32[]{:S(2)}, u32[]{:S(2)}) collective-permute-start(bf16[1,48,4224]{2,1,0:T(8,128)(2,1)S(1)} %get-tuple-element.69), channel_id=1, source_target_pairs={{0,2},{1,5},{2,0},{3,7},{4,6},{5,1},{6,4},{7,3},{8,10},{9,13},{10,... | collective-permute-start | bytes 1216520 | tf_op jit(solution)/shard_map/ppermute | solution.py:222
  66.7 11.2 %collective-permute-start.14 = (bf16[1,48,4224]{2,1,0:T(8,128)(2,1)S(1)}, bf16[1,48,4224]{2,1,0:T(8,128)(2,1)S(1)}, u32[]{:S(2)}, u32[]{:S(2)}) collective-permute-start(bf16[1,48,4224]{2,1,0:T(8,128)(2,1)S(1)} %get-tuple-element.70), channel_id=1, source_target_pairs={{0,3},{1,4},{2,1},{3,6},{4,7},{5,0},{6,5},{7,2},{8,11},{9,12},{10,... | collective-permute-start | bytes 1216520 | tf_op jit(solution)/shard_map/ppermute | solution.py:222

commit v6 on v5

--- a/solution.py
+++ b/solution.py
@@ -143,7 +143,7 @@
 
 def sketch_kernel(spots, top, rank, docs_total, expert, *refs):
     pieces = refs[: len(spots)]
-    gate_w, up_w, proj, total_in, total_out, rows_at, hidden_at = refs[len(spots) :]
+    gate_w, up_w, proj, total_in, total_out, rows_at, hidden_at, *folded = refs[len(spots) :]
     width, hidden = gate_w.shape
     for ref, (lead, row, column) in zip(pieces, spots):
         r, c = ref.shape[1:]
@@ -181,10 +181,15 @@
     total = total_in[...]
     for part in (high, low):
         total += across(table, part, (0, 0))
-    total_out[...] = total
-
-
-def sketch(pieces, expert, weights, proj, total, top, rank):
+    if not folded:
+        total_out[...] = total
+        return
+    for at in range(0, rank * rank, LANES):
+        folded[0][:, at // LANES, :] = total[:, at : at + LANES]
+    total_out[...] = folded[0][...].astype(total_out.dtype)
+
+
+def sketch(pieces, expert, weights, proj, total, top, rank, fold=False):
     width, hidden = weights[0].shape
     rows, arrays, spots = 0, [], []
     for beside in pieces:
@@ -194,15 +199,20 @@
         rows += -(-beside[0][0].shape[1] // 16) * 16
     body = functools.partial(sketch_kernel, tuple(spots), top, rank, total.shape[0])
     vmem = pl.BlockSpec(memory_space=pltpu.VMEM)
+    folded = (total.shape[0], rank * rank // LANES, LANES)
+    result = jax.ShapeDtypeStruct(total.shape, jnp.float32)
+    if fold:
+        result = jax.ShapeDtypeStruct(folded, jnp.bfloat16)
     return pl.pallas_call(
         body,
-        out_shape=jax.ShapeDtypeStruct(total.shape, jnp.float32),
+        out_shape=result,
         in_specs=[pl.BlockSpec(memory_space=pltpu.SMEM)] + [vmem] * (len(arrays) + 4),
         out_specs=vmem,
         scratch_shapes=[
             pltpu.VMEM((rows, width + LANES), jnp.bfloat16),
             pltpu.VMEM((rows, hidden), jnp.bfloat16),
-        ],
+        ]
+        + [pltpu.VMEM(folded, jnp.float32)] * fold,
         compiler_params=pltpu.CompilerParams(vmem_limit_bytes=14 * MIB),
         cost_estimate=LIGHT,
         name="sketch_rows",
@@ -241,8 +251,8 @@
     own_id = me.reshape(1)
     args = (capacity, top, rank)
 
-    def sketch_of(total, pieces):
-        return sketch(pieces, own_id, weights, proj_hidden.T, total, top, rank)
+    def sketch_of(total, pieces, fold=False):
+        return sketch(pieces, own_id, weights, proj_hidden.T, total, top, rank, fold)
 
     def gather(slot):
         sources = [slot]
@@ -292,9 +302,9 @@
     near_now, far_kept = tied((near_now, far_kept))
     total = sketch_of(total, near(near_kept, near_now) + far(*map(across_core, far_kept)))
     far_now, total = tied((far_now, total))
-    total = sketch_of(total, near(far_now))
-    owned = lax.all_to_all(total, AXES, split_axis=0, concat_axis=0, tiled=True)
-    return owned[None]
+    folded = sketch_of(total, near(far_now), True)
+    owned = lax.all_to_all(folded, AXES, split_axis=0, concat_axis=0, tiled=True)
+    return owned.reshape(1, devices, rank * rank).astype(jnp.float32)
 
 
 def solution(mesh):

time: 94.9 us -> 94 us (level)
  no operation moved by 1% of the time
where the time goes in v6:
time: 94 us; the launch traced here: 93.9 us
  Pallas kernels  31.3 us (33%)
  waiting for transfers between devices  27.6 us (29%)
  starting transfers between devices  22.1 us (24%)
  blocking collectives  11.9 us (13%)
    pallas_call x3, Pallas kernels, sketch(): pl.pallas_call(body, out_shape=result, in_specs=[pl.BlockSpec(memory_spac...  16.8 us
    ppermute x16, waiting for transfers between devices, swap(): lax.ppermute(value, AXES, [(i, i ^ hops[i & 1]) for i in range(devices)])  15.8 us
    ppermute x16, starting transfers between devices, swap(): lax.ppermute(value, AXES, [(i, i ^ hops[i & 1]) for i in range(devices)])  12.7 us
    all_to_all x1, blocking collectives, on_device(): lax.all_to_all(folded, AXES, split_axis=0, concat_axis=0, tiled=True)  11.9 us
    ppermute x3, waiting for transfers between devices, turn(): lax.ppermute(value, AXES, [(a * planes + b, c * planes + d) for (a, b), (...  11.8 us
    ppermute x3, starting transfers between devices, turn(): lax.ppermute(value, AXES, [(a * planes + b, c * planes + d) for (a, b), (...  9.47 us
    pallas_call x4, Pallas kernels, compact(): pl.pallas_call(body, out_shape=[jax.ShapeDtypeStruct((n, rows, width), jn...  6.37 us
    pallas_call x1, Pallas kernels, hold(): pl.pallas_call(hold_kernel, out_shape=[pltpu.VMEM(shape, jnp.bfloat16)] *...  6.3 us
  transfers between devices with their start and end apart: 19, of which 9 were waited for; matrix products, arithmetic and copies ran while one was open for 0% of the time, Pallas kernels for 28%

profile of v6, /device:TPU:0, one launch (start us, length us, event | category | flops | bytes accessed | tf_op | source)
XLA Modules:
  0.0 93.9 jit_solution(11698062279518872460)
XLA Ops:
  0.0 1.8 %extend_rows.1.refs_0_ = bf16[64,4224]{1,0:T(8,128)(2,1)S(1)} custom-call(bf16[64,4096]{1,0:T(8,128)(2,1)} %tokens.1, bf16[64,4096]{1,0:T(8,128)(2,1)} %refs_0_.1, bf16[32,4096]{1,0:T(8,128)(2,1)} %bitcast.12, s32[8,64]{1,0:T(8,128)} %bitcast.13, bf16[8,64]{1,0:T(8,128)(2,1)} %bitcast.14, s32[1,64]{1,0:T(1,128)} %bitcast.15), custom_call_target="tpu_custom_call" | custom-call | tf_op jit(solution)/shard_map/extend_rows/pallas_call | solution.py:54
  1.8 3.0 %collective-permute-start = (bf16[64,4224]{1,0:T(8,128)(2,1)S(1)}, bf16[64,4224]{1,0:T(8,128)(2,1)S(1)}, u32[]{:S(2)}, u32[]{:S(2)}) collective-permute-start(bf16[64,4224]{1,0:T(8,128)(2,1)S(1)} %extend_rows.1.refs_0_), channel_id=1, source_target_pairs={{0,4},{1,3},{2,6},{3,1},{4,0},{5,7},{6,2},{7,5},{8,12},{9,11},{10,... | collective-permute-start | bytes 1622024 | tf_op jit(solution)/shard_map/ppermute | solution.py:232
  4.8 3.6 %collective-permute-start.3 = (bf16[64,4224]{1,0:T(8,128)(2,1)S(1)}, bf16[64,4224]{1,0:T(8,128)(2,1)S(1)}, u32[]{:S(2)}, u32[]{:S(2)}) collective-permute-start(bf16[64,4224]{1,0:T(8,128)(2,1)S(1)} %extend_rows.1.refs_0_), channel_id=1, source_target_pairs={{8,0},{9,1},{10,2},{11,3},{12,4},{13,5},{14,6},{15,7},{16,8},{17,9... | collective-permute-start | bytes 1622024 | tf_op jit(solution)/shard_map/ppermute | solution.py:236
  8.5 0.1 pad_add_fusion.targets
  8.5 3.6 %collective-permute-done.refs_1_ = bf16[64,4224]{1,0:T(8,128)(2,1)S(1)} collective-permute-done((bf16[64,4224]{1,0:T(8,128)(2,1)S(1)}, bf16[64,4224]{1,0:T(8,128)(2,1)S(1)}, u32[]{:S(2)}, u32[]{:S(2)}) %collective-permute-start) | collective-permute-done | bytes 540704 | tf_op jit(solution)/shard_map/ppermute | solution.py:232
  12.2 1.4 %compact_rows.4 = (bf16[1,48,4224]{2,1,0:T(8,128)(2,1)S(1)}, bf16[1,48,4224]{2,1,0:T(8,128)(2,1)S(1)}, bf16[2,48,4224]{2,1,0:T(8,128)(2,1)S(1)}) custom-call(s32[4]{0:T(128)S(1)} %pad_add_fusion.targets, s32[1]{0:T(128)} %bitcast.after.expert, bf16[64,4224]{1,0:T(8,128)(2,1)S(1)} %extend_rows.1.refs_0_, bf16[64,4224]{1,0:T(8,128)(2,1)S(1)} %collective-permute-done.refs_1_), custom_call_target="tpu_custom_call" | custom-call | flops 1 | bytes 1 | tf_op jit(solution)/shard_map/compact_rows/pallas_call | solution.py:105
  13.6 2.1 %collective-permute-start.2 = (bf16[2,48,4224]{2,1,0:T(8,128)(2,1)S(1)}, bf16[2,48,4224]{2,1,0:T(8,128)(2,1)S(1)}, u32[]{:S(2)}, u32[]{:S(2)}) collective-permute-start(bf16[2,48,4224]{2,1,0:T(8,128)(2,1)S(1)} %get-tuple-element.46), channel_id=1, source_target_pairs={{0,2},{1,5},{2,0},{3,7},{4,6},{5,1},{6,4},{7,3},{8,10},{9,13},{10,... | collective-permute-start | bytes 2433032 | tf_op jit(solution)/shard_map/ppermute | solution.py:232
  15.7 1.6 %collective-permute-start.5 = (bf16[64,4224]{1,0:T(8,128)(2,1)S(1)}, bf16[64,4224]{1,0:T(8,128)(2,1)S(1)}, u32[]{:S(2)}, u32[]{:S(2)}) collective-permute-start(bf16[64,4224]{1,0:T(8,128)(2,1)S(1)} %extend_rows.1.refs_0_), channel_id=1, source_target_pairs={{24,0},{25,1},{26,2},{27,3},{28,4},{29,5},{30,6},{31,7},{0,8},{1,9... | collective-permute-start | bytes 1622024 | tf_op jit(solution)/shard_map/ppermute | solution.py:236
  17.3 4.0 %collective-permute-done.3.refs_0_ = bf16[64,4224]{1,0:T(8,128)(2,1)S(1)} collective-permute-done((bf16[64,4224]{1,0:T(8,128)(2,1)S(1)}, bf16[64,4224]{1,0:T(8,128)(2,1)S(1)}, u32[]{:S(2)}, u32[]{:S(2)}) %collective-permute-start.3) | collective-permute-done | bytes 540704 | tf_op jit(solution)/shard_map/ppermute | solution.py:236
  21.2 0.4 collective-permute-start.4
  21.6 0.0 collective-permute-start.1
  21.6 4.3 %collective-permute-start.9 = (bf16[64,4224]{1,0:T(8,128)(2,1)S(1)}, bf16[64,4224]{1,0:T(8,128)(2,1)S(1)}, u32[]{:S(2)}, u32[]{:S(2)}) collective-permute-start(bf16[64,4224]{1,0:T(8,128)(2,1)S(1)} %collective-permute-done.3.refs_0_), channel_id=1, source_target_pairs={{8,0},{9,1},{10,2},{11,3},{12,4},{13,5},{14,6},{15,7},{16,8},{17,9... | collective-permute-start | bytes 1622024 | tf_op jit(solution)/shard_map/ppermute | solution.py:236
  25.9 7.8 %collective-permute-done.5.refs_0_ = bf16[64,4224]{1,0:T(8,128)(2,1)S(1)} collective-permute-done((bf16[64,4224]{1,0:T(8,128)(2,1)S(1)}, bf16[64,4224]{1,0:T(8,128)(2,1)S(1)}, u32[]{:S(2)}, u32[]{:S(2)}) %collective-permute-start.5) | collective-permute-done | bytes 540704 | tf_op jit(solution)/shard_map/ppermute | solution.py:236
  33.7 0.0 collective-permute-done.1.refs_1_
  33.7 0.0 collective-permute-done.4.refs_1_
  33.7 0.0 collective-permute-done.2.refs_6_
  33.7 0.6 collective-permute-start.8
  34.3 1.4 %compact_rows.5 = (bf16[1,48,4224]{2,1,0:T(8,128)(2,1)S(1)}, bf16[1,48,4224]{2,1,0:T(8,128)(2,1)S(1)}, bf16[2,48,4224]{2,1,0:T(8,128)(2,1)S(1)}) custom-call(s32[4]{0:T(128)S(1)} %pad_add_fusion.targets, s32[1]{0:T(128)} %bitcast.after.expert, bf16[64,4224]{1,0:T(8,128)(2,1)S(1)} %collective-permute-done.3.refs_0_, ...), custom_call_target="tpu_custom_call" | custom-call | flops 1 | bytes 1 | tf_op jit(solution)/shard_map/compact_rows/pallas_call | solution.py:105
  35.8 0.1 collective-permute-start.7
  35.9 0.5 collective-permute-start.12
  36.4 1.5 %collective-permute-start.6 = (bf16[2,48,4224]{2,1,0:T(8,128)(2,1)S(1)}, bf16[2,48,4224]{2,1,0:T(8,128)(2,1)S(1)}, u32[]{:S(2)}, u32[]{:S(2)}) collective-permute-start(bf16[2,48,4224]{2,1,0:T(8,128)(2,1)S(1)} %get-tuple-element.49), channel_id=1, source_target_pairs={{0,2},{1,5},{2,0},{3,7},{4,6},{5,1},{6,4},{7,3},{8,10},{9,13},{10,... | collective-permute-start | bytes 2433032 | tf_op jit(solution)/shard_map/ppermute | solution.py:232
  37.8 6.3 %hold_weights.1 = (bf16[4096,1024]{1,0:T(8,128)(2,1)S(1)}, bf16[4096,1024]{1,0:T(8,128)(2,1)S(1)}, s32[1]{0:T(128)}) custom-call(bf16[1,4096,1024]{2,1,0:T(8,128)(2,1)} %gate_w.1, bf16[1,4096,1024]{2,1,0:T(8,128)(2,1)} %up_w.1), custom_call_target="tpu_custom_call" | custom-call | flops 1 | bytes 1 | tf_op jit(solution)/shard_map/hold_weights/pallas_call | solution.py:131
  44.1 0.0 collective-permute-done.9.refs_0_
  44.2 3.0 %collective-permute-done.8.refs_1_ = bf16[64,4224]{1,0:T(8,128)(2,1)S(1)} collective-permute-done((bf16[64,4224]{1,0:T(8,128)(2,1)S(1)}, bf16[64,4224]{1,0:T(8,128)(2,1)S(1)}, u32[]{:S(2)}, u32[]{:S(2)}) %collective-permute-start.8) | collective-permute-done | bytes 540704 | tf_op jit(solution)/shard_map/ppermute | solution.py:232
  47.2 2.1 %compact_rows.6 = (bf16[1,48,4224]{2,1,0:T(8,128)(2,1)S(1)}, bf16[1,48,4224]{2,1,0:T(8,128)(2,1)S(1)}, bf16[2,48,4224]{2,1,0:T(8,128)(2,1)S(1)}) custom-call(s32[4]{0:T(128)S(1)} %pad_add_fusion.targets, s32[1]{0:T(128)} %get-tuple-element.59.after, bf16[64,4224]{1,0:T(8,128)(2,1)S(1)} %collective-permute-done.5.refs_0_, ...), custom_call_target="tpu_custom_call" | custom-call | flops 1 | bytes 1 | tf_op jit(solution)/shard_map/compact_rows/pallas_call | solution.py:105
  49.3 0.1 collective-permute-start.11
  49.4 2.1 %collective-permute-start.16 = (bf16[2,48,4224]{2,1,0:T(8,128)(2,1)S(1)}, bf16[2,48,4224]{2,1,0:T(8,128)(2,1)S(1)}, u32[]{:S(2)}, u32[]{:S(2)}) collective-permute-start(bf16[2,48,4224]{2,1,0:T(8,128)(2,1)S(1)} %get-tuple-element.74), channel_id=1, source_target_pairs={{0,2},{1,5},{2,0},{3,7},{4,6},{5,1},{6,4},{7,3},{8,10},{9,13},{10,... | collective-permute-start | bytes 2433032 | tf_op jit(solution)/shard_map/ppermute | solution.py:232
  51.4 0.0 collective-permute-done.12.refs_7_
  51.4 0.0 collective-permute-done.11.refs_5_
  51.5 7.7 %sketch_rows.3.refs_9_ = f32[32,1024]{1,0:T(8,128)S(1)} custom-call(s32[1]{0:T(128)} %bitcast.after.expert, bf16[1,48,4224]{2,1,0:T(8,128)(2,1)S(1)} %get-tuple-element.55.refs_0_, bf16[1,48,4224]{2,1,0:T(8,128)(2,1)S(1)} %collective-permute-done.1.refs_1_, bf16[1,48,4224]{2,1,0:T(8,128)(2,1)S(1)} %get-tuple-element.57.refs_2_, ...), custom_call_target="tpu_custom_call" | custom-call | flops 1 | bytes 1 | tf_op jit(solution)/shard_map/sketch_rows/pallas_call | solution.py:206
  59.1 0.0 collective-permute-done.6.refs_2_
  59.2 3.3 %collective-permute-done.10.refs_1_ = bf16[64,4224]{1,0:T(8,128)(2,1)S(1)} collective-permute-done((bf16[64,4224]{1,0:T(8,128)(2,1)S(1)}, bf16[64,4224]{1,0:T(8,128)(2,1)S(1)}, u32[]{:S(2)}, u32[]{:S(2)}) %collective-permute-start.10) | collective-permute-done | bytes 540704 | tf_op jit(solution)/shard_map/ppermute | solution.py:232
  62.4 1.4 %compact_rows.7 = (bf16[1,48,4224]{2,1,0:T(8,128)(2,1)S(1)}, bf16[1,48,4224]{2,1,0:T(8,128)(2,1)S(1)}, bf16[1,48,4224]{2,1,0:T(8,128)(2,1)S(1)}, bf16[1,48,4224]{2,1,0:T(8,128)(2,1)S(1)}) custom-call(s32[4]{0:T(128)S(1)} %pad_add_fusion.targets, s32[1]{0:T(128)} %bitcast.after.expert, bf16[64,4224]{1,0:T(8,128)(2,1)S(1)} %collective-permute-done.9.refs_0_, ...), custom_call_target="tpu_custom_call" | custom-call | flops 1 | bytes 1 | tf_op jit(solution)/shard_map/compact_rows/pallas_call | solution.py:105
  63.9 0.1 collective-permute-start.15
  63.9 0.0 collective-permute-done.16.refs_4_
  63.9 1.7 %collective-permute-done.15.refs_1_ = bf16[1,48,4224]{2,1,0:T(8,128)(2,1)S(1)} collective-permute-done((bf16[1,48,4224]{2,1,0:T(8,128)(2,1)S(1)}, bf16[1,48,4224]{2,1,0:T(8,128)(2,1)S(1)}, u32[]{:S(2)}, u32[]{:S(2)}) %collective-permute-start.15) | collective-permute-done | bytes 405536 | tf_op jit(solution)/shard_map/ppermute | solution.py:232
  65.7 0.5 collective-permute-start.17
  66.1 0.0 collective-permute-start.18
  66.2 0.5 collective-permute-start.13
  66.7 1.3 %collective-permute-start.14 = (bf16[1,48,4224]{2,1,0:T(8,128)(2,1)S(1)}, bf16[1,48,4224]{2,1,0:T(8,128)(2,1)S(1)}, u32[]{:S(2)}, u32[]{:S(2)}) collective-permute-start(bf16[1,48,4224]{2,1,0:T(8,128)(2,1)S(1)} %get-tuple-element.70), channel_id=1, source_target_pairs={{0,3},{1,4},{2,1},{3,6},{4,7},{5,0},{6,5},{7,2},{8,11},{9,12},{10,... | collective-permute-start | bytes 1216520 | tf_op jit(solution)/shard_map/ppermute | solution.py:232
  68.0 0.1 collective-permute-done.17.refs_3_
  68.1 1.2 %collective-permute-done.18.refs_5_ = bf16[2,48,4224]{2,1,0:T(8,128)(2,1)S(1)} collective-permute-done((bf16[2,48,4224]{2,1,0:T(8,128)(2,1)S(1)}, bf16[2,48,4224]{2,1,0:T(8,128)(2,1)S(1)}, u32[]{:S(2)}, u32[]{:S(2)}) %collective-permute-start.18) | collective-permute-done | bytes 811040 | tf_op jit(solution)/shard_map/ppermute | solution.py:232
  69.3 5.9 %sketch_rows.4.refs_5_ = f32[32,1024]{1,0:T(8,128)S(1)} custom-call(s32[1]{0:T(128)} %bitcast.after.expert, bf16[1,48,4224]{2,1,0:T(8,128)(2,1)S(1)} %get-tuple-element.75.refs_0_, bf16[1,48,4224]{2,1,0:T(8,128)(2,1)S(1)} %collective-permute-done.15.refs_1_, bf16[2,48,4224]{2,1,0:T(8,128)(2,1)S(1)} %collective-permute-done.6.refs_2_, ...), custom_call_target="tpu_custom_call" | custom-call | flops 1 | bytes 1 | tf_op jit(solution)/shard_map/sketch_rows/pallas_call | solution.py:206
  75.1 0.0 collective-permute-done.13.refs_0_
  75.1 2.8 %collective-permute-done.14.refs_1_ = bf16[1,48,4224]{2,1,0:T(8,128)(2,1)S(1)} collective-permute-done((bf16[1,48,4224]{2,1,0:T(8,128)(2,1)S(1)}, bf16[1,48,4224]{2,1,0:T(8,128)(2,1)S(1)}, u32[]{:S(2)}, u32[]{:S(2)}) %collective-permute-start.14) | collective-permute-done | bytes 405536 | tf_op jit(solution)/shard_map/ppermute | solution.py:232
  77.9 3.3 %sketch_rows.5 = bf16[32,8,128]{2,1,0:T(8,128)(2,1)S(1)} custom-call(s32[1]{0:T(128)} %bitcast.after.expert, bf16[1,48,4224]{2,1,0:T(8,128)(2,1)S(1)} %collective-permute-done.13.refs_0_, bf16[1,48,4224]{2,1,0:T(8,128)(2,1)S(1)} %collective-permute-done.14.refs_1_, bf16[4096,1024]{1,0:T(8,128)(2,1)S(1)} %get-tuple-element.65.refs_8_.refs_6_.refs_2_, ...), custom_call_target="tpu_custom_call" | custom-call | flops 1 | bytes 1 | tf_op jit(solution)/shard_map/sketch_rows/pallas_call | solution.py:206
  81.3 11.9 %all_to_all.5 = bf16[32,8,128]{2,1,0:T(8,128)(2,1)S(1)} all-to-all(bf16[32,8,128]{2,1,0:T(8,128)(2,1)S(1)} %sketch_rows.5), channel_id=1, replica_groups=mesh['expert'=4,'dp'=8] {'expert','dp'}, dimensions={0} | all-to-all | bytes 131072 | tf_op jit(solution)/shard_map/all_to_all | solution.py:306
  93.2 0.7 reshape.23
  (5 shorter events, 0.0 us)
Async XLA Ops:
  1.8 10.4 %collective-permute-start = (bf16[64,4224]{1,0:T(8,128)(2,1)S(1)}, bf16[64,4224]{1,0:T(8,128)(2,1)S(1)}, u32[]{:S(2)}, u32[]{:S(2)}) collective-permute-start(bf16[64,4224]{1,0:T(8,128)(2,1)S(1)} %extend_rows.1.refs_0_), channel_id=1, source_target_pairs={{0,4},{1,3},{2,6},{3,1},{4,0},{5,7},{6,2},{7,5},{8,12},{9,11},{10,... | collective-permute-start | bytes 1622024 | tf_op jit(solution)/shard_map/ppermute | solution.py:232
  4.8 16.4 %collective-permute-start.3 = (bf16[64,4224]{1,0:T(8,128)(2,1)S(1)}, bf16[64,4224]{1,0:T(8,128)(2,1)S(1)}, u32[]{:S(2)}, u32[]{:S(2)}) collective-permute-start(bf16[64,4224]{1,0:T(8,128)(2,1)S(1)} %extend_rows.1.refs_0_), channel_id=1, source_target_pairs={{8,0},{9,1},{10,2},{11,3},{12,4},{13,5},{14,6},{15,7},{16,8},{17,9... | collective-permute-start | bytes 1622024 | tf_op jit(solution)/shard_map/ppermute | solution.py:236
  13.6 20.1 %collective-permute-start.2 = (bf16[2,48,4224]{2,1,0:T(8,128)(2,1)S(1)}, bf16[2,48,4224]{2,1,0:T(8,128)(2,1)S(1)}, u32[]{:S(2)}, u32[]{:S(2)}) collective-permute-start(bf16[2,48,4224]{2,1,0:T(8,128)(2,1)S(1)} %get-tuple-element.46), channel_id=1, source_target_pairs={{0,2},{1,5},{2,0},{3,7},{4,6},{5,1},{6,4},{7,3},{8,10},{9,13},{10,... | collective-permute-start | bytes 2433032 | tf_op jit(solution)/shard_map/ppermute | solution.py:232
  15.7 18.0 %collective-permute-start.5 = (bf16[64,4224]{1,0:T(8,128)(2,1)S(1)}, bf16[64,4224]{1,0:T(8,128)(2,1)S(1)}, u32[]{:S(2)}, u32[]{:S(2)}) collective-permute-start(bf16[64,4224]{1,0:T(8,128)(2,1)S(1)} %extend_rows.1.refs_0_), channel_id=1, source_target_pairs={{24,0},{25,1},{26,2},{27,3},{28,4},{29,5},{30,6},{31,7},{0,8},{1,9... | collective-permute-start | bytes 1622024 | tf_op jit(solution)/shard_map/ppermute | solution.py:236
  21.2 12.5 %collective-permute-start.4 = (bf16[64,4224]{1,0:T(8,128)(2,1)S(1)}, bf16[64,4224]{1,0:T(8,128)(2,1)S(1)}, u32[]{:S(2)}, u32[]{:S(2)}) collective-permute-start(bf16[64,4224]{1,0:T(8,128)(2,1)S(1)} %collective-permute-done.3.refs_0_), channel_id=1, source_target_pairs={{0,4},{1,3},{2,6},{3,1},{4,0},{5,7},{6,2},{7,5},{8,12},{9,11},{10,... | collective-permute-start | bytes 1622024 | tf_op jit(solution)/shard_map/ppermute | solution.py:232
  21.6 12.1 %collective-permute-start.1 = (bf16[1,48,4224]{2,1,0:T(8,128)(2,1)S(1)}, bf16[1,48,4224]{2,1,0:T(8,128)(2,1)S(1)}, u32[]{:S(2)}, u32[]{:S(2)}) collective-permute-start(bf16[1,48,4224]{2,1,0:T(8,128)(2,1)S(1)} %get-tuple-element.45), channel_id=1, source_target_pairs={{0,1},{1,0},{2,3},{3,2},{4,5},{5,4},{6,7},{7,6},{8,9},{9,8},{10,11... | collective-permute-start | bytes 1216520 | tf_op jit(solution)/shard_map/ppermute | solution.py:232
  21.6 22.6 %collective-permute-start.9 = (bf16[64,4224]{1,0:T(8,128)(2,1)S(1)}, bf16[64,4224]{1,0:T(8,128)(2,1)S(1)}, u32[]{:S(2)}, u32[]{:S(2)}) collective-permute-start(bf16[64,4224]{1,0:T(8,128)(2,1)S(1)} %collective-permute-done.3.refs_0_), channel_id=1, source_target_pairs={{8,0},{9,1},{10,2},{11,3},{12,4},{13,5},{14,6},{15,7},{16,8},{17,9... | collective-permute-start | bytes 1622024 | tf_op jit(solution)/shard_map/ppermute | solution.py:236
  33.7 13.5 %collective-permute-start.8 = (bf16[64,4224]{1,0:T(8,128)(2,1)S(1)}, bf16[64,4224]{1,0:T(8,128)(2,1)S(1)}, u32[]{:S(2)}, u32[]{:S(2)}) collective-permute-start(bf16[64,4224]{1,0:T(8,128)(2,1)S(1)} %collective-permute-done.5.refs_0_), channel_id=1, source_target_pairs={{0,4},{1,3},{2,6},{3,1},{4,0},{5,7},{6,2},{7,5},{8,12},{9,11},{10,... | collective-permute-start | bytes 1622024 | tf_op jit(solution)/shard_map/ppermute | solution.py:232
  35.8 8.4 %collective-permute-start.7 = (bf16[1,48,4224]{2,1,0:T(8,128)(2,1)S(1)}, bf16[1,48,4224]{2,1,0:T(8,128)(2,1)S(1)}, u32[]{:S(2)}, u32[]{:S(2)}) collective-permute-start(bf16[1,48,4224]{2,1,0:T(8,128)(2,1)S(1)} %get-tuple-element.51), channel_id=1, source_target_pairs={{0,1},{1,0},{2,3},{3,2},{4,5},{5,4},{6,7},{7,6},{8,9},{9,8},{10,11... | collective-permute-start | bytes 1216520 | tf_op jit(solution)/shard_map/ppermute | solution.py:232
  35.9 15.6 %collective-permute-start.12 = (bf16[2,48,4224]{2,1,0:T(8,128)(2,1)S(1)}, bf16[2,48,4224]{2,1,0:T(8,128)(2,1)S(1)}, u32[]{:S(2)}, u32[]{:S(2)}) collective-permute-start(bf16[2,48,4224]{2,1,0:T(8,128)(2,1)S(1)} %collective-permute-done.2.refs_6_), channel_id=1, source_target_pairs={{0,1},{1,0},{2,3},{3,2},{4,5},{5,4},{6,7},{7,6},{8,9},{9,8},{10,11... | collective-permute-start | bytes 2433032 | tf_op jit(solution)/shard_map/ppermute | solution.py:232
  36.4 15.1 %copy-start = (bf16[1024,32]{0,1:T(8,128)(2,1)S(1)}, bf16[1024,32]{0,1:T(8,128)(2,1)}, u32[]{:S(2)}) copy-start(bf16[1024,32]{0,1:T(8,128)(2,1)} %param.16) | copy-start | bytes 196612
  36.4 22.8 %collective-permute-start.6 = (bf16[2,48,4224]{2,1,0:T(8,128)(2,1)S(1)}, bf16[2,48,4224]{2,1,0:T(8,128)(2,1)S(1)}, u32[]{:S(2)}, u32[]{:S(2)}) collective-permute-start(bf16[2,48,4224]{2,1,0:T(8,128)(2,1)S(1)} %get-tuple-element.49), channel_id=1, source_target_pairs={{0,2},{1,5},{2,0},{3,7},{4,6},{5,1},{6,4},{7,3},{8,10},{9,13},{10,... | collective-permute-start | bytes 2433032 | tf_op jit(solution)/shard_map/ppermute | solution.py:232
  47.2 15.2 %collective-permute-start.10 = (bf16[64,4224]{1,0:T(8,128)(2,1)S(1)}, bf16[64,4224]{1,0:T(8,128)(2,1)S(1)}, u32[]{:S(2)}, u32[]{:S(2)}) collective-permute-start(bf16[64,4224]{1,0:T(8,128)(2,1)S(1)} %collective-permute-done.9.refs_0_), channel_id=1, source_target_pairs={{0,4},{1,3},{2,6},{3,1},{4,0},{5,7},{6,2},{7,5},{8,12},{9,11},{10,... | collective-permute-start | bytes 1622024 | tf_op jit(solution)/shard_map/ppermute | solution.py:232
  49.3 2.2 %collective-permute-start.11 = (bf16[1,48,4224]{2,1,0:T(8,128)(2,1)S(1)}, bf16[1,48,4224]{2,1,0:T(8,128)(2,1)S(1)}, u32[]{:S(2)}, u32[]{:S(2)}) collective-permute-start(bf16[1,48,4224]{2,1,0:T(8,128)(2,1)S(1)} %get-tuple-element.63), channel_id=1, source_target_pairs={{0,1},{1,0},{2,3},{3,2},{4,5},{5,4},{6,7},{7,6},{8,9},{9,8},{10,11... | collective-permute-start | bytes 1216520 | tf_op jit(solution)/shard_map/ppermute | solution.py:232
  49.4 14.6 %collective-permute-start.16 = (bf16[2,48,4224]{2,1,0:T(8,128)(2,1)S(1)}, bf16[2,48,4224]{2,1,0:T(8,128)(2,1)S(1)}, u32[]{:S(2)}, u32[]{:S(2)}) collective-permute-start(bf16[2,48,4224]{2,1,0:T(8,128)(2,1)S(1)} %get-tuple-element.74), channel_id=1, source_target_pairs={{0,2},{1,5},{2,0},{3,7},{4,6},{5,1},{6,4},{7,3},{8,10},{9,13},{10,... | collective-permute-start | bytes 2433032 | tf_op jit(solution)/shard_map/ppermute | solution.py:232
  63.9 1.8 %collective-permute-start.15 = (bf16[1,48,4224]{2,1,0:T(8,128)(2,1)S(1)}, bf16[1,48,4224]{2,1,0:T(8,128)(2,1)S(1)}, u32[]{:S(2)}, u32[]{:S(2)}) collective-permute-start(bf16[1,48,4224]{2,1,0:T(8,128)(2,1)S(1)} %get-tuple-element.72), channel_id=1, source_target_pairs={{0,1},{1,0},{2,3},{3,2},{4,5},{5,4},{6,7},{7,6},{8,9},{9,8},{10,11... | collective-permute-start | bytes 1216520 | tf_op jit(solution)/shard_map/ppermute | solution.py:232
  65.7 2.4 %collective-permute-start.17 = (bf16[2,48,4224]{2,1,0:T(8,128)(2,1)S(1)}, bf16[2,48,4224]{2,1,0:T(8,128)(2,1)S(1)}, u32[]{:S(2)}, u32[]{:S(2)}) collective-permute-start(bf16[2,48,4224]{2,1,0:T(8,128)(2,1)S(1)} %collective-permute-done.6.refs_2_), channel_id=1, source_target_pairs={{0,1},{1,0},{2,3},{3,2},{4,5},{5,4},{6,7},{7,6},{8,9},{9,8},{10,11... | collective-permute-start | bytes 2433032 | tf_op jit(solution)/shard_map/ppermute | solution.py:232
  66.1 3.1 %collective-permute-start.18 = (bf16[2,48,4224]{2,1,0:T(8,128)(2,1)S(1)}, bf16[2,48,4224]{2,1,0:T(8,128)(2,1)S(1)}, u32[]{:S(2)}, u32[]{:S(2)}) collective-permute-start(bf16[2,48,4224]{2,1,0:T(8,128)(2,1)S(1)} %collective-permute-done.16.refs_4_), channel_id=1, source_target_pairs={{0,1},{1,0},{2,3},{3,2},{4,5},{5,4},{6,7},{7,6},{8,9},{9,8},{10,11... | collective-permute-start | bytes 2433032 | tf_op jit(solution)/shard_map/ppermute | solution.py:232
  66.2 8.9 %collective-permute-start.13 = (bf16[1,48,4224]{2,1,0:T(8,128)(2,1)S(1)}, bf16[1,48,4224]{2,1,0:T(8,128)(2,1)S(1)}, u32[]{:S(2)}, u32[]{:S(2)}) collective-permute-start(bf16[1,48,4224]{2,1,0:T(8,128)(2,1)S(1)} %get-tuple-element.69), channel_id=1, source_target_pairs={{0,2},{1,5},{2,0},{3,7},{4,6},{5,1},{6,4},{7,3},{8,10},{9,13},{10,... | collective-permute-start | bytes 1216520 | tf_op jit(solution)/shard_map/ppermute | solution.py:232
  66.7 11.2 %collective-permute-start.14 = (bf16[1,48,4224]{2,1,0:T(8,128)(2,1)S(1)}, bf16[1,48,4224]{2,1,0:T(8,128)(2,1)S(1)}, u32[]{:S(2)}, u32[]{:S(2)}) collective-permute-start(bf16[1,48,4224]{2,1,0:T(8,128)(2,1)S(1)} %get-tuple-element.70), channel_id=1, source_target_pairs={{0,3},{1,4},{2,1},{3,6},{4,7},{5,0},{6,5},{7,2},{8,11},{9,12},{10,... | collective-permute-start | bytes 1216520 | tf_op jit(solution)/shard_map/ppermute | solution.py:232

commit v7 on v6

--- a/solution.py
+++ b/solution.py
@@ -34,7 +34,7 @@
     copies.append(pltpu.make_async_copy(tokens, out.at[:, :width], sems.at[5]))
     for copy in copies:
         copy.start()
-    for copy in copies:
+    for copy in copies[:-1]:
         copy.wait()
     grads, proj, routes, gates, docs = held
     small = jnp.float32
@@ -45,6 +45,7 @@
     doc = jnp.concatenate([docs[...].astype(small)] * 8, axis=0).astype(jnp.bfloat16)
     meta += across(doc, place(8, rank + 2 * top), (0, 0))
     out[:, width:] = meta.astype(jnp.bfloat16)
+    copies[-1].wait()
 
 
 def extend(tokens, out_grad, proj_out, routes, gate_probs, doc_ids):
@@ -63,7 +64,14 @@
     )(*[pltpu.with_memory_space_constraint(o, pltpu.HBM) for o in operands])
 
 
-def compact_kernel(spots, capacity, top, rank, targets, after, *refs):
+def position(planes):
+    return (lax.axis_index("expert") * planes + lax.axis_index("dp")).astype(jnp.int32)
+
+
+def compact_kernel(spots, sides, planes, capacity, top, rank, after, *refs):
+    me = position(planes)
+    side = jnp.where(me & 1 == 0, sides[0], sides[1])
+    targets = [me, me ^ 1, me ^ side, me ^ side ^ 1]
     parts = 1 + spots[-1][0]
     sources, outs = refs[:-parts], refs[-parts:]
     count = len(sources)
@@ -98,20 +106,20 @@
             outs[out][lead, :, at:end] = part
 
 
-def compact(sources, targets, after, leads, capacity, top, rank):
+def compact(sources, after, leads, sides, planes, capacity, top, rank):
     spots = tuple((i, lead) for i, n in enumerate(leads) for lead in range(n))
-    body = functools.partial(compact_kernel, spots, capacity, top, rank)
+    body = functools.partial(compact_kernel, spots, sides, planes, capacity, top, rank)
     rows, width = len(sources) * capacity, sources[0].shape[1]
     return pl.pallas_call(
         body,
         out_shape=[jax.ShapeDtypeStruct((n, rows, width), jnp.bfloat16) for n in leads],
-        in_specs=[pl.BlockSpec(memory_space=pltpu.SMEM)] * 2
+        in_specs=[pl.BlockSpec(memory_space=pl.ANY)]
         + [pl.BlockSpec(memory_space=pltpu.VMEM)] * len(sources),
         out_specs=[pl.BlockSpec(memory_space=pltpu.VMEM)] * len(leads),
         compiler_params=pltpu.CompilerParams(vmem_limit_bytes=8 * MIB),
         cost_estimate=LIGHT,
         name="compact_rows",
-    )(targets, after, *sources)
+    )(after, *sources)
 
 
 def hold_kernel(gate_w, up_w, gate_out, up_out, done, sems):
@@ -141,7 +149,7 @@
     )(*[pltpu.with_memory_space_constraint(w, pltpu.HBM) for w in (w_gate, w_up)])
 
 
-def sketch_kernel(spots, top, rank, docs_total, expert, *refs):
+def sketch_kernel(spots, planes, top, rank, docs_total, *refs):
     pieces = refs[: len(spots)]
     gate_w, up_w, proj, total_in, total_out, rows_at, hidden_at, *folded = refs[len(spots) :]
     width, hidden = gate_w.shape
@@ -166,7 +174,7 @@
     wide = meta.astype(jnp.float32)
     lanes = lax.broadcasted_iota(jnp.int32, wide.shape, 1)
     is_route = (lanes >= rank + top) & (lanes < rank + 2 * top)
-    named = (is_route & (wide == expert[0].astype(jnp.float32))).astype(jnp.float32)
+    named = (is_route & (wide == position(planes).astype(jnp.float32))).astype(jnp.float32)
     gate = jnp.sum(wide * pltpu.roll(named, LANES - top, 1), axis=1, keepdims=True)
     spread_from = lax.broadcasted_iota(jnp.int32, (LANES, rank * rank), 0)
     spread_to = lax.broadcasted_iota(jnp.int32, (LANES, rank * rank), 1) // rank
@@ -189,7 +197,7 @@
     total_out[...] = folded[0][...].astype(total_out.dtype)
 
 
-def sketch(pieces, expert, weights, proj, total, top, rank, fold=False):
+def sketch(pieces, weights, proj, total, planes, top, rank, fold=False):
     width, hidden = weights[0].shape
     rows, arrays, spots = 0, [], []
     for beside in pieces:
@@ -197,7 +205,7 @@
             arrays.append(array)
             spots.append((lead, rows, column))
         rows += -(-beside[0][0].shape[1] // 16) * 16
-    body = functools.partial(sketch_kernel, tuple(spots), top, rank, total.shape[0])
+    body = functools.partial(sketch_kernel, tuple(spots), planes, top, rank, total.shape[0])
     vmem = pl.BlockSpec(memory_space=pltpu.VMEM)
     folded = (total.shape[0], rank * rank // LANES, LANES)
     result = jax.ShapeDtypeStruct(total.shape, jnp.float32)
@@ -206,7 +214,7 @@
     return pl.pallas_call(
         body,
         out_shape=result,
-        in_specs=[pl.BlockSpec(memory_space=pltpu.SMEM)] + [vmem] * (len(arrays) + 4),
+        in_specs=[vmem] * (len(arrays) + 4),
         out_specs=vmem,
         scratch_shapes=[
             pltpu.VMEM((rows, width + LANES), jnp.bfloat16),
@@ -216,7 +224,7 @@
         compiler_params=pltpu.CompilerParams(vmem_limit_bytes=14 * MIB),
         cost_estimate=LIGHT,
         name="sketch_rows",
-    )(expert, *arrays, *weights, proj, total)
+    )(*arrays, *weights, proj, total)
 
 
 def on_device(tokens, out_grad, routes, gate_probs, doc_ids, w_gate, w_up, proj_hidden, proj_out):
@@ -226,7 +234,6 @@
     top = routes.shape[1]
     rank = proj_out.shape[1]
     capacity = max(2, 3 * row_count * top // (2 * devices))
-    me = lax.axis_index(AXES).astype(jnp.int32)
 
     def swap(value, hops):
         return lax.ppermute(value, AXES, [(i, i ^ hops[i & 1]) for i in range(devices)])
@@ -244,15 +251,13 @@
     slots.insert(groups - 2, turn(ext, groups - 1))
     bits = [1 << b for b in range(1, planes.bit_length() - 1)]
     shared = [[b for b in bits if b != bits[core]] for core in (0, 1)]
-    side = jnp.where(me & 1 == 0, bits[0], bits[1]).astype(jnp.int32)
-    targets = jnp.stack([me, me ^ 1, me ^ side, me ^ side ^ 1])
     *weights, held = hold(w_gate, w_up)
     total = jnp.zeros((devices, rank * rank), jnp.float32)
-    own_id = me.reshape(1)
-    args = (capacity, top, rank)
+    own_id = jnp.zeros((1,), jnp.int32)
+    args = (tuple(bits[:2]), planes, capacity, top, rank)
 
     def sketch_of(total, pieces, fold=False):
-        return sketch(pieces, own_id, weights, proj_hidden.T, total, top, rank, fold)
+        return sketch(pieces, weights, proj_hidden.T, total, planes, top, rank, fold)
 
     def gather(slot):
         sources = [slot]
@@ -261,11 +266,11 @@
         return sources
 
     def spread(sources, after=own_id):
-        own, other, further = compact(sources, targets, after, (1, 1, 2), *args)
+        own, other, further = compact(sources, after, (1, 1, 2), *args)
         return [own, swap(other, (1, 1))], swap(further, bits)
 
     def spread_apart(sources):
-        own, other, same, crossed = compact(sources, targets, own_id, (1, 1, 1, 1), *args)
+        own, other, same, crossed = compact(sources, own_id, (1, 1, 1, 1), *args)
         return [own, swap(other, (1, 1))], [swap(same, bits), swap(crossed, [b ^ 1 for b in bits])]
 
     def near(*pairs):

time: 94 us -> 93.8 us (level)
  Pallas kernels: 31.3 us -> 29 us
  waiting for transfers between devices: 27.6 us -> 29.2 us
    pallas_call x4, Pallas kernels: 6.37 us -> 4.23 us  [compact(): pl.pallas_call(body, out_shape=[jax.ShapeDtypeStruct((n, rows, width), jn...]
  transfers between devices with their start and end apart: 19 -> 19, of which waited for: 9 -> 10; matrix products, arithmetic and copies ran while one was open for 0% -> 0% of each run, Pallas kernels for 28% -> 26%
where the time goes in v7:
time: 93.8 us; the launch traced here: 93.6 us
  waiting for transfers between devices  29.2 us (31%)
  Pallas kernels  29 us (31%)
  starting transfers between devices  22.8 us (24%)
  blocking collectives  11.9 us (13%)
    pallas_call x3, Pallas kernels, sketch(): pl.pallas_call(body, out_shape=result, in_specs=[vmem] * (len(arrays) + 4...  16.9 us
    ppermute x16, waiting for transfers between devices, swap(): lax.ppermute(value, AXES, [(i, i ^ hops[i & 1]) for i in range(devices)])  16.7 us
    ppermute x16, starting transfers between devices, swap(): lax.ppermute(value, AXES, [(i, i ^ hops[i & 1]) for i in range(devices)])  13.3 us
    ppermute x3, waiting for transfers between devices, turn(): lax.ppermute(value, AXES, [(a * planes + b, c * planes + d) for (a, b), (...  12.5 us
    all_to_all x1, blocking collectives, on_device(): lax.all_to_all(folded, AXES, split_axis=0, concat_axis=0, tiled=True)  11.9 us
    ppermute x3, starting transfers between devices, turn(): lax.ppermute(value, AXES, [(a * planes + b, c * planes + d) for (a, b), (...  9.45 us
    pallas_call x1, Pallas kernels, hold(): pl.pallas_call(hold_kernel, out_shape=[pltpu.VMEM(shape, jnp.bfloat16)] *...  6.3 us
    pallas_call x4, Pallas kernels, compact(): pl.pallas_call(body, out_shape=[jax.ShapeDtypeStruct((n, rows, width), jn...  4.23 us
  transfers between devices with their start and end apart: 19, of which 10 were waited for; matrix products, arithmetic and copies ran while one was open for 0% of the time, Pallas kernels for 26%

profile of v7, /device:TPU:0, one launch (start us, length us, event | category | flops | bytes accessed | tf_op | source)
XLA Modules:
  0.0 93.6 jit_solution(2477487711034569456)
XLA Ops:
  0.0 1.6 %extend_rows.1.refs_0_ = bf16[64,4224]{1,0:T(8,128)(2,1)S(1)} custom-call(bf16[64,4096]{1,0:T(8,128)(2,1)} %tokens.1, bf16[64,4096]{1,0:T(8,128)(2,1)} %refs_0_.1, bf16[32,4096]{1,0:T(8,128)(2,1)} %bitcast.8, s32[8,64]{1,0:T(8,128)} %bitcast.9, bf16[8,64]{1,0:T(8,128)(2,1)} %bitcast.10, s32[1,64]{1,0:T(1,128)} %bitcast.11), custom_call_target="tpu_custom_call" | custom-call | tf_op jit(solution)/shard_map/extend_rows/pallas_call | solution.py:55
  1.6 3.0 %collective-permute-start = (bf16[64,4224]{1,0:T(8,128)(2,1)S(1)}, bf16[64,4224]{1,0:T(8,128)(2,1)S(1)}, u32[]{:S(2)}, u32[]{:S(2)}) collective-permute-start(bf16[64,4224]{1,0:T(8,128)(2,1)S(1)} %extend_rows.1.refs_0_), channel_id=1, source_target_pairs={{0,4},{1,3},{2,6},{3,1},{4,0},{5,7},{6,2},{7,5},{8,12},{9,11},{10,... | collective-permute-start | bytes 1622024 | tf_op jit(solution)/shard_map/ppermute | solution.py:239
  4.6 3.6 %collective-permute-start.3 = (bf16[64,4224]{1,0:T(8,128)(2,1)S(1)}, bf16[64,4224]{1,0:T(8,128)(2,1)S(1)}, u32[]{:S(2)}, u32[]{:S(2)}) collective-permute-start(bf16[64,4224]{1,0:T(8,128)(2,1)S(1)} %extend_rows.1.refs_0_), channel_id=1, source_target_pairs={{8,0},{9,1},{10,2},{11,3},{12,4},{13,5},{14,6},{15,7},{16,8},{17,9... | collective-permute-start | bytes 1622024 | tf_op jit(solution)/shard_map/ppermute | solution.py:243
  8.2 3.8 %collective-permute-done.refs_1_ = bf16[64,4224]{1,0:T(8,128)(2,1)S(1)} collective-permute-done((bf16[64,4224]{1,0:T(8,128)(2,1)S(1)}, bf16[64,4224]{1,0:T(8,128)(2,1)S(1)}, u32[]{:S(2)}, u32[]{:S(2)}) %collective-permute-start) | collective-permute-done | bytes 540704 | tf_op jit(solution)/shard_map/ppermute | solution.py:239
  12.0 0.9 compact_rows.4
  12.9 2.1 %collective-permute-start.2 = (bf16[2,48,4224]{2,1,0:T(8,128)(2,1)S(1)}, bf16[2,48,4224]{2,1,0:T(8,128)(2,1)S(1)}, u32[]{:S(2)}, u32[]{:S(2)}) collective-permute-start(bf16[2,48,4224]{2,1,0:T(8,128)(2,1)S(1)} %get-tuple-element.46), channel_id=1, source_target_pairs={{0,2},{1,5},{2,0},{3,7},{4,6},{5,1},{6,4},{7,3},{8,10},{9,13},{10,... | collective-permute-start | bytes 2433032 | tf_op jit(solution)/shard_map/ppermute | solution.py:239
  14.9 1.6 %collective-permute-start.5 = (bf16[64,4224]{1,0:T(8,128)(2,1)S(1)}, bf16[64,4224]{1,0:T(8,128)(2,1)S(1)}, u32[]{:S(2)}, u32[]{:S(2)}) collective-permute-start(bf16[64,4224]{1,0:T(8,128)(2,1)S(1)} %extend_rows.1.refs_0_), channel_id=1, source_target_pairs={{24,0},{25,1},{26,2},{27,3},{28,4},{29,5},{30,6},{31,7},{0,8},{1,9... | collective-permute-start | bytes 1622024 | tf_op jit(solution)/shard_map/ppermute | solution.py:243
  16.5 4.5 %collective-permute-done.3.refs_0_ = bf16[64,4224]{1,0:T(8,128)(2,1)S(1)} collective-permute-done((bf16[64,4224]{1,0:T(8,128)(2,1)S(1)}, bf16[64,4224]{1,0:T(8,128)(2,1)S(1)}, u32[]{:S(2)}, u32[]{:S(2)}) %collective-permute-start.3) | collective-permute-done | bytes 540704 | tf_op jit(solution)/shard_map/ppermute | solution.py:243
  21.0 0.4 collective-permute-start.4
  21.4 0.0 collective-permute-start.1
  21.4 4.3 %collective-permute-start.9 = (bf16[64,4224]{1,0:T(8,128)(2,1)S(1)}, bf16[64,4224]{1,0:T(8,128)(2,1)S(1)}, u32[]{:S(2)}, u32[]{:S(2)}) collective-permute-start(bf16[64,4224]{1,0:T(8,128)(2,1)S(1)} %collective-permute-done.3.refs_0_), channel_id=1, source_target_pairs={{8,0},{9,1},{10,2},{11,3},{12,4},{13,5},{14,6},{15,7},{16,8},{17,9... | collective-permute-start | bytes 1622024 | tf_op jit(solution)/shard_map/ppermute | solution.py:243
  25.7 7.8 %collective-permute-done.5.refs_0_ = bf16[64,4224]{1,0:T(8,128)(2,1)S(1)} collective-permute-done((bf16[64,4224]{1,0:T(8,128)(2,1)S(1)}, bf16[64,4224]{1,0:T(8,128)(2,1)S(1)}, u32[]{:S(2)}, u32[]{:S(2)}) %collective-permute-start.5) | collective-permute-done | bytes 540704 | tf_op jit(solution)/shard_map/ppermute | solution.py:243
  33.5 0.0 collective-permute-done.1.refs_1_
  33.5 0.0 collective-permute-done.4.refs_1_
  33.5 0.0 collective-permute-done.2.refs_6_
  33.5 0.4 collective-permute-start.8
  33.9 0.9 compact_rows.5
  34.8 0.1 collective-permute-start.7
  34.9 0.5 collective-permute-start.12
  35.4 1.7 %collective-permute-start.6 = (bf16[2,48,4224]{2,1,0:T(8,128)(2,1)S(1)}, bf16[2,48,4224]{2,1,0:T(8,128)(2,1)S(1)}, u32[]{:S(2)}, u32[]{:S(2)}) collective-permute-start(bf16[2,48,4224]{2,1,0:T(8,128)(2,1)S(1)} %get-tuple-element.49), channel_id=1, source_target_pairs={{0,2},{1,5},{2,0},{3,7},{4,6},{5,1},{6,4},{7,3},{8,10},{9,13},{10,... | collective-permute-start | bytes 2433032 | tf_op jit(solution)/shard_map/ppermute | solution.py:239
  37.1 6.3 %hold_weights.1 = (bf16[4096,1024]{1,0:T(8,128)(2,1)S(1)}, bf16[4096,1024]{1,0:T(8,128)(2,1)S(1)}, s32[1]{0:T(128)}) custom-call(bf16[1,4096,1024]{2,1,0:T(8,128)(2,1)} %gate_w.1, bf16[1,4096,1024]{2,1,0:T(8,128)(2,1)} %up_w.1), custom_call_target="tpu_custom_call" | custom-call | flops 1 | bytes 1 | tf_op jit(solution)/shard_map/hold_weights/pallas_call | solution.py:139
  43.4 0.2 collective-permute-done.9.refs_0_
  43.6 0.0 collective-permute-done.7.refs_3_
  43.6 4.2 %collective-permute-done.8.refs_1_ = bf16[64,4224]{1,0:T(8,128)(2,1)S(1)} collective-permute-done((bf16[64,4224]{1,0:T(8,128)(2,1)S(1)}, bf16[64,4224]{1,0:T(8,128)(2,1)S(1)}, u32[]{:S(2)}, u32[]{:S(2)}) %collective-permute-start.8) | collective-permute-done | bytes 540704 | tf_op jit(solution)/shard_map/ppermute | solution.py:239
  47.8 1.6 %compact_rows.6 = (bf16[1,48,4224]{2,1,0:T(8,128)(2,1)S(1)}, bf16[1,48,4224]{2,1,0:T(8,128)(2,1)S(1)}, bf16[2,48,4224]{2,1,0:T(8,128)(2,1)S(1)}) custom-call(s32[1]{0:T(128)} %get-tuple-element.59.after, bf16[64,4224]{1,0:T(8,128)(2,1)S(1)} %collective-permute-done.5.refs_0_, bf16[64,4224]{1,0:T(8,128)(2,1)S(1)} %collective-permute-done.8.refs_1_), custom_call_target="tpu_custom_call" | custom-call | flops 1 | bytes 1 | tf_op jit(solution)/shard_map/compact_rows/pallas_call | solution.py:113
  49.3 0.1 collective-permute-start.11
  49.4 1.9 %collective-permute-start.16 = (bf16[2,48,4224]{2,1,0:T(8,128)(2,1)S(1)}, bf16[2,48,4224]{2,1,0:T(8,128)(2,1)S(1)}, u32[]{:S(2)}, u32[]{:S(2)}) collective-permute-start(bf16[2,48,4224]{2,1,0:T(8,128)(2,1)S(1)} %get-tuple-element.74), channel_id=1, source_target_pairs={{0,2},{1,5},{2,0},{3,7},{4,6},{5,1},{6,4},{7,3},{8,10},{9,13},{10,... | collective-permute-start | bytes 2433032 | tf_op jit(solution)/shard_map/ppermute | solution.py:239
  51.3 0.0 collective-permute-done.12.refs_7_
  51.3 0.0 collective-permute-done.11.refs_5_
  51.4 7.7 %sketch_rows.3.refs_9_ = f32[32,1024]{1,0:T(8,128)S(1)} custom-call(bf16[1,48,4224]{2,1,0:T(8,128)(2,1)S(1)} %get-tuple-element.55.refs_0_, bf16[1,48,4224]{2,1,0:T(8,128)(2,1)S(1)} %collective-permute-done.1.refs_1_, bf16[1,48,4224]{2,1,0:T(8,128)(2,1)S(1)} %get-tuple-element.57.refs_2_, bf16[1,48,4224]{2,1,0:T(8,128)(2,1)S(1)} %collective-permute-done.7.refs_3_, ...), custom_call_target="tpu_custom_call" | custom-call | flops 1 | bytes 1 | tf_op jit(solution)/shard_map/sketch_rows/pallas_call | solution.py:214
  59.0 0.0 collective-permute-done.6.refs_2_
  59.1 2.9 %collective-permute-done.10.refs_1_ = bf16[64,4224]{1,0:T(8,128)(2,1)S(1)} collective-permute-done((bf16[64,4224]{1,0:T(8,128)(2,1)S(1)}, bf16[64,4224]{1,0:T(8,128)(2,1)S(1)}, u32[]{:S(2)}, u32[]{:S(2)}) %collective-permute-start.10) | collective-permute-done | bytes 540704 | tf_op jit(solution)/shard_map/ppermute | solution.py:239
  62.0 0.9 compact_rows.7
  62.9 0.1 collective-permute-start.15
  63.0 0.0 collective-permute-done.16.refs_4_
  63.0 1.7 %collective-permute-done.15.refs_1_ = bf16[1,48,4224]{2,1,0:T(8,128)(2,1)S(1)} collective-permute-done((bf16[1,48,4224]{2,1,0:T(8,128)(2,1)S(1)}, bf16[1,48,4224]{2,1,0:T(8,128)(2,1)S(1)}, u32[]{:S(2)}, u32[]{:S(2)}) %collective-permute-start.15) | collective-permute-done | bytes 405536 | tf_op jit(solution)/shard_map/ppermute | solution.py:239
  64.7 1.2 %collective-permute-start.17 = (bf16[2,48,4224]{2,1,0:T(8,128)(2,1)S(1)}, bf16[2,48,4224]{2,1,0:T(8,128)(2,1)S(1)}, u32[]{:S(2)}, u32[]{:S(2)}) collective-permute-start(bf16[2,48,4224]{2,1,0:T(8,128)(2,1)S(1)} %collective-permute-done.6.refs_2_), channel_id=1, source_target_pairs={{0,1},{1,0},{2,3},{3,2},{4,5},{5,4},{6,7},{7,6},{8,9},{9,8},{10,11... | collective-permute-start | bytes 2433032 | tf_op jit(solution)/shard_map/ppermute | solution.py:239
  65.9 0.0 collective-permute-start.18
  65.9 0.6 collective-permute-start.13
  66.5 1.3 %collective-permute-start.14 = (bf16[1,48,4224]{2,1,0:T(8,128)(2,1)S(1)}, bf16[1,48,4224]{2,1,0:T(8,128)(2,1)S(1)}, u32[]{:S(2)}, u32[]{:S(2)}) collective-permute-start(bf16[1,48,4224]{2,1,0:T(8,128)(2,1)S(1)} %get-tuple-element.70), channel_id=1, source_target_pairs={{0,3},{1,4},{2,1},{3,6},{4,7},{5,0},{6,5},{7,2},{8,11},{9,12},{10,... | collective-permute-start | bytes 1216520 | tf_op jit(solution)/shard_map/ppermute | solution.py:239
  67.8 0.1 collective-permute-done.17.refs_3_
  67.9 1.2 %collective-permute-done.18.refs_5_ = bf16[2,48,4224]{2,1,0:T(8,128)(2,1)S(1)} collective-permute-done((bf16[2,48,4224]{2,1,0:T(8,128)(2,1)S(1)}, bf16[2,48,4224]{2,1,0:T(8,128)(2,1)S(1)}, u32[]{:S(2)}, u32[]{:S(2)}) %collective-permute-start.18) | collective-permute-done | bytes 811040 | tf_op jit(solution)/shard_map/ppermute | solution.py:239
  69.0 5.9 %sketch_rows.4.refs_5_ = f32[32,1024]{1,0:T(8,128)S(1)} custom-call(bf16[1,48,4224]{2,1,0:T(8,128)(2,1)S(1)} %get-tuple-element.75.refs_0_, bf16[1,48,4224]{2,1,0:T(8,128)(2,1)S(1)} %collective-permute-done.15.refs_1_, bf16[2,48,4224]{2,1,0:T(8,128)(2,1)S(1)} %collective-permute-done.6.refs_2_, bf16[2,48,4224]{2,1,0:T(8,128)(2,1)S(1)} %collective-permute-done.17.refs_3_, ...), custom_call_target="tpu_custom_call" | custom-call | flops 1 | bytes 1 | tf_op jit(solution)/shard_map/sketch_rows/pallas_call | solution.py:214
  74.9 0.0 collective-permute-done.13.refs_0_
  74.9 2.8 %collective-permute-done.14.refs_1_ = bf16[1,48,4224]{2,1,0:T(8,128)(2,1)S(1)} collective-permute-done((bf16[1,48,4224]{2,1,0:T(8,128)(2,1)S(1)}, bf16[1,48,4224]{2,1,0:T(8,128)(2,1)S(1)}, u32[]{:S(2)}, u32[]{:S(2)}) %collective-permute-start.14) | collective-permute-done | bytes 405536 | tf_op jit(solution)/shard_map/ppermute | solution.py:239
  77.7 3.3 %sketch_rows.5 = bf16[32,8,128]{2,1,0:T(8,128)(2,1)S(1)} custom-call(bf16[1,48,4224]{2,1,0:T(8,128)(2,1)S(1)} %collective-permute-done.13.refs_0_, bf16[1,48,4224]{2,1,0:T(8,128)(2,1)S(1)} %collective-permute-done.14.refs_1_, bf16[4096,1024]{1,0:T(8,128)(2,1)S(1)} %get-tuple-element.65.refs_8_.refs_6_.refs_2_, ...), custom_call_target="tpu_custom_call" | custom-call | flops 1 | bytes 1 | tf_op jit(solution)/shard_map/sketch_rows/pallas_call | solution.py:214
  81.1 11.9 %all_to_all.5 = bf16[32,8,128]{2,1,0:T(8,128)(2,1)S(1)} all-to-all(bf16[32,8,128]{2,1,0:T(8,128)(2,1)S(1)} %sketch_rows.5), channel_id=1, replica_groups=mesh['expert'=4,'dp'=8] {'expert','dp'}, dimensions={0} | all-to-all | bytes 131072 | tf_op jit(solution)/shard_map/all_to_all | solution.py:311
  92.9 0.7 reshape.19
  (4 shorter events, 0.0 us)
Async XLA Ops:
  1.6 10.4 %collective-permute-start = (bf16[64,4224]{1,0:T(8,128)(2,1)S(1)}, bf16[64,4224]{1,0:T(8,128)(2,1)S(1)}, u32[]{:S(2)}, u32[]{:S(2)}) collective-permute-start(bf16[64,4224]{1,0:T(8,128)(2,1)S(1)} %extend_rows.1.refs_0_), channel_id=1, source_target_pairs={{0,4},{1,3},{2,6},{3,1},{4,0},{5,7},{6,2},{7,5},{8,12},{9,11},{10,... | collective-permute-start | bytes 1622024 | tf_op jit(solution)/shard_map/ppermute | solution.py:239
  4.6 16.4 %collective-permute-start.3 = (bf16[64,4224]{1,0:T(8,128)(2,1)S(1)}, bf16[64,4224]{1,0:T(8,128)(2,1)S(1)}, u32[]{:S(2)}, u32[]{:S(2)}) collective-permute-start(bf16[64,4224]{1,0:T(8,128)(2,1)S(1)} %extend_rows.1.refs_0_), channel_id=1, source_target_pairs={{8,0},{9,1},{10,2},{11,3},{12,4},{13,5},{14,6},{15,7},{16,8},{17,9... | collective-permute-start | bytes 1622024 | tf_op jit(solution)/shard_map/ppermute | solution.py:243
  12.9 20.6 %collective-permute-start.2 = (bf16[2,48,4224]{2,1,0:T(8,128)(2,1)S(1)}, bf16[2,48,4224]{2,1,0:T(8,128)(2,1)S(1)}, u32[]{:S(2)}, u32[]{:S(2)}) collective-permute-start(bf16[2,48,4224]{2,1,0:T(8,128)(2,1)S(1)} %get-tuple-element.46), channel_id=1, source_target_pairs={{0,2},{1,5},{2,0},{3,7},{4,6},{5,1},{6,4},{7,3},{8,10},{9,13},{10,... | collective-permute-start | bytes 2433032 | tf_op jit(solution)/shard_map/ppermute | solution.py:239
  14.9 18.6 %collective-permute-start.5 = (bf16[64,4224]{1,0:T(8,128)(2,1)S(1)}, bf16[64,4224]{1,0:T(8,128)(2,1)S(1)}, u32[]{:S(2)}, u32[]{:S(2)}) collective-permute-start(bf16[64,4224]{1,0:T(8,128)(2,1)S(1)} %extend_rows.1.refs_0_), channel_id=1, source_target_pairs={{24,0},{25,1},{26,2},{27,3},{28,4},{29,5},{30,6},{31,7},{0,8},{1,9... | collective-permute-start | bytes 1622024 | tf_op jit(solution)/shard_map/ppermute | solution.py:243
  21.0 12.5 %collective-permute-start.4 = (bf16[64,4224]{1,0:T(8,128)(2,1)S(1)}, bf16[64,4224]{1,0:T(8,128)(2,1)S(1)}, u32[]{:S(2)}, u32[]{:S(2)}) collective-permute-start(bf16[64,4224]{1,0:T(8,128)(2,1)S(1)} %collective-permute-done.3.refs_0_), channel_id=1, source_target_pairs={{0,4},{1,3},{2,6},{3,1},{4,0},{5,7},{6,2},{7,5},{8,12},{9,11},{10,... | collective-permute-start | bytes 1622024 | tf_op jit(solution)/shard_map/ppermute | solution.py:239
  21.4 12.1 %collective-permute-start.1 = (bf16[1,48,4224]{2,1,0:T(8,128)(2,1)S(1)}, bf16[1,48,4224]{2,1,0:T(8,128)(2,1)S(1)}, u32[]{:S(2)}, u32[]{:S(2)}) collective-permute-start(bf16[1,48,4224]{2,1,0:T(8,128)(2,1)S(1)} %get-tuple-element.45), channel_id=1, source_target_pairs={{0,1},{1,0},{2,3},{3,2},{4,5},{5,4},{6,7},{7,6},{8,9},{9,8},{10,11... | collective-permute-start | bytes 1216520 | tf_op jit(solution)/shard_map/ppermute | solution.py:239
  21.4 22.2 %collective-permute-start.9 = (bf16[64,4224]{1,0:T(8,128)(2,1)S(1)}, bf16[64,4224]{1,0:T(8,128)(2,1)S(1)}, u32[]{:S(2)}, u32[]{:S(2)}) collective-permute-start(bf16[64,4224]{1,0:T(8,128)(2,1)S(1)} %collective-permute-done.3.refs_0_), channel_id=1, source_target_pairs={{8,0},{9,1},{10,2},{11,3},{12,4},{13,5},{14,6},{15,7},{16,8},{17,9... | collective-permute-start | bytes 1622024 | tf_op jit(solution)/shard_map/ppermute | solution.py:243
  33.5 14.3 %collective-permute-start.8 = (bf16[64,4224]{1,0:T(8,128)(2,1)S(1)}, bf16[64,4224]{1,0:T(8,128)(2,1)S(1)}, u32[]{:S(2)}, u32[]{:S(2)}) collective-permute-start(bf16[64,4224]{1,0:T(8,128)(2,1)S(1)} %collective-permute-done.5.refs_0_), channel_id=1, source_target_pairs={{0,4},{1,3},{2,6},{3,1},{4,0},{5,7},{6,2},{7,5},{8,12},{9,11},{10,... | collective-permute-start | bytes 1622024 | tf_op jit(solution)/shard_map/ppermute | solution.py:239
  34.8 8.7 %collective-permute-start.7 = (bf16[1,48,4224]{2,1,0:T(8,128)(2,1)S(1)}, bf16[1,48,4224]{2,1,0:T(8,128)(2,1)S(1)}, u32[]{:S(2)}, u32[]{:S(2)}) collective-permute-start(bf16[1,48,4224]{2,1,0:T(8,128)(2,1)S(1)} %get-tuple-element.51), channel_id=1, source_target_pairs={{0,1},{1,0},{2,3},{3,2},{4,5},{5,4},{6,7},{7,6},{8,9},{9,8},{10,11... | collective-permute-start | bytes 1216520 | tf_op jit(solution)/shard_map/ppermute | solution.py:239
  34.9 16.4 %collective-permute-start.12 = (bf16[2,48,4224]{2,1,0:T(8,128)(2,1)S(1)}, bf16[2,48,4224]{2,1,0:T(8,128)(2,1)S(1)}, u32[]{:S(2)}, u32[]{:S(2)}) collective-permute-start(bf16[2,48,4224]{2,1,0:T(8,128)(2,1)S(1)} %collective-permute-done.2.refs_6_), channel_id=1, source_target_pairs={{0,1},{1,0},{2,3},{3,2},{4,5},{5,4},{6,7},{7,6},{8,9},{9,8},{10,11... | collective-permute-start | bytes 2433032 | tf_op jit(solution)/shard_map/ppermute | solution.py:239
  35.4 15.9 %copy-start = (bf16[1024,32]{0,1:T(8,128)(2,1)S(1)}, bf16[1024,32]{0,1:T(8,128)(2,1)}, u32[]{:S(2)}) copy-start(bf16[1024,32]{0,1:T(8,128)(2,1)} %param.16) | copy-start | bytes 196612
  35.4 23.6 %collective-permute-start.6 = (bf16[2,48,4224]{2,1,0:T(8,128)(2,1)S(1)}, bf16[2,48,4224]{2,1,0:T(8,128)(2,1)S(1)}, u32[]{:S(2)}, u32[]{:S(2)}) collective-permute-start(bf16[2,48,4224]{2,1,0:T(8,128)(2,1)S(1)} %get-tuple-element.49), channel_id=1, source_target_pairs={{0,2},{1,5},{2,0},{3,7},{4,6},{5,1},{6,4},{7,3},{8,10},{9,13},{10,... | collective-permute-start | bytes 2433032 | tf_op jit(solution)/shard_map/ppermute | solution.py:239
  47.8 14.2 %collective-permute-start.10 = (bf16[64,4224]{1,0:T(8,128)(2,1)S(1)}, bf16[64,4224]{1,0:T(8,128)(2,1)S(1)}, u32[]{:S(2)}, u32[]{:S(2)}) collective-permute-start(bf16[64,4224]{1,0:T(8,128)(2,1)S(1)} %collective-permute-done.9.refs_0_), channel_id=1, source_target_pairs={{0,4},{1,3},{2,6},{3,1},{4,0},{5,7},{6,2},{7,5},{8,12},{9,11},{10,... | collective-permute-start | bytes 1622024 | tf_op jit(solution)/shard_map/ppermute | solution.py:239
  49.3 2.0 %collective-permute-start.11 = (bf16[1,48,4224]{2,1,0:T(8,128)(2,1)S(1)}, bf16[1,48,4224]{2,1,0:T(8,128)(2,1)S(1)}, u32[]{:S(2)}, u32[]{:S(2)}) collective-permute-start(bf16[1,48,4224]{2,1,0:T(8,128)(2,1)S(1)} %get-tuple-element.63), channel_id=1, source_target_pairs={{0,1},{1,0},{2,3},{3,2},{4,5},{5,4},{6,7},{7,6},{8,9},{9,8},{10,11... | collective-permute-start | bytes 1216520 | tf_op jit(solution)/shard_map/ppermute | solution.py:239
  49.4 13.5 %collective-permute-start.16 = (bf16[2,48,4224]{2,1,0:T(8,128)(2,1)S(1)}, bf16[2,48,4224]{2,1,0:T(8,128)(2,1)S(1)}, u32[]{:S(2)}, u32[]{:S(2)}) collective-permute-start(bf16[2,48,4224]{2,1,0:T(8,128)(2,1)S(1)} %get-tuple-element.74), channel_id=1, source_target_pairs={{0,2},{1,5},{2,0},{3,7},{4,6},{5,1},{6,4},{7,3},{8,10},{9,13},{10,... | collective-permute-start | bytes 2433032 | tf_op jit(solution)/shard_map/ppermute | solution.py:239
  62.9 1.8 %collective-permute-start.15 = (bf16[1,48,4224]{2,1,0:T(8,128)(2,1)S(1)}, bf16[1,48,4224]{2,1,0:T(8,128)(2,1)S(1)}, u32[]{:S(2)}, u32[]{:S(2)}) collective-permute-start(bf16[1,48,4224]{2,1,0:T(8,128)(2,1)S(1)} %get-tuple-element.72), channel_id=1, source_target_pairs={{0,1},{1,0},{2,3},{3,2},{4,5},{5,4},{6,7},{7,6},{8,9},{9,8},{10,11... | collective-permute-start | bytes 1216520 | tf_op jit(solution)/shard_map/ppermute | solution.py:239
  64.7 3.2 %collective-permute-start.17 = (bf16[2,48,4224]{2,1,0:T(8,128)(2,1)S(1)}, bf16[2,48,4224]{2,1,0:T(8,128)(2,1)S(1)}, u32[]{:S(2)}, u32[]{:S(2)}) collective-permute-start(bf16[2,48,4224]{2,1,0:T(8,128)(2,1)S(1)} %collective-permute-done.6.refs_2_), channel_id=1, source_target_pairs={{0,1},{1,0},{2,3},{3,2},{4,5},{5,4},{6,7},{7,6},{8,9},{9,8},{10,11... | collective-permute-start | bytes 2433032 | tf_op jit(solution)/shard_map/ppermute | solution.py:239
  65.9 3.1 %collective-permute-start.18 = (bf16[2,48,4224]{2,1,0:T(8,128)(2,1)S(1)}, bf16[2,48,4224]{2,1,0:T(8,128)(2,1)S(1)}, u32[]{:S(2)}, u32[]{:S(2)}) collective-permute-start(bf16[2,48,4224]{2,1,0:T(8,128)(2,1)S(1)} %collective-permute-done.16.refs_4_), channel_id=1, source_target_pairs={{0,1},{1,0},{2,3},{3,2},{4,5},{5,4},{6,7},{7,6},{8,9},{9,8},{10,11... | collective-permute-start | bytes 2433032 | tf_op jit(solution)/shard_map/ppermute | solution.py:239
  65.9 9.0 %collective-permute-start.13 = (bf16[1,48,4224]{2,1,0:T(8,128)(2,1)S(1)}, bf16[1,48,4224]{2,1,0:T(8,128)(2,1)S(1)}, u32[]{:S(2)}, u32[]{:S(2)}) collective-permute-start(bf16[1,48,4224]{2,1,0:T(8,128)(2,1)S(1)} %get-tuple-element.69), channel_id=1, source_target_pairs={{0,2},{1,5},{2,0},{3,7},{4,6},{5,1},{6,4},{7,3},{8,10},{9,13},{10,... | collective-permute-start | bytes 1216520 | tf_op jit(solution)/shard_map/ppermute | solution.py:239
  66.5 11.2 %collective-permute-start.14 = (bf16[1,48,4224]{2,1,0:T(8,128)(2,1)S(1)}, bf16[1,48,4224]{2,1,0:T(8,128)(2,1)S(1)}, u32[]{:S(2)}, u32[]{:S(2)}) collective-permute-start(bf16[1,48,4224]{2,1,0:T(8,128)(2,1)S(1)} %get-tuple-element.70), channel_id=1, source_target_pairs={{0,3},{1,4},{2,1},{3,6},{4,7},{5,0},{6,5},{7,2},{8,11},{9,12},{10,... | collective-permute-start | bytes 1216520 | tf_op jit(solution)/shard_map/ppermute | solution.py:239

commit v8 on v7

--- a/solution.py
+++ b/solution.py
@@ -80,18 +80,18 @@
     meta = jnp.concatenate([s[:, width:] for s in sources], axis=0).astype(jnp.float32)
     lanes = lax.broadcasted_iota(jnp.int32, meta.shape, 1)
     is_route = (lanes >= rank + top) & (lanes < rank + 2 * top)
-    hits = jnp.zeros(meta.shape, jnp.float32)
-    for q in range(4):
-        named = is_route & (meta == targets[q].astype(jnp.float32))
-        hit = jnp.sum(named.astype(jnp.float32), axis=1, keepdims=True)
-        hits = jnp.where(lanes == q, hit, hits)
+    named = [is_route & (meta == targets[q].astype(jnp.float32)) for q in range(4)]
+    named = jnp.concatenate([n.astype(jnp.float32).astype(jnp.bfloat16) for n in named], axis=1)
+    expert = lax.broadcasted_iota(jnp.int32, (8, 4 * LANES), 0)
+    column = lax.broadcasted_iota(jnp.int32, (8, 4 * LANES), 1)
+    hits = across((expert == column // LANES).astype(jnp.bfloat16), named, (1, 1))
     every = count * rows
-    here = lax.broadcasted_iota(jnp.int32, (every, every), 0)
-    other = lax.broadcasted_iota(jnp.int32, (every, every), 1)
+    other = lax.broadcasted_iota(jnp.int32, (every, every), 0)
+    here = lax.broadcasted_iota(jnp.int32, (every, every), 1)
     earlier = ((other < here) & (other // rows == here // rows)).astype(jnp.bfloat16)
-    before = dot(earlier, hits.astype(jnp.bfloat16))
-    first = lax.broadcasted_iota(jnp.int32, meta.shape, 0) // rows * capacity
-    slots = jnp.where(hits > 0, before + first.astype(jnp.float32), -1.0).T
+    before = dot(hits.astype(jnp.bfloat16), earlier)
+    first = lax.broadcasted_iota(jnp.int32, hits.shape, 1) // rows * capacity
+    slots = jnp.where(hits > 0, before + first.astype(jnp.float32), -1.0)
     picked = count * capacity
     spot = lax.broadcasted_iota(jnp.int32, (picked, every), 0).astype(jnp.float32)
     pick = jnp.concatenate(

time: 93.8 us -> 93.8 us (level)
  no operation moved by 1% of the time
where the time goes in v8:
time: 93.8 us; the launch traced here: 93.6 us
  waiting for transfers between devices  29.2 us (31%)
  Pallas kernels  28.9 us (31%)
  starting transfers between devices  22.8 us (24%)
  blocking collectives  11.9 us (13%)
    pallas_call x3, Pallas kernels, sketch(): pl.pallas_call(body, out_shape=result, in_specs=[vmem] * (len(arrays) + 4...  16.9 us
    ppermute x16, waiting for transfers between devices, swap(): lax.ppermute(value, AXES, [(i, i ^ hops[i & 1]) for i in range(devices)])  16.7 us
    ppermute x16, starting transfers between devices, swap(): lax.ppermute(value, AXES, [(i, i ^ hops[i & 1]) for i in range(devices)])  13.3 us
    ppermute x3, waiting for transfers between devices, turn(): lax.ppermute(value, AXES, [(a * planes + b, c * planes + d) for (a, b), (...  12.5 us
    all_to_all x1, blocking collectives, on_device(): lax.all_to_all(folded, AXES, split_axis=0, concat_axis=0, tiled=True)  11.9 us
    ppermute x3, starting transfers between devices, turn(): lax.ppermute(value, AXES, [(a * planes + b, c * planes + d) for (a, b), (...  9.46 us
    pallas_call x1, Pallas kernels, hold(): pl.pallas_call(hold_kernel, out_shape=[pltpu.VMEM(shape, jnp.bfloat16)] *...  6.3 us
    pallas_call x4, Pallas kernels, compact(): pl.pallas_call(body, out_shape=[jax.ShapeDtypeStruct((n, rows, width), jn...  4.14 us
  transfers between devices with their start and end apart: 19, of which 10 were waited for; matrix products, arithmetic and copies ran while one was open for 0% of the time, Pallas kernels for 26%

profile of v8, /device:TPU:0, one launch (start us, length us, event | category | flops | bytes accessed | tf_op | source)
XLA Modules:
  0.0 93.6 jit_solution(2176061616291198203)
XLA Ops:
  0.0 1.6 %extend_rows.1.refs_0_ = bf16[64,4224]{1,0:T(8,128)(2,1)S(1)} custom-call(bf16[64,4096]{1,0:T(8,128)(2,1)} %tokens.1, bf16[64,4096]{1,0:T(8,128)(2,1)} %refs_0_.1, bf16[32,4096]{1,0:T(8,128)(2,1)} %bitcast.8, s32[8,64]{1,0:T(8,128)} %bitcast.9, bf16[8,64]{1,0:T(8,128)(2,1)} %bitcast.10, s32[1,64]{1,0:T(1,128)} %bitcast.11), custom_call_target="tpu_custom_call" | custom-call | tf_op jit(solution)/shard_map/extend_rows/pallas_call | solution.py:55
  1.6 3.0 %collective-permute-start = (bf16[64,4224]{1,0:T(8,128)(2,1)S(1)}, bf16[64,4224]{1,0:T(8,128)(2,1)S(1)}, u32[]{:S(2)}, u32[]{:S(2)}) collective-permute-start(bf16[64,4224]{1,0:T(8,128)(2,1)S(1)} %extend_rows.1.refs_0_), channel_id=1, source_target_pairs={{0,4},{1,3},{2,6},{3,1},{4,0},{5,7},{6,2},{7,5},{8,12},{9,11},{10,... | collective-permute-start | bytes 1622024 | tf_op jit(solution)/shard_map/ppermute | solution.py:239
  4.6 3.6 %collective-permute-start.3 = (bf16[64,4224]{1,0:T(8,128)(2,1)S(1)}, bf16[64,4224]{1,0:T(8,128)(2,1)S(1)}, u32[]{:S(2)}, u32[]{:S(2)}) collective-permute-start(bf16[64,4224]{1,0:T(8,128)(2,1)S(1)} %extend_rows.1.refs_0_), channel_id=1, source_target_pairs={{8,0},{9,1},{10,2},{11,3},{12,4},{13,5},{14,6},{15,7},{16,8},{17,9... | collective-permute-start | bytes 1622024 | tf_op jit(solution)/shard_map/ppermute | solution.py:243
  8.2 3.8 %collective-permute-done.refs_1_ = bf16[64,4224]{1,0:T(8,128)(2,1)S(1)} collective-permute-done((bf16[64,4224]{1,0:T(8,128)(2,1)S(1)}, bf16[64,4224]{1,0:T(8,128)(2,1)S(1)}, u32[]{:S(2)}, u32[]{:S(2)}) %collective-permute-start) | collective-permute-done | bytes 540704 | tf_op jit(solution)/shard_map/ppermute | solution.py:239
  12.0 0.9 compact_rows.4
  12.9 2.0 %collective-permute-start.2 = (bf16[2,48,4224]{2,1,0:T(8,128)(2,1)S(1)}, bf16[2,48,4224]{2,1,0:T(8,128)(2,1)S(1)}, u32[]{:S(2)}, u32[]{:S(2)}) collective-permute-start(bf16[2,48,4224]{2,1,0:T(8,128)(2,1)S(1)} %get-tuple-element.46), channel_id=1, source_target_pairs={{0,2},{1,5},{2,0},{3,7},{4,6},{5,1},{6,4},{7,3},{8,10},{9,13},{10,... | collective-permute-start | bytes 2433032 | tf_op jit(solution)/shard_map/ppermute | solution.py:239
  14.9 1.6 %collective-permute-start.5 = (bf16[64,4224]{1,0:T(8,128)(2,1)S(1)}, bf16[64,4224]{1,0:T(8,128)(2,1)S(1)}, u32[]{:S(2)}, u32[]{:S(2)}) collective-permute-start(bf16[64,4224]{1,0:T(8,128)(2,1)S(1)} %extend_rows.1.refs_0_), channel_id=1, source_target_pairs={{24,0},{25,1},{26,2},{27,3},{28,4},{29,5},{30,6},{31,7},{0,8},{1,9... | collective-permute-start | bytes 1622024 | tf_op jit(solution)/shard_map/ppermute | solution.py:243
  16.5 4.5 %collective-permute-done.3.refs_0_ = bf16[64,4224]{1,0:T(8,128)(2,1)S(1)} collective-permute-done((bf16[64,4224]{1,0:T(8,128)(2,1)S(1)}, bf16[64,4224]{1,0:T(8,128)(2,1)S(1)}, u32[]{:S(2)}, u32[]{:S(2)}) %collective-permute-start.3) | collective-permute-done | bytes 540704 | tf_op jit(solution)/shard_map/ppermute | solution.py:243
  21.0 0.4 collective-permute-start.4
  21.4 0.0 collective-permute-start.1
  21.4 4.3 %collective-permute-start.9 = (bf16[64,4224]{1,0:T(8,128)(2,1)S(1)}, bf16[64,4224]{1,0:T(8,128)(2,1)S(1)}, u32[]{:S(2)}, u32[]{:S(2)}) collective-permute-start(bf16[64,4224]{1,0:T(8,128)(2,1)S(1)} %collective-permute-done.3.refs_0_), channel_id=1, source_target_pairs={{8,0},{9,1},{10,2},{11,3},{12,4},{13,5},{14,6},{15,7},{16,8},{17,9... | collective-permute-start | bytes 1622024 | tf_op jit(solution)/shard_map/ppermute | solution.py:243
  25.6 7.8 %collective-permute-done.5.refs_0_ = bf16[64,4224]{1,0:T(8,128)(2,1)S(1)} collective-permute-done((bf16[64,4224]{1,0:T(8,128)(2,1)S(1)}, bf16[64,4224]{1,0:T(8,128)(2,1)S(1)}, u32[]{:S(2)}, u32[]{:S(2)}) %collective-permute-start.5) | collective-permute-done | bytes 540704 | tf_op jit(solution)/shard_map/ppermute | solution.py:243
  33.5 0.0 collective-permute-done.1.refs_1_
  33.5 0.0 collective-permute-done.4.refs_1_
  33.5 0.0 collective-permute-done.2.refs_6_
  33.5 0.4 collective-permute-start.8
  33.9 0.9 compact_rows.5
  34.8 0.1 collective-permute-start.7
  34.9 0.5 collective-permute-start.12
  35.4 1.7 %collective-permute-start.6 = (bf16[2,48,4224]{2,1,0:T(8,128)(2,1)S(1)}, bf16[2,48,4224]{2,1,0:T(8,128)(2,1)S(1)}, u32[]{:S(2)}, u32[]{:S(2)}) collective-permute-start(bf16[2,48,4224]{2,1,0:T(8,128)(2,1)S(1)} %get-tuple-element.49), channel_id=1, source_target_pairs={{0,2},{1,5},{2,0},{3,7},{4,6},{5,1},{6,4},{7,3},{8,10},{9,13},{10,... | collective-permute-start | bytes 2433032 | tf_op jit(solution)/shard_map/ppermute | solution.py:239
  37.1 6.3 %hold_weights.1 = (bf16[4096,1024]{1,0:T(8,128)(2,1)S(1)}, bf16[4096,1024]{1,0:T(8,128)(2,1)S(1)}, s32[1]{0:T(128)}) custom-call(bf16[1,4096,1024]{2,1,0:T(8,128)(2,1)} %gate_w.1, bf16[1,4096,1024]{2,1,0:T(8,128)(2,1)} %up_w.1), custom_call_target="tpu_custom_call" | custom-call | flops 1 | bytes 1 | tf_op jit(solution)/shard_map/hold_weights/pallas_call | solution.py:139
  43.4 0.2 collective-permute-done.9.refs_0_
  43.6 0.0 collective-permute-done.7.refs_3_
  43.6 4.2 %collective-permute-done.8.refs_1_ = bf16[64,4224]{1,0:T(8,128)(2,1)S(1)} collective-permute-done((bf16[64,4224]{1,0:T(8,128)(2,1)S(1)}, bf16[64,4224]{1,0:T(8,128)(2,1)S(1)}, u32[]{:S(2)}, u32[]{:S(2)}) %collective-permute-start.8) | collective-permute-done | bytes 540704 | tf_op jit(solution)/shard_map/ppermute | solution.py:239
  47.8 0.0 collective-permute-start.10
  47.8 1.5 %compact_rows.6 = (bf16[1,48,4224]{2,1,0:T(8,128)(2,1)S(1)}, bf16[1,48,4224]{2,1,0:T(8,128)(2,1)S(1)}, bf16[2,48,4224]{2,1,0:T(8,128)(2,1)S(1)}) custom-call(s32[1]{0:T(128)} %get-tuple-element.59.after, bf16[64,4224]{1,0:T(8,128)(2,1)S(1)} %collective-permute-done.5.refs_0_, bf16[64,4224]{1,0:T(8,128)(2,1)S(1)} %collective-permute-done.8.refs_1_), custom_call_target="tpu_custom_call" | custom-call | flops 1 | bytes 1 | tf_op jit(solution)/shard_map/compact_rows/pallas_call | solution.py:113
  49.3 0.1 collective-permute-start.11
  49.4 1.9 %collective-permute-start.16 = (bf16[2,48,4224]{2,1,0:T(8,128)(2,1)S(1)}, bf16[2,48,4224]{2,1,0:T(8,128)(2,1)S(1)}, u32[]{:S(2)}, u32[]{:S(2)}) collective-permute-start(bf16[2,48,4224]{2,1,0:T(8,128)(2,1)S(1)} %get-tuple-element.74), channel_id=1, source_target_pairs={{0,2},{1,5},{2,0},{3,7},{4,6},{5,1},{6,4},{7,3},{8,10},{9,13},{10,... | collective-permute-start | bytes 2433032 | tf_op jit(solution)/shard_map/ppermute | solution.py:239
  51.3 0.0 collective-permute-done.12.refs_7_
  51.4 7.7 %sketch_rows.3.refs_9_ = f32[32,1024]{1,0:T(8,128)S(1)} custom-call(bf16[1,48,4224]{2,1,0:T(8,128)(2,1)S(1)} %get-tuple-element.55.refs_0_, bf16[1,48,4224]{2,1,0:T(8,128)(2,1)S(1)} %collective-permute-done.1.refs_1_, bf16[1,48,4224]{2,1,0:T(8,128)(2,1)S(1)} %get-tuple-element.57.refs_2_, bf16[1,48,4224]{2,1,0:T(8,128)(2,1)S(1)} %collective-permute-done.7.refs_3_, ...), custom_call_target="tpu_custom_call" | custom-call | flops 1 | bytes 1 | tf_op jit(solution)/shard_map/sketch_rows/pallas_call | solution.py:214
  59.0 0.0 collective-permute-done.6.refs_2_
  59.1 2.9 %collective-permute-done.10.refs_1_ = bf16[64,4224]{1,0:T(8,128)(2,1)S(1)} collective-permute-done((bf16[64,4224]{1,0:T(8,128)(2,1)S(1)}, bf16[64,4224]{1,0:T(8,128)(2,1)S(1)}, u32[]{:S(2)}, u32[]{:S(2)}) %collective-permute-start.10) | collective-permute-done | bytes 540704 | tf_op jit(solution)/shard_map/ppermute | solution.py:239
  62.0 0.9 compact_rows.7
  62.9 0.1 collective-permute-start.15
  62.9 0.0 collective-permute-done.16.refs_4_
  62.9 1.7 %collective-permute-done.15.refs_1_ = bf16[1,48,4224]{2,1,0:T(8,128)(2,1)S(1)} collective-permute-done((bf16[1,48,4224]{2,1,0:T(8,128)(2,1)S(1)}, bf16[1,48,4224]{2,1,0:T(8,128)(2,1)S(1)}, u32[]{:S(2)}, u32[]{:S(2)}) %collective-permute-start.15) | collective-permute-done | bytes 405536 | tf_op jit(solution)/shard_map/ppermute | solution.py:239
  64.7 1.3 %collective-permute-start.17 = (bf16[2,48,4224]{2,1,0:T(8,128)(2,1)S(1)}, bf16[2,48,4224]{2,1,0:T(8,128)(2,1)S(1)}, u32[]{:S(2)}, u32[]{:S(2)}) collective-permute-start(bf16[2,48,4224]{2,1,0:T(8,128)(2,1)S(1)} %collective-permute-done.6.refs_2_), channel_id=1, source_target_pairs={{0,1},{1,0},{2,3},{3,2},{4,5},{5,4},{6,7},{7,6},{8,9},{9,8},{10,11... | collective-permute-start | bytes 2433032 | tf_op jit(solution)/shard_map/ppermute | solution.py:239
  65.9 0.0 collective-permute-start.18
  65.9 0.6 collective-permute-start.13
  66.5 1.3 %collective-permute-start.14 = (bf16[1,48,4224]{2,1,0:T(8,128)(2,1)S(1)}, bf16[1,48,4224]{2,1,0:T(8,128)(2,1)S(1)}, u32[]{:S(2)}, u32[]{:S(2)}) collective-permute-start(bf16[1,48,4224]{2,1,0:T(8,128)(2,1)S(1)} %get-tuple-element.70), channel_id=1, source_target_pairs={{0,3},{1,4},{2,1},{3,6},{4,7},{5,0},{6,5},{7,2},{8,11},{9,12},{10,... | collective-permute-start | bytes 1216520 | tf_op jit(solution)/shard_map/ppermute | solution.py:239
  67.8 0.1 collective-permute-done.17.refs_3_
  67.9 1.2 %collective-permute-done.18.refs_5_ = bf16[2,48,4224]{2,1,0:T(8,128)(2,1)S(1)} collective-permute-done((bf16[2,48,4224]{2,1,0:T(8,128)(2,1)S(1)}, bf16[2,48,4224]{2,1,0:T(8,128)(2,1)S(1)}, u32[]{:S(2)}, u32[]{:S(2)}) %collective-permute-start.18) | collective-permute-done | bytes 811040 | tf_op jit(solution)/shard_map/ppermute | solution.py:239
  69.0 5.9 %sketch_rows.4.refs_5_ = f32[32,1024]{1,0:T(8,128)S(1)} custom-call(bf16[1,48,4224]{2,1,0:T(8,128)(2,1)S(1)} %get-tuple-element.75.refs_0_, bf16[1,48,4224]{2,1,0:T(8,128)(2,1)S(1)} %collective-permute-done.15.refs_1_, bf16[2,48,4224]{2,1,0:T(8,128)(2,1)S(1)} %collective-permute-done.6.refs_2_, bf16[2,48,4224]{2,1,0:T(8,128)(2,1)S(1)} %collective-permute-done.17.refs_3_, ...), custom_call_target="tpu_custom_call" | custom-call | flops 1 | bytes 1 | tf_op jit(solution)/shard_map/sketch_rows/pallas_call | solution.py:214
  74.9 0.0 collective-permute-done.13.refs_0_
  74.9 2.8 %collective-permute-done.14.refs_1_ = bf16[1,48,4224]{2,1,0:T(8,128)(2,1)S(1)} collective-permute-done((bf16[1,48,4224]{2,1,0:T(8,128)(2,1)S(1)}, bf16[1,48,4224]{2,1,0:T(8,128)(2,1)S(1)}, u32[]{:S(2)}, u32[]{:S(2)}) %collective-permute-start.14) | collective-permute-done | bytes 405536 | tf_op jit(solution)/shard_map/ppermute | solution.py:239
  77.7 3.3 %sketch_rows.5 = bf16[32,8,128]{2,1,0:T(8,128)(2,1)S(1)} custom-call(bf16[1,48,4224]{2,1,0:T(8,128)(2,1)S(1)} %collective-permute-done.13.refs_0_, bf16[1,48,4224]{2,1,0:T(8,128)(2,1)S(1)} %collective-permute-done.14.refs_1_, bf16[4096,1024]{1,0:T(8,128)(2,1)S(1)} %get-tuple-element.65.refs_8_.refs_6_.refs_2_, ...), custom_call_target="tpu_custom_call" | custom-call | flops 1 | bytes 1 | tf_op jit(solution)/shard_map/sketch_rows/pallas_call | solution.py:214
  81.1 11.9 %all_to_all.5 = bf16[32,8,128]{2,1,0:T(8,128)(2,1)S(1)} all-to-all(bf16[32,8,128]{2,1,0:T(8,128)(2,1)S(1)} %sketch_rows.5), channel_id=1, replica_groups=mesh['expert'=4,'dp'=8] {'expert','dp'}, dimensions={0} | all-to-all | bytes 131072 | tf_op jit(solution)/shard_map/all_to_all | solution.py:311
  92.9 0.7 reshape.19
  (4 shorter events, 0.0 us)
Async XLA Ops:
  1.6 10.4 %collective-permute-start = (bf16[64,4224]{1,0:T(8,128)(2,1)S(1)}, bf16[64,4224]{1,0:T(8,128)(2,1)S(1)}, u32[]{:S(2)}, u32[]{:S(2)}) collective-permute-start(bf16[64,4224]{1,0:T(8,128)(2,1)S(1)} %extend_rows.1.refs_0_), channel_id=1, source_target_pairs={{0,4},{1,3},{2,6},{3,1},{4,0},{5,7},{6,2},{7,5},{8,12},{9,11},{10,... | collective-permute-start | bytes 1622024 | tf_op jit(solution)/shard_map/ppermute | solution.py:239
  4.6 16.4 %collective-permute-start.3 = (bf16[64,4224]{1,0:T(8,128)(2,1)S(1)}, bf16[64,4224]{1,0:T(8,128)(2,1)S(1)}, u32[]{:S(2)}, u32[]{:S(2)}) collective-permute-start(bf16[64,4224]{1,0:T(8,128)(2,1)S(1)} %extend_rows.1.refs_0_), channel_id=1, source_target_pairs={{8,0},{9,1},{10,2},{11,3},{12,4},{13,5},{14,6},{15,7},{16,8},{17,9... | collective-permute-start | bytes 1622024 | tf_op jit(solution)/shard_map/ppermute | solution.py:243
  12.9 20.6 %collective-permute-start.2 = (bf16[2,48,4224]{2,1,0:T(8,128)(2,1)S(1)}, bf16[2,48,4224]{2,1,0:T(8,128)(2,1)S(1)}, u32[]{:S(2)}, u32[]{:S(2)}) collective-permute-start(bf16[2,48,4224]{2,1,0:T(8,128)(2,1)S(1)} %get-tuple-element.46), channel_id=1, source_target_pairs={{0,2},{1,5},{2,0},{3,7},{4,6},{5,1},{6,4},{7,3},{8,10},{9,13},{10,... | collective-permute-start | bytes 2433032 | tf_op jit(solution)/shard_map/ppermute | solution.py:239
  14.9 18.6 %collective-permute-start.5 = (bf16[64,4224]{1,0:T(8,128)(2,1)S(1)}, bf16[64,4224]{1,0:T(8,128)(2,1)S(1)}, u32[]{:S(2)}, u32[]{:S(2)}) collective-permute-start(bf16[64,4224]{1,0:T(8,128)(2,1)S(1)} %extend_rows.1.refs_0_), channel_id=1, source_target_pairs={{24,0},{25,1},{26,2},{27,3},{28,4},{29,5},{30,6},{31,7},{0,8},{1,9... | collective-permute-start | bytes 1622024 | tf_op jit(solution)/shard_map/ppermute | solution.py:243
  21.0 12.5 %collective-permute-start.4 = (bf16[64,4224]{1,0:T(8,128)(2,1)S(1)}, bf16[64,4224]{1,0:T(8,128)(2,1)S(1)}, u32[]{:S(2)}, u32[]{:S(2)}) collective-permute-start(bf16[64,4224]{1,0:T(8,128)(2,1)S(1)} %collective-permute-done.3.refs_0_), channel_id=1, source_target_pairs={{0,4},{1,3},{2,6},{3,1},{4,0},{5,7},{6,2},{7,5},{8,12},{9,11},{10,... | collective-permute-start | bytes 1622024 | tf_op jit(solution)/shard_map/ppermute | solution.py:239
  21.4 12.1 %collective-permute-start.1 = (bf16[1,48,4224]{2,1,0:T(8,128)(2,1)S(1)}, bf16[1,48,4224]{2,1,0:T(8,128)(2,1)S(1)}, u32[]{:S(2)}, u32[]{:S(2)}) collective-permute-start(bf16[1,48,4224]{2,1,0:T(8,128)(2,1)S(1)} %get-tuple-element.45), channel_id=1, source_target_pairs={{0,1},{1,0},{2,3},{3,2},{4,5},{5,4},{6,7},{7,6},{8,9},{9,8},{10,11... | collective-permute-start | bytes 1216520 | tf_op jit(solution)/shard_map/ppermute | solution.py:239
  21.4 22.2 %collective-permute-start.9 = (bf16[64,4224]{1,0:T(8,128)(2,1)S(1)}, bf16[64,4224]{1,0:T(8,128)(2,1)S(1)}, u32[]{:S(2)}, u32[]{:S(2)}) collective-permute-start(bf16[64,4224]{1,0:T(8,128)(2,1)S(1)} %collective-permute-done.3.refs_0_), channel_id=1, source_target_pairs={{8,0},{9,1},{10,2},{11,3},{12,4},{13,5},{14,6},{15,7},{16,8},{17,9... | collective-permute-start | bytes 1622024 | tf_op jit(solution)/shard_map/ppermute | solution.py:243
  33.5 14.3 %collective-permute-start.8 = (bf16[64,4224]{1,0:T(8,128)(2,1)S(1)}, bf16[64,4224]{1,0:T(8,128)(2,1)S(1)}, u32[]{:S(2)}, u32[]{:S(2)}) collective-permute-start(bf16[64,4224]{1,0:T(8,128)(2,1)S(1)} %collective-permute-done.5.refs_0_), channel_id=1, source_target_pairs={{0,4},{1,3},{2,6},{3,1},{4,0},{5,7},{6,2},{7,5},{8,12},{9,11},{10,... | collective-permute-start | bytes 1622024 | tf_op jit(solution)/shard_map/ppermute | solution.py:239
  34.8 8.8 %collective-permute-start.7 = (bf16[1,48,4224]{2,1,0:T(8,128)(2,1)S(1)}, bf16[1,48,4224]{2,1,0:T(8,128)(2,1)S(1)}, u32[]{:S(2)}, u32[]{:S(2)}) collective-permute-start(bf16[1,48,4224]{2,1,0:T(8,128)(2,1)S(1)} %get-tuple-element.51), channel_id=1, source_target_pairs={{0,1},{1,0},{2,3},{3,2},{4,5},{5,4},{6,7},{7,6},{8,9},{9,8},{10,11... | collective-permute-start | bytes 1216520 | tf_op jit(solution)/shard_map/ppermute | solution.py:239
  34.9 16.4 %collective-permute-start.12 = (bf16[2,48,4224]{2,1,0:T(8,128)(2,1)S(1)}, bf16[2,48,4224]{2,1,0:T(8,128)(2,1)S(1)}, u32[]{:S(2)}, u32[]{:S(2)}) collective-permute-start(bf16[2,48,4224]{2,1,0:T(8,128)(2,1)S(1)} %collective-permute-done.2.refs_6_), channel_id=1, source_target_pairs={{0,1},{1,0},{2,3},{3,2},{4,5},{5,4},{6,7},{7,6},{8,9},{9,8},{10,11... | collective-permute-start | bytes 2433032 | tf_op jit(solution)/shard_map/ppermute | solution.py:239
  35.4 16.0 %copy-start = (bf16[1024,32]{0,1:T(8,128)(2,1)S(1)}, bf16[1024,32]{0,1:T(8,128)(2,1)}, u32[]{:S(2)}) copy-start(bf16[1024,32]{0,1:T(8,128)(2,1)} %param.16) | copy-start | bytes 196612
  35.4 23.7 %collective-permute-start.6 = (bf16[2,48,4224]{2,1,0:T(8,128)(2,1)S(1)}, bf16[2,48,4224]{2,1,0:T(8,128)(2,1)S(1)}, u32[]{:S(2)}, u32[]{:S(2)}) collective-permute-start(bf16[2,48,4224]{2,1,0:T(8,128)(2,1)S(1)} %get-tuple-element.49), channel_id=1, source_target_pairs={{0,2},{1,5},{2,0},{3,7},{4,6},{5,1},{6,4},{7,3},{8,10},{9,13},{10,... | collective-permute-start | bytes 2433032 | tf_op jit(solution)/shard_map/ppermute | solution.py:239
  47.8 14.2 %collective-permute-start.10 = (bf16[64,4224]{1,0:T(8,128)(2,1)S(1)}, bf16[64,4224]{1,0:T(8,128)(2,1)S(1)}, u32[]{:S(2)}, u32[]{:S(2)}) collective-permute-start(bf16[64,4224]{1,0:T(8,128)(2,1)S(1)} %collective-permute-done.9.refs_0_), channel_id=1, source_target_pairs={{0,4},{1,3},{2,6},{3,1},{4,0},{5,7},{6,2},{7,5},{8,12},{9,11},{10,... | collective-permute-start | bytes 1622024 | tf_op jit(solution)/shard_map/ppermute | solution.py:239
  49.3 2.0 %collective-permute-start.11 = (bf16[1,48,4224]{2,1,0:T(8,128)(2,1)S(1)}, bf16[1,48,4224]{2,1,0:T(8,128)(2,1)S(1)}, u32[]{:S(2)}, u32[]{:S(2)}) collective-permute-start(bf16[1,48,4224]{2,1,0:T(8,128)(2,1)S(1)} %get-tuple-element.63), channel_id=1, source_target_pairs={{0,1},{1,0},{2,3},{3,2},{4,5},{5,4},{6,7},{7,6},{8,9},{9,8},{10,11... | collective-permute-start | bytes 1216520 | tf_op jit(solution)/shard_map/ppermute | solution.py:239
  49.4 13.5 %collective-permute-start.16 = (bf16[2,48,4224]{2,1,0:T(8,128)(2,1)S(1)}, bf16[2,48,4224]{2,1,0:T(8,128)(2,1)S(1)}, u32[]{:S(2)}, u32[]{:S(2)}) collective-permute-start(bf16[2,48,4224]{2,1,0:T(8,128)(2,1)S(1)} %get-tuple-element.74), channel_id=1, source_target_pairs={{0,2},{1,5},{2,0},{3,7},{4,6},{5,1},{6,4},{7,3},{8,10},{9,13},{10,... | collective-permute-start | bytes 2433032 | tf_op jit(solution)/shard_map/ppermute | solution.py:239
  62.9 1.8 %collective-permute-start.15 = (bf16[1,48,4224]{2,1,0:T(8,128)(2,1)S(1)}, bf16[1,48,4224]{2,1,0:T(8,128)(2,1)S(1)}, u32[]{:S(2)}, u32[]{:S(2)}) collective-permute-start(bf16[1,48,4224]{2,1,0:T(8,128)(2,1)S(1)} %get-tuple-element.72), channel_id=1, source_target_pairs={{0,1},{1,0},{2,3},{3,2},{4,5},{5,4},{6,7},{7,6},{8,9},{9,8},{10,11... | collective-permute-start | bytes 1216520 | tf_op jit(solution)/shard_map/ppermute | solution.py:239
  64.7 3.2 %collective-permute-start.17 = (bf16[2,48,4224]{2,1,0:T(8,128)(2,1)S(1)}, bf16[2,48,4224]{2,1,0:T(8,128)(2,1)S(1)}, u32[]{:S(2)}, u32[]{:S(2)}) collective-permute-start(bf16[2,48,4224]{2,1,0:T(8,128)(2,1)S(1)} %collective-permute-done.6.refs_2_), channel_id=1, source_target_pairs={{0,1},{1,0},{2,3},{3,2},{4,5},{5,4},{6,7},{7,6},{8,9},{9,8},{10,11... | collective-permute-start | bytes 2433032 | tf_op jit(solution)/shard_map/ppermute | solution.py:239
  65.9 3.1 %collective-permute-start.18 = (bf16[2,48,4224]{2,1,0:T(8,128)(2,1)S(1)}, bf16[2,48,4224]{2,1,0:T(8,128)(2,1)S(1)}, u32[]{:S(2)}, u32[]{:S(2)}) collective-permute-start(bf16[2,48,4224]{2,1,0:T(8,128)(2,1)S(1)} %collective-permute-done.16.refs_4_), channel_id=1, source_target_pairs={{0,1},{1,0},{2,3},{3,2},{4,5},{5,4},{6,7},{7,6},{8,9},{9,8},{10,11... | collective-permute-start | bytes 2433032 | tf_op jit(solution)/shard_map/ppermute | solution.py:239
  65.9 9.0 %collective-permute-start.13 = (bf16[1,48,4224]{2,1,0:T(8,128)(2,1)S(1)}, bf16[1,48,4224]{2,1,0:T(8,128)(2,1)S(1)}, u32[]{:S(2)}, u32[]{:S(2)}) collective-permute-start(bf16[1,48,4224]{2,1,0:T(8,128)(2,1)S(1)} %get-tuple-element.69), channel_id=1, source_target_pairs={{0,2},{1,5},{2,0},{3,7},{4,6},{5,1},{6,4},{7,3},{8,10},{9,13},{10,... | collective-permute-start | bytes 1216520 | tf_op jit(solution)/shard_map/ppermute | solution.py:239
  66.5 11.2 %collective-permute-start.14 = (bf16[1,48,4224]{2,1,0:T(8,128)(2,1)S(1)}, bf16[1,48,4224]{2,1,0:T(8,128)(2,1)S(1)}, u32[]{:S(2)}, u32[]{:S(2)}) collective-permute-start(bf16[1,48,4224]{2,1,0:T(8,128)(2,1)S(1)} %get-tuple-element.70), channel_id=1, source_target_pairs={{0,3},{1,4},{2,1},{3,6},{4,7},{5,0},{6,5},{7,2},{8,11},{9,12},{10,... | collective-permute-start | bytes 1216520 | tf_op jit(solution)/shard_map/ppermute | solution.py:239
